TPU v7x, 256 devices: a whole 4x4x8 slice. The times are simulated.
256 devices in a mesh: dom: 64 (over z, x, core), rep: 4 (over y).
Axes of the slice: x: 4, y: 4, z: 8, core: 2. Of those that a mesh axis runs over, the one named last changes fastest.
Arguments:
- feats: bfloat16 [65536, 768], P('dom'), may hold values from -6 to 6
- seed_rows: int32 [65536], P(('dom', 'rep')), may hold values from 0 to 1023
- edge_rows: int32 [256, 64, 64], P(('dom', 'rep')), may hold values from 0 to 1023
- edge_slots: int32 [256, 64, 64], P(('dom', 'rep')), may hold values from 0 to 32, as said below
- slot_seeds: int32 [256, 64, 32], P(('dom', 'rep')), may hold values from 0 to 256, as said below
- w_self: bfloat16 [768, 1024], replicated, may hold values from -0.21875 to 0.21875
- w_neigh: bfloat16 [768, 1024], replicated, may hold values from -0.21875 to 0.21875
- bias: float32 [1024], replicated, may hold values from -3 to 3
- cotangent: bfloat16 [65536, 1024], P(('dom', 'rep')), may hold values from -6 to 6
Outputs:
- hidden_out: bfloat16 [65536, 1024], P(('dom', 'rep'))
- self_grad: bfloat16 [65536, 768], P(('dom', 'rep'))
- feat_grads: bfloat16 [65536, 768], P(('dom', 'rep'))
- grad_self: float32 [768, 1024], replicated
- grad_neigh: float32 [768, 1024], replicated
- grad_bias: float32 [1024], replicated
Inputs may be any that keep to these rules, and one draw needn't show every extreme that they name: `edge_slots`: the value 32 marks an unused edge entry. In each bucket (one device, one destination partition) every used slot is named by at least one entry and the used entries name only used slots. Each device has a bucket with all 64 entries used, naming all 32 slots. `slot_seeds`: the value 256 marks an unused slot. Slot p from source partition o at group d * 4 + r is used exactly when the edge entries of device o * 4 + r for destination d name it; the used slots from one source name distinct seeds.
All inputs are finite; a program needn't handle non-finite values.
Results may differ from a plain program's by a relative error of at most 0.007.
Values may be sent and summed in bfloat16 or wider, within the bound.
No kernel may reach another device: no remote copies, remote signals or barrier semaphores. Data moves between devices by JAX's collectives and lax.ppermute only.
A program may use at most 128 MiB of HBM per device.

v0:
```python
import jax
import jax.numpy as jnp
from jax import lax
from jax.sharding import PartitionSpec as P


def contract_first(left, right):
    return lax.dot_general(
        left, right, (((0,), (0,)), ((), ())), preferred_element_type=jnp.float32
    )


def contract_last(left, right):
    return lax.dot_general(
        left, right, (((1,), (1,)), ((), ())), preferred_element_type=jnp.float32
    )


def on_device(
    feats, seed_rows, edge_rows, edge_slots, slot_seeds, w_self, w_neigh, bias, cotangent
):
    edge_rows = edge_rows[0]
    edge_slots = edge_slots[0]
    slot_seeds = slot_seeds[0]
    sources, slot_cap = slot_seeds.shape
    seed_count = seed_rows.shape[0]
    width = feats.shape[1]
    gathered = jnp.take(feats, edge_rows, axis=0)
    slot_onehot = (
        edge_slots[:, :, None] == jnp.arange(slot_cap, dtype=jnp.int32)[None, None, :]
    ).astype(jnp.bfloat16)
    partial_value = jnp.einsum(
        "dep,def->dpf", slot_onehot, gathered, preferred_element_type=jnp.float32
    ).astype(jnp.bfloat16)
    counts = jnp.sum(slot_onehot.astype(jnp.float32), axis=1).astype(jnp.bfloat16)
    arrived, arrived_counts = (
        lax.all_to_all(partial_value, "dom", split_axis=0, concat_axis=0, tiled=True),
        lax.all_to_all(counts, "dom", split_axis=0, concat_axis=0, tiled=True),
    )
    seed_onehot = (
        slot_seeds.reshape(-1)[:, None] == jnp.arange(seed_count, dtype=jnp.int32)[None, :]
    ).astype(jnp.bfloat16)
    agg_sum = contract_first(seed_onehot, arrived.reshape(-1, width))
    degree_raw = contract_first(seed_onehot, arrived_counts.reshape(-1, 1))
    degree = jnp.maximum(degree_raw, 1.0)
    aggregate = (agg_sum / degree).astype(jnp.bfloat16)
    self_rows = jnp.take(feats, seed_rows, axis=0)
    pre = jnp.dot(self_rows, w_self, preferred_element_type=jnp.float32)
    pre = pre + jnp.dot(aggregate, w_neigh, preferred_element_type=jnp.float32) + bias[None, :]
    hidden_out = jax.nn.gelu(pre).astype(jnp.bfloat16)
    _, pullback = jax.vjp(jax.nn.gelu, pre)
    delta = pullback(cotangent.astype(jnp.float32))[0].astype(jnp.bfloat16)
    scale = float(seed_count * lax.axis_size("dom") * lax.axis_size("rep")) ** (-0.5)
    term_self = contract_first(self_rows, delta) * scale
    term_neigh = contract_first(aggregate, delta) * scale
    term_bias = jnp.sum(delta.astype(jnp.float32), axis=0) * scale
    grad_self, grad_neigh, grad_bias = lax.psum((term_self, term_neigh, term_bias), ("dom", "rep"))
    self_grad = contract_last(delta, w_self).astype(jnp.bfloat16)
    delta_neigh = (delta.astype(jnp.float32) / degree).astype(jnp.bfloat16)
    aggregate_grad = contract_last(delta_neigh, w_neigh).astype(jnp.bfloat16)
    routed = jnp.dot(seed_onehot, aggregate_grad, preferred_element_type=jnp.float32).astype(
        jnp.bfloat16
    )
    slot_grad = lax.all_to_all(
        routed.reshape(sources, slot_cap, width), "dom", split_axis=0, concat_axis=0, tiled=True
    )
    edge_grad = jnp.einsum(
        "dep,dpf->def", slot_onehot, slot_grad, preferred_element_type=jnp.float32
    )
    local_sum = jax.ops.segment_sum(
        edge_grad.reshape(-1, width), edge_rows.reshape(-1), num_segments=feats.shape[0]
    )
    feat_grads = lax.psum_scatter(local_sum, "rep", scatter_dimension=0, tiled=True).astype(
        jnp.bfloat16
    )
    return (hidden_out, self_grad, feat_grads, grad_self, grad_neigh, grad_bias)


def solution(mesh):
    in_specs = (
        P("dom", None),
        P(("dom", "rep")),
        P(("dom", "rep"), None, None),
        P(("dom", "rep"), None, None),
        P(("dom", "rep"), None, None),
        P(),
        P(),
        P(),
        P(("dom", "rep"), None),
    )
    out_specs = (
        P(("dom", "rep"), None),
        P(("dom", "rep"), None),
        P(("dom", "rep"), None),
        P(),
        P(),
        P(),
    )
    return jax.shard_map(
        on_device, mesh=mesh, in_specs=in_specs, out_specs=out_specs, check_vma=False
    )
```

profile of v0, /device:TPU:1, one launch (start us, length us, event | category | flops | bytes accessed | tf_op | source)
XLA Modules:
  0.0 557.2 jit_solution(4271743349254302712)
XLA Ops:
  8.0 0.0 copy-start
  8.0 1.2 fusion.32
  9.2 0.6 copy.21
  9.9 13.0 %all-to-all-start.1 = ((bf16[64,1,32]{2,1,0:T(2,128)(2,1)}), bf16[64,1,32]{2,1,0:T(2,128)(2,1)S(1)}, u32[]{:S(2)}, u32[]{:S(2)}) async-start(bf16[64,1,32]{2,1,0:T(2,128)(2,1)} %copy.21), calls=%async_computation.1 | async-start | bytes 65536 | tf_op jit(solution)/shard_map/all_to_all | solution.py:38
  22.9 0.8 compare_select_fusion
  23.6 0.8 compare_and_fusion
  24.4 0.1 reshape.88
  24.5 0.0 copy-done
  24.5 0.0 copy-start.5
  24.5 17.8 %gather_fusion.1 = bf16[4096,768]{1,0:T(8,128)(2,1)} fusion(bf16[1024,768]{1,0:T(8,128)(2,1)S(1)} %copy-done, s32[4096]{0:T(1024)S(1)} %broadcast_clamp_fusion), kind=kCustom, calls=%fused_computation.1 | custom fusion | bytes 12599296 | tf_op jit(solution)/shard_map/jit(_take)/gather | solution.py:28
  42.3 0.0 copy-done.5
  42.3 4.7 fusion.4
  47.0 0.0 copy-start.9
  47.0 0.0 all-to-all-done.1
  47.0 0.0 copy-start.7
  47.0 0.6 copy-done.7
  47.6 10.5 %all-to-all-start = ((bf16[64,32,768]{2,1,0:T(8,128)(2,1)}), bf16[64,32,768]{2,1,0:T(8,128)(2,1)}, u32[]{:S(2)}, u32[]{:S(2)}) async-start(bf16[64,32,768]{2,1,0:T(8,128)(2,1)} %fusion.4), calls=%async_computation | async-start | bytes 6291456 | tf_op jit(solution)/shard_map/all_to_all | solution.py:37
  58.1 0.0 copy-done.9
  58.1 0.0 copy-start.8
  58.1 0.0 copy-start.2
  58.1 0.6 pad_clamp_fusion
  58.7 1.3 gather_fusion
  60.1 0.0 copy-done.8
  60.1 0.7 copy.19
  60.8 0.8 eq.30
  61.6 0.7 compare_and_fusion.1
  62.3 0.0 copy-done.2
  62.3 1.6 fusion.37
  63.9 0.9 reduce.1
  64.7 0.1 reshape.105
  64.8 0.5 fusion.7
  65.3 65.3 %all-to-all-done = bf16[64,32,768]{2,1,0:T(8,128)(2,1)} async-done(((bf16[64,32,768]{2,1,0:T(8,128)(2,1)}), bf16[64,32,768]{2,1,0:T(8,128)(2,1)}, u32[]{:S(2)}, u32[]{:S(2)}) %all-to-all-start) | async-done | bytes 3145760 | tf_op jit(solution)/shard_map/all_to_all | solution.py:37
  130.6 0.0 copy-start.3
  130.6 0.0 copy-start.10
  130.6 0.0 copy-start.11
  130.6 0.0 copy-start.12
  130.6 3.5 fusion.13
  134.1 0.0 copy-done.3
  134.1 0.0 copy-done.10
  134.1 0.0 copy-done.11
  134.1 0.0 copy-done.12
  134.1 2.2 convert_reduce_fusion
  136.3 4.6 convolution_convert_fusion
  141.0 0.0 copy-start.4
  141.0 6.9 %all-to-all-start.2 = ((bf16[64,32,768]{2,1,0:T(8,128)(2,1)}), bf16[64,32,768]{2,1,0:T(8,128)(2,1)}, u32[]{:S(2)}, u32[]{:S(2)}) async-start(bf16[64,32,768]{2,1,0:T(8,128)(2,1)} %bitcast.29), calls=%async_computation.2 | async-start | bytes 6291456 | tf_op jit(solution)/shard_map/all_to_all | solution.py:64
  147.9 0.2 reduce-scatter.2.cloned.1.call-start
  148.1 0.0 copy-done.4
  148.1 0.1 reshape.96
  148.2 72.4 %all-to-all-done.2 = bf16[64,32,768]{2,1,0:T(8,128)(2,1)} async-done(((bf16[64,32,768]{2,1,0:T(8,128)(2,1)}), bf16[64,32,768]{2,1,0:T(8,128)(2,1)}, u32[]{:S(2)}, u32[]{:S(2)}) %all-to-all-start.2) | async-done | bytes 3145760 | tf_op jit(solution)/shard_map/all_to_all | solution.py:64
  220.6 0.0 copy-done.6
  220.6 8.3 %fusion.25 = f32[64,64,768]{2,1,0:T(8,128)} fusion(bf16[64,32,768]{2,1,0:T(8,128)(2,1)} %all-to-all-done.2, s32[64,64]{1,0:T(8,128)S(1)} %bitcast.32), kind=kOutput, calls=%fused_computation.41 | convolution fusion | flops 201457664 | bytes 15745024 | tf_op jit(solution)/shard_map/dep,dpf->def/dot_general | solution.py:67
  228.8 29.3 %scatter_custom_fusion = f32[1024,768]{1,0:T(8,128)} fusion(s32[4096]{0:T(1024)S(1)} %reshape.96, f32[4096,768]{1,0:T(8,128)} %bitcast.27, f32[]{:T(128)} %constant.47.clone.1), kind=kCustom, calls=%fused_computation.14 | custom fusion | flops 3145728 | bytes 3146240 | tf_op jit(solution)/shard_map/scatter-add | solution.py:70
  258.2 0.0 reduce-scatter.2.cloned.1.call-update
  258.2 0.0 all-reduce.3.cloned.1.call-start
  258.3 2.3 convolution_multiply_fusion
  260.6 2.4 convolution_multiply_fusion.1
  262.9 0.0 all-reduce.3.cloned.1.call-update
  262.9 78.1 %psum.23 = f32[1024]{0:T(1024)} all-reduce(f32[1024]{0:T(1024)S(1)} %broadcast_multiply_fusion), channel_id=1, replica_groups=mesh['dom'=64,'rep'=4] {'dom','rep'}, use_global_device_ids=true, to_apply=%region_6.7 | all-reduce | flops 1024 | bytes 8192 | tf_op jit(solution)/shard_map/psum | solution.py:57
  341.1 2.8 convolution_convert_fusion.2
  343.9 1.9 convert_element_type.51
  345.8 198.2 %all-reduce.3.cloned.1.call-done = (f32[768,1024]{1,0:T(8,128)}, f32[768,1024]{1,0:T(8,128)}) async-done(((f32[768,1024]{1,0:T(8,128)}, f32[768,1024]{1,0:T(8,128)}), (f32[768,1024]{1,0:T(8,128)}, f32[768,1024]{1,0:T(8,128)})) %all-reduce.3.cloned.1.call-update) | async-done | bytes 6291472 | tf_op jit(solution)/shard_map/psum | solution.py:57
  543.9 4.1 copy.26
  548.0 0.0 copy-done.1
  548.0 1.7 copy.27
  (7 shorter events, 0.0 us)
Async XLA Ops:
  8.0 16.5 %copy-start = (bf16[1024,768]{1,0:T(8,128)(2,1)S(1)}, bf16[1024,768]{1,0:T(8,128)(2,1)}, u32[]{:S(2)}) copy-start(bf16[1024,768]{1,0:T(8,128)(2,1)} %param.9) | copy-start | bytes 4718596
  9.9 37.1 %all-to-all-start.1 = ((bf16[64,1,32]{2,1,0:T(2,128)(2,1)}), bf16[64,1,32]{2,1,0:T(2,128)(2,1)S(1)}, u32[]{:S(2)}, u32[]{:S(2)}) async-start(bf16[64,1,32]{2,1,0:T(2,128)(2,1)} %copy.21), calls=%async_computation.1 | async-start | bytes 65536 | tf_op jit(solution)/shard_map/all_to_all | solution.py:38
  24.5 17.8 %copy-start.5 = (s32[1,64,64]{2,1,0:T(8,128)S(1)}, s32[1,64,64]{2,1,0:T(8,128)}, u32[]{:S(2)}) copy-start(s32[1,64,64]{2,1,0:T(8,128)} %param.12) | copy-start | bytes 49156
  47.0 11.1 %copy-start.9 = (s32[256]{0:T(256)S(1)}, s32[256]{0:T(256)}, u32[]{:S(2)}) copy-start(s32[256]{0:T(256)} %param.10) | copy-start | bytes 3076
  47.0 0.6 copy-start.7
  47.6 83.0 %all-to-all-start = ((bf16[64,32,768]{2,1,0:T(8,128)(2,1)}), bf16[64,32,768]{2,1,0:T(8,128)(2,1)}, u32[]{:S(2)}, u32[]{:S(2)}) async-start(bf16[64,32,768]{2,1,0:T(8,128)(2,1)} %fusion.4), calls=%async_computation | async-start | bytes 6291456 | tf_op jit(solution)/shard_map/all_to_all | solution.py:37
  58.1 2.0 copy-start.8
  58.1 4.2 copy-start.2
  130.6 3.5 copy-start.3
  130.6 3.5 copy-start.10
  130.6 3.5 copy-start.11
  130.6 3.5 copy-start.12
  141.0 7.1 %copy-start.4 = (s32[1,64,64]{2,1,0:T(8,128)S(1)}, s32[1,64,64]{2,1,0:T(8,128)}, u32[]{:S(2)}) copy-start(s32[1,64,64]{2,1,0:T(8,128)} %param.11) | copy-start | bytes 49156
  141.0 79.6 %copy-start.6 = (s32[1,64,64]{2,1,0:T(8,128)S(1)}, s32[1,64,64]{2,1,0:T(8,128)}, u32[]{:S(2)}) copy-start(s32[1,64,64]{2,1,0:T(8,128)} %param.12) | copy-start | bytes 49156
  141.0 79.6 %all-to-all-start.2 = ((bf16[64,32,768]{2,1,0:T(8,128)(2,1)}), bf16[64,32,768]{2,1,0:T(8,128)(2,1)}, u32[]{:S(2)}, u32[]{:S(2)}) async-start(bf16[64,32,768]{2,1,0:T(8,128)(2,1)} %bitcast.29), calls=%async_computation.2 | async-start | bytes 6291456 | tf_op jit(solution)/shard_map/all_to_all | solution.py:64
  147.9 196.0 %reduce-scatter.2.cloned.1.call-start = ((), (), s32[]{:S(2)}) async-start(), calls=%async_computation.4 | async-start | bytes 3932160 | tf_op jit(solution)/shard_map/reduce_scatter | solution.py:73
  258.2 285.7 %all-reduce.3.cloned.1.call-start = ((), (), s32[]{:S(2)}) async-start(), calls=%async_computation.5 | async-start | bytes 12582912 | tf_op jit(solution)/shard_map/psum | solution.py:57
  543.9 4.1 copy-start.1
Sparse Core Ops, SparseCore 0:
  258.3 41.3 reduce-scatter.1
Sparse Core Ops, SparseCore 1:
  264.9 279.0 all-reduce.2
where the time goes:
time: 559 us; the launch traced here: 557 us
  waiting for transfers between devices  336 us (60%)
  blocking collectives  78.1 us (14%)
  other arithmetic  36.2 us (6%)
  matrix products  32.8 us (6%)
  starting transfers between devices  30.6 us (5%)
  local copies, waits for them, and re-layouts  28 us (5%)
  between operations  15.6 us (3%)
    psum x1, waiting for transfers between devices, on_device(): lax.psum((term_self, term_neigh, term_bias), ('dom', 'rep'))  198 us
    psum x1, blocking collectives, on_device(): lax.psum((term_self, term_neigh, term_bias), ('dom', 'rep'))  78.1 us
    all_to_all x1, waiting for transfers between devices, on_device(): lax.all_to_all(routed.reshape(sources, slot_cap, width), 'dom', split_axi...  72.4 us
    all_to_all x1, waiting for transfers between devices, on_device(): lax.all_to_all(partial_value, 'dom', split_axis=0, concat_axis=0, tiled=T...  65.3 us
    scatter-add x1, other arithmetic, on_device(): jax.ops.segment_sum(edge_grad.reshape(-1, width), edge_rows.reshape(-1),...  29.3 us
    gather x1, local copies, waits for them, and re-layouts, on_device(): gathered = jnp.take(feats, edge_rows, axis=0)  17.8 us
    all_to_all x1, starting transfers between devices, on_device(): lax.all_to_all(counts, 'dom', split_axis=0, concat_axis=0, tiled=True)  13 us
  transfers between devices with their start and end apart: 5, of which 3 were waited for; matrix products, arithmetic and copies ran while one was open for 7% of the time, Pallas kernels for 0%

commit v1 on v0

v1 whole, which is shorter than its diff:
```python
import jax
import jax.numpy as jnp
import numpy as np
from jax import lax
from jax.experimental import pallas as pl
from jax.experimental.pallas import tpu as pltpu
from jax.sharding import Mesh, PartitionSpec as P

DOM = ("z", "x", "c")
NEAR = ("c", "rep")
FAR = ("z", "x")
bf16 = jnp.bfloat16
f32 = jnp.float32

GROUP = 4
STEP = 4


def contract_first(left, right):
    return lax.dot_general(
        left, right, (((0,), (0,)), ((), ())), preferred_element_type=f32
    )


def contract_last(left, right):
    return lax.dot_general(
        left, right, (((1,), (1,)), ((), ())), preferred_element_type=f32
    )


def exchange(value, axes):
    return lax.all_to_all(value, axes, split_axis=0, concat_axis=0, tiled=True)


def select_kernel(rows_ref, keys_ref, feats_ref, select_ref, partial_ref, count_ref):
    row_count = feats_ref.shape[0]
    entries = rows_ref.shape[2]
    slots = select_ref.shape[0] // STEP
    row_ids = lax.broadcasted_iota(jnp.int32, (row_count, entries), 0)
    slot_ids = lax.broadcasted_iota(jnp.int32, (slots, entries), 0)
    ones = jnp.ones((8, entries), bf16)
    for step in range(STEP):
        by_row = jnp.where(row_ids == rows_ref[step], 1.0, 0.0).astype(bf16)
        by_slot = jnp.where(slot_ids == keys_ref[step], 1.0, 0.0).astype(bf16)
        select_ref[step * slots : (step + 1) * slots, :] = contract_last(
            by_slot, by_row
        ).astype(bf16)
        count_ref[step] = contract_last(ones, by_slot)[0:1]
    partial_ref[...] = jnp.dot(
        select_ref[...], feats_ref[...], preferred_element_type=f32
    ).astype(bf16)


def select_and_sum(feats, edge_rows, edge_slots, slot_cap):
    dests, entry_cap = edge_rows.shape
    row_count, width = feats.shape
    groups = dests // GROUP
    entries = GROUP * entry_cap
    slots = GROUP * slot_cap
    offset = (jnp.arange(dests, dtype=jnp.int32) % GROUP * slot_cap)[:, None]
    keys = jnp.where(edge_slots < slot_cap, edge_slots + offset, -1)
    return pl.pallas_call(
        select_kernel,
        grid=(groups // STEP,),
        in_specs=[
            pl.BlockSpec((STEP, 1, entries), lambda i: (i, 0, 0)),
            pl.BlockSpec((STEP, 1, entries), lambda i: (i, 0, 0)),
            pl.BlockSpec((row_count, width), lambda i: (0, 0)),
        ],
        out_specs=[
            pl.BlockSpec((STEP * slots, row_count), lambda i: (i, 0)),
            pl.BlockSpec((STEP * slots, width), lambda i: (i, 0)),
            pl.BlockSpec((STEP, 1, slots), lambda i: (i, 0, 0)),
        ],
        out_shape=[
            jax.ShapeDtypeStruct((groups * slots, row_count), bf16),
            jax.ShapeDtypeStruct((groups * slots, width), bf16),
            jax.ShapeDtypeStruct((groups, 1, slots), f32),
        ],
        compiler_params=pltpu.CompilerParams(vmem_limit_bytes=40 * 1024 * 1024),
        cost_estimate=pl.CostEstimate(
            flops=2 * groups * slots * row_count * (width + entries),
            bytes_accessed=2 * (row_count * width + groups * slots * (row_count + width)),
            transcendentals=0,
        ),
    )(
        edge_rows.reshape(groups, 1, entries),
        keys.reshape(groups, 1, entries),
        feats,
    )


def reduce_everywhere(left, bias_column, delta):
    near = lax.axis_size(NEAR)
    far = lax.axis_size(FAR)
    seeds, depth = left.shape
    width = delta.shape[1]
    block = depth // near
    piece = block // far
    columns = jnp.concatenate(
        [
            left.reshape(seeds, near, block),
            jnp.broadcast_to(bias_column[:, None, :], (seeds, near, bias_column.shape[1])),
        ],
        axis=2,
    ).reshape(seeds, -1)
    terms = contract_first(columns, delta).astype(bf16).reshape(near, -1, width)
    summed = jnp.sum(exchange(terms, NEAR).astype(f32), axis=0)
    pieces = jnp.concatenate(
        [
            summed[:block].reshape(far, piece, width),
            jnp.broadcast_to(summed[None, block : block + 2], (far, 2, width)),
        ],
        axis=1,
    ).astype(bf16)
    total = jnp.sum(exchange(pieces, FAR).astype(f32), axis=0)
    bias_total = total[piece]
    spread = exchange(
        jnp.broadcast_to(total.astype(bf16)[None], (far,) + total.shape), FAR
    )
    own = spread[:, :piece].reshape(block, width)
    full = exchange(jnp.broadcast_to(own[None], (near, block, width)), NEAR)
    return full.reshape(depth, width), bias_total


def on_device(
    feats, seed_rows, edge_rows, edge_slots, slot_seeds, w_self, w_neigh, bias, cotangent
):
    edge_rows = edge_rows[0]
    edge_slots = edge_slots[0]
    slot_seeds = slot_seeds[0]
    sources, slot_cap = slot_seeds.shape
    seed_count = seed_rows.shape[0]
    row_count, width = feats.shape
    replicas = lax.axis_size("rep")
    select, partial_value, counts = select_and_sum(feats, edge_rows, edge_slots, slot_cap)
    arrived = exchange(partial_value.reshape(sources, slot_cap, width), DOM)
    arrived_counts = exchange(counts.astype(bf16).reshape(sources, 1, slot_cap), DOM)
    seed_onehot = (
        slot_seeds.reshape(-1)[:, None] == jnp.arange(seed_count, dtype=jnp.int32)[None, :]
    ).astype(bf16)
    agg_sum = contract_first(seed_onehot, arrived.reshape(-1, width))
    degree_raw = contract_first(seed_onehot, arrived_counts.reshape(-1, 1))
    degree = jnp.maximum(degree_raw, 1.0)
    aggregate = (agg_sum / degree).astype(bf16)
    self_rows = jnp.take(feats, seed_rows, axis=0)
    pre = jnp.dot(self_rows, w_self, preferred_element_type=f32)
    pre = pre + jnp.dot(aggregate, w_neigh, preferred_element_type=f32) + bias[None, :]
    hidden_out = jax.nn.gelu(pre).astype(bf16)
    _, pullback = jax.vjp(jax.nn.gelu, pre)
    delta = pullback(cotangent.astype(f32))[0].astype(bf16)
    delta_neigh = (delta.astype(f32) / degree).astype(bf16)
    aggregate_grad = contract_last(delta_neigh, w_neigh).astype(bf16)
    routed = jnp.dot(seed_onehot, aggregate_grad, preferred_element_type=f32).astype(bf16)
    slot_grad = exchange(routed.reshape(sources, slot_cap, width), DOM)
    scale = float(seed_count * lax.axis_size(DOM) * replicas) ** (-0.5)
    marker = jnp.broadcast_to(
        (jnp.arange(16) == 0).astype(bf16)[None, :], (seed_count, 16)
    )
    grads, bias_total = reduce_everywhere(
        jnp.concatenate([self_rows, aggregate], axis=1), marker, delta
    )
    grads = grads.astype(f32) * scale
    self_grad = contract_last(delta, w_self).astype(bf16)
    local_sum = contract_first(select, slot_grad.reshape(-1, width)).astype(bf16)
    shares = exchange(local_sum.reshape(replicas, row_count // replicas, width), "rep")
    feat_grads = jnp.sum(shares.astype(f32), axis=0).astype(bf16)
    return (
        hidden_out,
        self_grad,
        feat_grads,
        grads[:width],
        grads[width:],
        bias_total * scale,
    )


def solution(mesh):
    fine = Mesh(
        np.asarray(mesh.devices).reshape(8, 4, 2, 4), ("z", "x", "c", "rep")
    )
    every = DOM + ("rep",)
    in_specs = (
        P(DOM, None),
        P(every),
        P(every, None, None),
        P(every, None, None),
        P(every, None, None),
        P(),
        P(),
        P(),
        P(every, None),
    )
    out_specs = (P(every, None), P(every, None), P(every, None), P(), P(), P())
    return jax.shard_map(
        on_device, mesh=fine, in_specs=in_specs, out_specs=out_specs, check_vma=False
    )
```

time: 559 us -> 373 us (0.67)
  waiting for transfers between devices: 336 us -> 210 us
  other arithmetic: 36.2 us -> 7.57 us
  between operations: 15.6 us -> 0.92 us
  blocking collectives: 78.1 us -> 68.4 us
  local copies, waits for them, and re-layouts: 28 us -> 18.7 us
  matrix products: 32.8 us -> 25.4 us
  Pallas kernels: 0 us -> 6.67 us
    psum x1 -> x0, waiting for transfers between devices: 198 us -> none  [on_device(): lax.psum((term_self, term_neigh, term_bias), ('dom', 'rep'))]
    psum x1 -> x0, blocking collectives: 78.1 us -> none  [on_device(): lax.psum((term_self, term_neigh, term_bias), ('dom', 'rep'))]
    all_to_all x3 -> x6, waiting for transfers between devices: 138 us -> 210 us  [exchange(): return lax.all_to_all(value, axes, split_axis=0, concat_axis=0, tiled=True)]
    all_to_all x0 -> x2, blocking collectives: none -> 68.4 us  [exchange(): return lax.all_to_all(value, axes, split_axis=0, concat_axis=0, tiled=True)]
    scatter-add x1 -> x0, other arithmetic: 29.3 us -> none  [on_device(): jax.ops.segment_sum(edge_grad.reshape(-1, width), edge_rows.reshape(-1),...]
    gather x1 -> x0, local copies, waits for them, and re-layouts: 17.8 us -> none  [on_device(): gathered = jnp.take(feats, edge_rows, axis=0)]
    dot_general x5 -> x3, matrix products: 21.4 us -> 9.73 us  [the longest x1 3.54 us: on_device(): jnp.dot(aggregate, w_neigh, preferred_element_type=f32)]
    pallas_call x0 -> x1, Pallas kernels: none -> 6.67 us  [select_and_sum(): pl.pallas_call(select_kernel, grid=(groups // STEP,), in_specs=[pl.BlockS...]
  transfers between devices with their start and end apart: 5 -> 6, of which waited for: 3 -> 6; matrix products, arithmetic and copies ran while one was open for 7% -> 6% of each run, Pallas kernels for 0% -> 0%
where the time goes in v1:
time: 373 us; the launch traced here: 372 us
  waiting for transfers between devices  210 us (56%)
  blocking collectives  68.4 us (18%)
  starting transfers between devices  34.2 us (9%)
  matrix products  25.4 us (7%)
  local copies, waits for them, and re-layouts  18.7 us (5%)
  other arithmetic  7.57 us (2%)
  Pallas kernels  6.67 us (2%)
    all_to_all x6, waiting for transfers between devices, exchange(): return lax.all_to_all(value, axes, split_axis=0, concat_axis=0, tiled=True)  210 us
    all_to_all x2, blocking collectives, exchange(): return lax.all_to_all(value, axes, split_axis=0, concat_axis=0, tiled=True)  68.4 us
    all_to_all x6, starting transfers between devices, exchange(): return lax.all_to_all(value, axes, split_axis=0, concat_axis=0, tiled=True)  34.2 us
    dot_general x4, matrix products, contract_first(): lax.dot_general(left, right, (((0,), (0,)), ((), ())), preferred_element_...  12.7 us
  transfers between devices with their start and end apart: 6, of which 6 were waited for; matrix products, arithmetic and copies ran while one was open for 6% of the time, Pallas kernels for 0%

profile of v1, /device:TPU:1, one launch (start us, length us, event | category | flops | bytes accessed | tf_op | source)
XLA Modules:
  0.0 371.9 jit_solution(4539294543281555610)
XLA Ops:
  0.6 0.0 copy-start
  0.7 1.0 reshape_squeeze.3.rows_ref
  1.6 0.8 squeeze.4
  2.5 0.1 add.59
  2.5 0.1 add.60
  2.7 0.0 copy-start.1
  2.7 1.4 copy-done.1
  4.1 6.7 %shard_map.136 = (bf16[2048,1024]{1,0:T(8,128)(2,1)S(1)}, bf16[2048,768]{1,0:T(8,128)(2,1)S(1)}, f32[16,1,128]{2,1,0:T(1,128)S(1)}) custom-call(s32[16,1,256]{2,1,0:T(1,128)S(1)} %reshape_squeeze.3.rows_ref, s32[16,1,256]{2,1,0:T(1,128)S(1)} %compare_select_fusion.keys_ref, bf16[1024,768]{1,0:T(8,128)(2,1)S(1)} %copy-done.1), custom_call_target="tpu_custom_call" | custom-call | flops 4294967296 | bytes 8912896 | tf_op jit(solution)/shard_map/pallas_call | solution.py:62
  10.8 0.0 copy-start.3
  10.8 1.7 copy-done.3
  12.5 1.9 copy-done.4
  14.4 0.1 reshape.140
  14.5 22.2 %all_to_all.40 = bf16[64,1,32]{2,1,0:T(2,128)(2,1)} all-to-all(bf16[64,1,32]{2,1,0:T(2,128)(2,1)S(1)} %reshape.140), channel_id=1, replica_groups=mesh['z'=8,'x'=4,'c'=2,'rep'=4] {'z','x','c'}, dimensions={0} | all-to-all | bytes 8192 | tf_op jit(solution)/shard_map/all_to_all | solution.py:32
  36.7 5.9 %all-to-all-start = ((bf16[64,32,768]{2,1,0:T(8,128)(2,1)}), bf16[64,32,768]{2,1,0:T(8,128)(2,1)}, u32[]{:S(2)}, u32[]{:S(2)}) async-start(bf16[64,32,768]{2,1,0:T(8,128)(2,1)} %bitcast.26), calls=%async_computation | async-start | bytes 6291456 | tf_op jit(solution)/shard_map/all_to_all | solution.py:32
  42.6 0.0 copy-done.9
  42.6 0.1 copy.17
  42.7 0.1 eq.20
  42.8 0.0 copy-done.10
  42.8 1.2 gather_fusion
  44.0 0.6 pad.3.clone
  44.6 0.1 broadcast_select_fusion
  44.7 3.0 fusion.25
  47.7 0.1 reduce.2
  47.8 0.1 reshape.138
  47.9 0.5 fusion
  48.4 66.9 %all-to-all-done = bf16[64,32,768]{2,1,0:T(8,128)(2,1)} async-done(((bf16[64,32,768]{2,1,0:T(8,128)(2,1)}), bf16[64,32,768]{2,1,0:T(8,128)(2,1)}, u32[]{:S(2)}, u32[]{:S(2)}) %all-to-all-start) | async-done | bytes 3145760 | tf_op jit(solution)/shard_map/all_to_all | solution.py:32
  115.3 3.3 fusion.4
  118.7 0.0 copy-start.11
  118.7 0.1 pad_maximum_fusion.1
  118.8 0.3 copy.19
  119.0 0.3 copy-done.11
  119.3 0.2 pad_maximum_fusion
  119.5 0.0 copy-done
  119.6 3.5 fusion.7
  123.1 1.1 convolution_convert_fusion
  124.2 46.2 %all_to_all.41 = bf16[8,208,1024]{2,1,0:T(8,128)(2,1)S(1)} all-to-all(bf16[8,208,1024]{2,1,0:T(8,128)(2,1)S(1)} %bitcast.27), channel_id=1, replica_groups=mesh['z'=8,'x'=4,'c'=2,'rep'=4] {'c','rep'}, dimensions={0} | all-to-all | bytes 6815744 | tf_op jit(solution)/shard_map/all_to_all | solution.py:32
  170.3 0.7 convert_reduce_fusion
  171.1 0.1 reshape.128
  171.2 0.1 broadcast_in_dim.43
  171.3 1.1 pad_maximum_fusion.2
  172.3 4.6 %all-to-all-start.5 = ((bf16[32,8,1024]{2,1,0:T(8,128)(2,1)}), bf16[32,8,1024]{2,1,0:T(8,128)(2,1)S(1)}, u32[]{:S(2)}, u32[]{:S(2)}) async-start(bf16[32,8,1024]{2,1,0:T(8,128)(2,1)} %pad_maximum_fusion.2), calls=%async_computation.5 | async-start | bytes 1048576 | tf_op jit(solution)/shard_map/all_to_all | solution.py:32
  176.9 3.2 convolution_convert_fusion.1
  180.2 13.2 %all-to-all-done.5 = bf16[32,8,1024]{2,1,0:T(8,128)(2,1)S(1)} async-done(((bf16[32,8,1024]{2,1,0:T(8,128)(2,1)}), bf16[32,8,1024]{2,1,0:T(8,128)(2,1)S(1)}, u32[]{:S(2)}, u32[]{:S(2)}) %all-to-all-start.5) | async-done | bytes 524320 | tf_op jit(solution)/shard_map/all_to_all | solution.py:32
  193.3 7.1 %all-to-all-start.2 = ((bf16[64,32,768]{2,1,0:T(8,128)(2,1)}), bf16[64,32,768]{2,1,0:T(8,128)(2,1)}, u32[]{:S(2)}, u32[]{:S(2)}) async-start(bf16[64,32,768]{2,1,0:T(8,128)(2,1)} %bitcast.29), calls=%async_computation.2 | async-start | bytes 6291456 | tf_op jit(solution)/shard_map/all_to_all | solution.py:32
  200.5 0.1 convert_reduce_fusion.1
  200.6 0.0 copy-start.7
  200.6 0.6 copy-done.7
  201.2 72.0 %all-to-all-done.2 = bf16[64,32,768]{2,1,0:T(8,128)(2,1)} async-done(((bf16[64,32,768]{2,1,0:T(8,128)(2,1)}), bf16[64,32,768]{2,1,0:T(8,128)(2,1)}, u32[]{:S(2)}, u32[]{:S(2)}) %all-to-all-start.2) | async-done | bytes 3145760 | tf_op jit(solution)/shard_map/all_to_all | solution.py:32
  273.2 0.9 broadcast_in_dim.44
  274.0 5.5 %all-to-all-start.6 = ((bf16[32,8,1024]{2,1,0:T(8,128)(2,1)}), bf16[32,8,1024]{2,1,0:T(8,128)(2,1)S(1)}, u32[]{:S(2)}, u32[]{:S(2)}) async-start(bf16[32,8,1024]{2,1,0:T(8,128)(2,1)} %broadcast_in_dim.44), calls=%async_computation.6 | async-start | bytes 1048576 | tf_op jit(solution)/shard_map/all_to_all | solution.py:32
  279.5 7.8 %convolution_convert_fusion.2 = bf16[1024,768]{1,0:T(8,128)(2,1)} fusion(bf16[2048,1024]{1,0:T(8,128)(2,1)} %copy-done.4, bf16[2048,768]{1,0:T(8,128)(2,1)} %bitcast.4), kind=kOutput, calls=%fused_computation.8 | convolution fusion | flops 3222011904 | bytes 8912896 | tf_op jit(solution)/shard_map/dot_general | solution.py:20
  287.4 8.5 %all-to-all-done.6 = bf16[32,8,1024]{2,1,0:T(8,128)(2,1)S(1)} async-done(((bf16[32,8,1024]{2,1,0:T(8,128)(2,1)}), bf16[32,8,1024]{2,1,0:T(8,128)(2,1)S(1)}, u32[]{:S(2)}, u32[]{:S(2)}) %all-to-all-start.6) | async-done | bytes 524320 | tf_op jit(solution)/shard_map/all_to_all | solution.py:32
  295.9 0.8 copy-done.5
  296.7 3.6 all-to-all-start.3
  300.3 1.2 broadcast_in_dim.45
  301.5 17.2 %all-to-all-done.3 = bf16[4,256,768]{2,1,0:T(8,128)(2,1)S(1)} async-done(((bf16[4,256,768]{2,1,0:T(8,128)(2,1)}), bf16[4,256,768]{2,1,0:T(8,128)(2,1)S(1)}, u32[]{:S(2)}, u32[]{:S(2)}) %all-to-all-start.3) | async-done | bytes 1572896 | tf_op jit(solution)/shard_map/all_to_all | solution.py:32
  318.6 2.1 broadcast_in_dim.46
  320.7 7.6 %all-to-all-start.7 = ((bf16[8,192,1024]{2,1,0:T(8,128)(2,1)}), bf16[8,192,1024]{2,1,0:T(8,128)(2,1)}, u32[]{:S(2)}, u32[]{:S(2)}) async-start(bf16[8,192,1024]{2,1,0:T(8,128)(2,1)} %broadcast_in_dim.46), calls=%async_computation.7 | async-start | bytes 6291456 | tf_op jit(solution)/shard_map/all_to_all | solution.py:32
  328.3 2.9 convolution_convert_fusion.4
  331.3 1.4 slice_multiply_fusion
  332.6 1.1 reduce_sum.30
  333.7 32.2 %all-to-all-done.7 = bf16[8,192,1024]{2,1,0:T(8,128)(2,1)} async-done(((bf16[8,192,1024]{2,1,0:T(8,128)(2,1)}), bf16[8,192,1024]{2,1,0:T(8,128)(2,1)}, u32[]{:S(2)}, u32[]{:S(2)}) %all-to-all-start.7) | async-done | bytes 3145760 | tf_op jit(solution)/shard_map/all_to_all | solution.py:32
  365.9 2.8 convert_multiply_fusion
  368.7 3.3 fusion.24
  (21 shorter events, 0.2 us)
Async XLA Ops:
  0.6 118.9 %copy-start = (bf16[768,1024]{1,0:T(8,128)(2,1)S(1)}, bf16[768,1024]{1,0:T(8,128)(2,1)}, u32[]{:S(2)}) copy-start(bf16[768,1024]{1,0:T(8,128)(2,1)} %param.15) | copy-start | bytes 4718596
  2.7 1.4 copy-start.1
  10.8 1.7 copy-start.3
  12.4 2.0 copy-start.4
  36.7 5.9 %copy-start.9 = (s32[1,64,32]{1,2,0:T(8,128)S(1)}, s32[1,64,32]{1,2,0:T(8,128)}, u32[]{:S(2)}) copy-start(s32[1,64,32]{1,2,0:T(8,128)} %param.13) | copy-start | bytes 24580
  36.7 6.0 %copy-start.10 = (s32[256]{0:T(256)S(1)}, s32[256]{0:T(256)}, u32[]{:S(2)}) copy-start(s32[256]{0:T(256)} %param.10) | copy-start | bytes 3076
  36.7 6.1 %copy-start.2 = (bf16[1024,768]{1,0:T(8,128)(2,1)S(1)}, bf16[1024,768]{1,0:T(8,128)(2,1)}, u32[]{:S(2)}) copy-start(bf16[1024,768]{1,0:T(8,128)(2,1)} %feats_ref.1) | copy-start | bytes 4718596
  36.7 78.6 %all-to-all-start = ((bf16[64,32,768]{2,1,0:T(8,128)(2,1)}), bf16[64,32,768]{2,1,0:T(8,128)(2,1)}, u32[]{:S(2)}, u32[]{:S(2)}) async-start(bf16[64,32,768]{2,1,0:T(8,128)(2,1)} %bitcast.26), calls=%async_computation | async-start | bytes 6291456 | tf_op jit(solution)/shard_map/all_to_all | solution.py:32
  44.0 3.7 copy-start.8
  118.7 0.7 copy-start.11
  123.1 53.8 %copy-start.6 = (bf16[256,1024]{1,0:T(8,128)(2,1)}, bf16[256,1024]{1,0:T(8,128)(2,1)S(1)}, u32[]{:S(2)}) copy-start(bf16[256,1024]{1,0:T(8,128)(2,1)S(1)} %get-tuple-element.14) | copy-start | bytes 1572868
  172.3 21.0 %all-to-all-start.5 = ((bf16[32,8,1024]{2,1,0:T(8,128)(2,1)}), bf16[32,8,1024]{2,1,0:T(8,128)(2,1)S(1)}, u32[]{:S(2)}, u32[]{:S(2)}) async-start(bf16[32,8,1024]{2,1,0:T(8,128)(2,1)} %pad_maximum_fusion.2), calls=%async_computation.5 | async-start | bytes 1048576 | tf_op jit(solution)/shard_map/all_to_all | solution.py:32
  193.3 79.9 %all-to-all-start.2 = ((bf16[64,32,768]{2,1,0:T(8,128)(2,1)}), bf16[64,32,768]{2,1,0:T(8,128)(2,1)}, u32[]{:S(2)}, u32[]{:S(2)}) async-start(bf16[64,32,768]{2,1,0:T(8,128)(2,1)} %bitcast.29), calls=%async_computation.2 | async-start | bytes 6291456 | tf_op jit(solution)/shard_map/all_to_all | solution.py:32
  200.6 0.6 copy-start.7
  274.0 21.9 %all-to-all-start.6 = ((bf16[32,8,1024]{2,1,0:T(8,128)(2,1)}), bf16[32,8,1024]{2,1,0:T(8,128)(2,1)S(1)}, u32[]{:S(2)}, u32[]{:S(2)}) async-start(bf16[32,8,1024]{2,1,0:T(8,128)(2,1)} %broadcast_in_dim.44), calls=%async_computation.6 | async-start | bytes 1048576 | tf_op jit(solution)/shard_map/all_to_all | solution.py:32
  295.9 0.8 copy-start.5
  296.7 21.9 %all-to-all-start.3 = ((bf16[4,256,768]{2,1,0:T(8,128)(2,1)}), bf16[4,256,768]{2,1,0:T(8,128)(2,1)S(1)}, u32[]{:S(2)}, u32[]{:S(2)}) async-start(bf16[4,256,768]{2,1,0:T(8,128)(2,1)} %bitcast.34), calls=%async_computation.3 | async-start | bytes 3145728 | tf_op jit(solution)/shard_map/all_to_all | solution.py:32
  320.7 45.2 %all-to-all-start.7 = ((bf16[8,192,1024]{2,1,0:T(8,128)(2,1)}), bf16[8,192,1024]{2,1,0:T(8,128)(2,1)}, u32[]{:S(2)}, u32[]{:S(2)}) async-start(bf16[8,192,1024]{2,1,0:T(8,128)(2,1)} %broadcast_in_dim.46), calls=%async_computation.7 | async-start | bytes 6291456 | tf_op jit(solution)/shard_map/all_to_all | solution.py:32

commit v2 on v1

v2 whole, which is shorter than its diff:
```python
import jax
import jax.numpy as jnp
import numpy as np
from jax import lax
from jax.experimental import pallas as pl
from jax.experimental.pallas import tpu as pltpu
from jax.sharding import Mesh, PartitionSpec as P

DOM = ("z", "x", "c")
NEAR = ("c", "rep")
FAR = ("z", "x")
bf16 = jnp.bfloat16
f32 = jnp.float32

GROUP = 4
STEP = 4
SPLIT = 4
EXTRA = 128
FIRST = 384
VMEM = pltpu.CompilerParams(vmem_limit_bytes=48 * 1024 * 1024)
MARGIN = 16


def contract_first(left, right):
    return lax.dot_general(
        left, right, (((0,), (0,)), ((), ())), preferred_element_type=f32
    )


def contract_last(left, right):
    return lax.dot_general(
        left, right, (((1,), (1,)), ((), ())), preferred_element_type=f32
    )


def exchange(value, axes):
    return lax.all_to_all(value, axes, split_axis=0, concat_axis=0, tiled=True)


def cost(flops, bytes_accessed):
    return pl.CostEstimate(flops=flops, bytes_accessed=bytes_accessed, transcendentals=0)


def select_kernel(rows_ref, keys_ref, feats_ref, select_ref, partial_ref):
    row_count, width = feats_ref.shape
    entries = rows_ref.shape[2]
    part = select_ref.shape[1] // STEP
    slots = SPLIT * part
    row_ids = lax.broadcasted_iota(jnp.int32, (row_count, entries), 0)
    slot_ids = lax.broadcasted_iota(jnp.int32, (slots, entries), 0)
    lanes = lax.broadcasted_iota(jnp.int32, (part, EXTRA), 1)
    for step in range(STEP):
        here = slice(step * part, (step + 1) * part)
        by_row = jnp.where(row_ids == rows_ref[step], 1.0, 0.0).astype(bf16)
        hits = jnp.where(slot_ids == keys_ref[step], 1.0, 0.0)
        chosen = contract_last(hits.astype(bf16), by_row).astype(bf16)
        count = jnp.sum(hits, axis=1, keepdims=True)
        tail = jnp.zeros((part, EXTRA), f32)
        for j in range(SPLIT):
            select_ref[j, here, :] = chosen[j * part : (j + 1) * part]
            tail = jnp.where(lanes == j, count[j * part : (j + 1) * part], tail)
        partial_ref[here, SPLIT * width :] = tail.astype(bf16)
    for j in range(SPLIT):
        partial_ref[:, j * width : (j + 1) * width] = jnp.dot(
            select_ref[j], feats_ref[...], preferred_element_type=f32
        ).astype(bf16)


def select_and_sum(feats, edge_rows, edge_slots, slot_cap):
    dests, entry_cap = edge_rows.shape
    row_count, width = feats.shape
    groups = dests // GROUP
    entries = GROUP * entry_cap
    s_count = slot_cap // SPLIT
    part = GROUP * s_count
    wide = SPLIT * width + EXTRA
    place = (jnp.arange(dests, dtype=jnp.int32) % GROUP * s_count)[:, None]
    keys = edge_slots // s_count * part + place + edge_slots % s_count
    keys = jnp.where(edge_slots < slot_cap, keys, -1)
    return pl.pallas_call(
        select_kernel,
        grid=(groups // STEP,),
        in_specs=[
            pl.BlockSpec((STEP, 1, entries), lambda i: (i, 0, 0)),
            pl.BlockSpec((STEP, 1, entries), lambda i: (i, 0, 0)),
            pl.BlockSpec((row_count, width), lambda i: (0, 0)),
        ],
        out_specs=[
            pl.BlockSpec((SPLIT, STEP * part, row_count), lambda i: (0, i, 0)),
            pl.BlockSpec((STEP * part, wide), lambda i: (i, 0)),
        ],
        out_shape=[
            jax.ShapeDtypeStruct((SPLIT, groups * part, row_count), bf16),
            jax.ShapeDtypeStruct((groups * part, wide), bf16),
        ],
        compiler_params=VMEM,
        cost_estimate=cost(
            2 * SPLIT * groups * part * row_count * (width + entries),
            2 * (row_count * width + groups * part * (SPLIT * row_count + wide)),
        ),
    )(
        edge_rows.reshape(groups, 1, entries),
        keys.reshape(groups, 1, entries),
        feats,
    )


def middle_kernel(
    arrived_ref,
    seeds_ref,
    base_ref,
    w_neigh_ref,
    cotangent_ref,
    hidden_ref,
    delta_ref,
    aggregate_ref,
    first_ref,
    second_ref,
    pre_ref,
    neigh_ref,
    degree_ref,
):
    seed_count = base_ref.shape[0]
    width = w_neigh_ref.shape[0]
    sent = seeds_ref.shape[2]
    ids = lax.broadcasted_iota(jnp.int32, (seed_count, sent), 0)
    lanes = lax.broadcasted_iota(jnp.int32, (seed_count, EXTRA), 1)

    def routing(j):
        return jnp.where(ids == seeds_ref[j], 1.0, 0.0).astype(bf16)

    total = jnp.zeros((seed_count, width), f32)
    counts = jnp.zeros((seed_count, EXTRA), f32)
    for j in range(SPLIT):
        route = routing(j)
        total += jnp.dot(
            route, arrived_ref[:, j * width : (j + 1) * width], preferred_element_type=f32
        )
        found = jnp.dot(route, arrived_ref[:, SPLIT * width :], preferred_element_type=f32)
        counts += jnp.where(lanes == j, found, 0.0)
    degree = jnp.maximum(jnp.sum(counts, axis=1, keepdims=True), 1.0)
    degree_ref[...] = jnp.broadcast_to(degree, (seed_count, EXTRA))
    aggregate_ref[...] = (total / degree).astype(bf16)
    pre_ref[...] = base_ref[...] + jnp.dot(
        aggregate_ref[...], w_neigh_ref[...], preferred_element_type=f32
    )

    rows = 16
    slope = (2.0 / np.pi) ** 0.5

    @pl.loop(0, seed_count // rows)
    def _(i):
        here = pl.ds(pl.multiple_of(i * rows, rows), rows)
        pre = pre_ref[here, :]
        square = pre * pre
        bend = jnp.tanh(slope * pre * (1.0 + 0.044715 * square))
        half = 0.5 * (1.0 + bend)
        hidden_ref[here, :] = (pre * half).astype(bf16)
        steep = half + 0.5 * pre * (1.0 - bend * bend) * (
            slope * (1.0 + 3 * 0.044715 * square)
        )
        delta = (cotangent_ref[here, :].astype(f32) * steep).astype(bf16)
        delta_ref[here, :] = delta
        neigh_ref[here, :] = (delta.astype(f32) / degree_ref[here, 0:1]).astype(bf16)

    grad = contract_last(neigh_ref[...], w_neigh_ref[...]).astype(bf16)
    rest = width - FIRST
    for j in range(SPLIT):
        routed = contract_first(routing(j), grad).astype(bf16)
        first_ref[:, j * FIRST : (j + 1) * FIRST] = routed[:, :FIRST]
        second_ref[:, j * rest : (j + 1) * rest] = routed[:, FIRST:]


def middle(arrived, seeds, base, w_neigh, cotangent):
    sent = arrived.shape[0]
    seed_count, hidden = base.shape
    width = w_neigh.shape[0]
    return pl.pallas_call(
        middle_kernel,
        out_shape=[
            jax.ShapeDtypeStruct((seed_count, hidden), bf16),
            jax.ShapeDtypeStruct((seed_count, hidden), bf16),
            jax.ShapeDtypeStruct((seed_count, width), bf16),
            jax.ShapeDtypeStruct((sent, SPLIT * FIRST), bf16),
            jax.ShapeDtypeStruct((sent, SPLIT * (width - FIRST)), bf16),
        ],
        scratch_shapes=[
            pltpu.VMEM((seed_count, hidden), f32),
            pltpu.VMEM((seed_count, hidden), bf16),
            pltpu.VMEM((seed_count, EXTRA), f32),
        ],
        compiler_params=VMEM,
        cost_estimate=cost(
            4 * seed_count * width * (SPLIT * sent + hidden),
            2 * (2 * arrived.size + w_neigh.size + 5 * base.size),
        ),
    )(arrived, seeds, base, w_neigh, cotangent)


def terms_kernel(self_ref, aggregate_ref, delta_ref, out_ref):
    near, tall, hidden = out_ref.shape
    block = tall - MARGIN
    delta = delta_ref[...]
    half = near // 2
    for side, left in enumerate((self_ref, aggregate_ref)):
        product = contract_first(left[...], delta).astype(bf16)
        for b in range(half):
            out_ref[side * half + b, :block, :] = product[b * block : (b + 1) * block]
    column = jnp.sum(delta.astype(f32), axis=0, keepdims=True)
    first = lax.broadcasted_iota(jnp.int32, (MARGIN, hidden), 0) == 0
    margin = jnp.where(first, column, 0.0).astype(bf16)
    for b in range(near):
        out_ref[b, block:, :] = margin


def reduce_everywhere(self_rows, aggregate, delta):
    near = lax.axis_size(NEAR)
    far = lax.axis_size(FAR)
    seeds, width = self_rows.shape
    hidden = delta.shape[1]
    block = 2 * width // near
    piece = block // far
    terms = pl.pallas_call(
        terms_kernel,
        out_shape=jax.ShapeDtypeStruct((near, block + MARGIN, hidden), bf16),
        compiler_params=VMEM,
        cost_estimate=cost(4 * seeds * width * hidden, 8 * width * hidden),
    )(self_rows, aggregate, delta)
    summed = lax.psum_scatter(
        terms.reshape(-1, hidden), NEAR, scatter_dimension=0, tiled=True
    )
    pieces = jnp.concatenate(
        [
            summed[:block].reshape(far, piece, hidden),
            jnp.broadcast_to(summed[None, block : block + 2], (far, 2, hidden)),
        ],
        axis=1,
    )
    total = jnp.sum(exchange(pieces, FAR).astype(f32), axis=0)
    bias_total = total[piece]
    spread = exchange(
        jnp.broadcast_to(total.astype(bf16)[None], (far,) + total.shape), FAR
    )
    own = spread[:, :piece].reshape(block, hidden)
    full = lax.all_gather(own, NEAR, axis=0, tiled=True)
    return full, bias_total, spread


def after(value, earlier):
    def kernel(value_ref, earlier_ref, out_ref):
        pass

    return pl.pallas_call(
        kernel,
        in_specs=[pl.BlockSpec(memory_space=pl.ANY)] * 2,
        out_specs=pl.BlockSpec(memory_space=pl.ANY),
        out_shape=jax.ShapeDtypeStruct(value.shape, value.dtype),
        input_output_aliases={0: 0},
    )(value, earlier)


def on_device(
    feats, seed_rows, edge_rows, edge_slots, slot_seeds, w_self, w_neigh, bias, cotangent
):
    edge_rows = edge_rows[0]
    edge_slots = edge_slots[0]
    slot_seeds = slot_seeds[0]
    sources, slot_cap = slot_seeds.shape
    s_count = slot_cap // SPLIT
    seed_count = seed_rows.shape[0]
    row_count, width = feats.shape
    replicas = lax.axis_size("rep")
    select, partial_value = select_and_sum(feats, edge_rows, edge_slots, slot_cap)
    arrived = exchange(partial_value.reshape(sources, s_count, -1), DOM)
    seeds = slot_seeds.reshape(sources, SPLIT, s_count).transpose(1, 0, 2)
    seeds = seeds.reshape(SPLIT, 1, sources * s_count)
    self_rows = jnp.take(feats, seed_rows, axis=0)
    base = jnp.dot(self_rows, w_self, preferred_element_type=f32) + bias[None, :]
    hidden_out, delta, aggregate, first, second = middle(
        arrived.reshape(sources * s_count, -1), seeds, base, w_neigh, cotangent
    )

    def back(routed):
        columns = routed.shape[1] // SPLIT
        slot_grad = exchange(routed.reshape(sources, s_count, -1), DOM)
        slot_grad = slot_grad.reshape(sources * s_count, -1)
        local = sum(
            contract_first(select[j], slot_grad[:, j * columns : (j + 1) * columns])
            for j in range(SPLIT)
        )
        return local.astype(bf16)

    grads, bias_total, done = reduce_everywhere(self_rows, aggregate, delta)
    share1 = lax.psum_scatter(back(first), "rep", scatter_dimension=0, tiled=True)
    local2 = back(after(second, done))
    shares2 = exchange(local2.reshape(replicas, row_count // replicas, -1), "rep")
    share2 = jnp.sum(shares2.astype(f32), axis=0).astype(bf16)
    feat_grads = jnp.concatenate([share1, share2], axis=1)
    self_grad = contract_last(delta, w_self).astype(bf16)
    scale = float(seed_count * lax.axis_size(DOM) * replicas) ** (-0.5)
    grads = grads.astype(f32) * scale
    return (
        hidden_out,
        self_grad,
        feat_grads,
        grads[:width],
        grads[width:],
        bias_total * scale,
    )


def solution(mesh):
    fine = Mesh(
        np.asarray(mesh.devices).reshape(8, 4, 2, 4), ("z", "x", "c", "rep")
    )
    every = DOM + ("rep",)
    in_specs = (
        P(DOM, None),
        P(every),
        P(every, None, None),
        P(every, None, None),
        P(every, None, None),
        P(),
        P(),
        P(),
        P(every, None),
    )
    out_specs = (P(every, None), P(every, None), P(every, None), P(), P(), P())
    return jax.shard_map(
        on_device, mesh=fine, in_specs=in_specs, out_specs=out_specs, check_vma=False
    )
```

time: 373 us -> 309 us (0.83)
  waiting for transfers between devices: 210 us -> 89.6 us
  blocking collectives: 68.4 us -> 113 us
  between operations: 0.92 us -> 15.8 us
  starting transfers between devices: 34.2 us -> 23.5 us
  Pallas kernels: 6.67 us -> 15.9 us
  matrix products: 25.4 us -> 19.9 us
    all_to_all x6 -> x3, waiting for transfers between devices: 210 us -> 89.5 us  [exchange(): return lax.all_to_all(value, axes, split_axis=0, concat_axis=0, tiled=True)]
    all_to_all x2 -> x3, blocking collectives: 68.4 us -> 113 us  [exchange(): return lax.all_to_all(value, axes, split_axis=0, concat_axis=0, tiled=True)]
    all_to_all x6 -> x3, starting transfers between devices: 34.2 us -> 23.2 us  [exchange(): return lax.all_to_all(value, axes, split_axis=0, concat_axis=0, tiled=True)]
    dot_general x3 -> x1, matrix products: 9.73 us -> 1.57 us  [on_device(): jnp.dot(self_rows, w_self, preferred_element_type=f32) + bias[None, :]]
    pallas_call x0 -> x3, Pallas kernels: none -> 8.05 us  [the longest x1 7.04 us: middle(): pl.pallas_call(middle_kernel, out_shape=[jax.ShapeDtypeStruct((seed_count...]
    dot_general x4 -> x8, matrix products: 12.7 us -> 17 us  [contract_first(): lax.dot_general(left, right, (((0,), (0,)), ((), ())), preferred_element_...]
    unnamed x25 -> x38, local copies, waits for them, and re-layouts: 6.85 us -> 8.44 us
  transfers between devices with their start and end apart: 6 -> 6, of which waited for: 6 -> 3; matrix products, arithmetic and copies ran while one was open for 6% -> 9% of each run, Pallas kernels for 0% -> 0%
where the time goes in v2:
time: 309 us; the launch traced here: 307 us
  blocking collectives  113 us (37%)
  waiting for transfers between devices  89.6 us (29%)
  starting transfers between devices  23.5 us (8%)
  matrix products  19.9 us (6%)
  local copies, waits for them, and re-layouts  18.9 us (6%)
  Pallas kernels  15.9 us (5%)
  between operations  15.8 us (5%)
  other arithmetic  9.72 us (3%)
    all_to_all x3, blocking collectives, exchange(): return lax.all_to_all(value, axes, split_axis=0, concat_axis=0, tiled=True)  113 us
    all_to_all x3, waiting for transfers between devices, exchange(): return lax.all_to_all(value, axes, split_axis=0, concat_axis=0, tiled=True)  89.5 us
    all_to_all x3, starting transfers between devices, exchange(): return lax.all_to_all(value, axes, split_axis=0, concat_axis=0, tiled=True)  23.2 us
    dot_general x8, matrix products, contract_first(): lax.dot_general(left, right, (((0,), (0,)), ((), ())), preferred_element_...  17 us
    unnamed x38, local copies, waits for them, and re-layouts  8.44 us
    pallas_call x1, Pallas kernels, select_and_sum(): pl.pallas_call(select_kernel, grid=(groups // STEP,), in_specs=[pl.BlockS...  7.87 us
    pallas_call x1, Pallas kernels, middle(): pl.pallas_call(middle_kernel, out_shape=[jax.ShapeDtypeStruct((seed_count...  7.04 us
  transfers between devices with their start and end apart: 6, of which 3 were waited for; matrix products, arithmetic and copies ran while one was open for 9% of the time, Pallas kernels for 0%

profile of v2, /device:TPU:1, one launch (start us, length us, event | category | flops | bytes accessed | tf_op | source)
XLA Modules:
  0.0 306.5 jit_solution(1149370871671234863)
XLA Ops:
  8.0 0.0 copy-start
  8.0 1.0 reshape_squeeze.6.rows_ref
  9.0 0.8 squeeze.20
  9.8 0.1 add.98
  9.9 0.1 add.99
  10.0 0.1 compare_select_fusion.keys_ref
  10.2 0.0 copy-start.3
  10.2 1.4 copy-done.3
  11.6 7.9 %shard_map.136 = (bf16[4,512,1024]{2,1,0:T(8,128)(2,1)}, bf16[512,3200]{1,0:T(8,128)(2,1)S(1)}) custom-call(s32[16,1,256]{2,1,0:T(1,128)S(1)} %reshape_squeeze.6.rows_ref, s32[16,1,256]{2,1,0:T(1,128)S(1)} %compare_select_fusion.keys_ref, bf16[1024,768]{1,0:T(8,128)(2,1)S(1)} %copy-done.3), custom_call_target="tpu_custom_call" | custom-call | flops 4294967296 | bytes 9043968 | tf_op jit(solution)/shard_map/pallas_call | solution.py:80
  19.5 1.8 copy-done.5
  21.3 13.3 %all-to-all-start = ((bf16[64,8,3200]{2,1,0:T(8,128)(2,1)}), bf16[64,8,3200]{2,1,0:T(8,128)(2,1)}, u32[]{:S(2)}, u32[]{:S(2)}) async-start(bf16[64,8,3200]{2,1,0:T(8,128)(2,1)} %bitcast.38), calls=%async_computation | async-start | bytes 6553600 | tf_op jit(solution)/shard_map/all_to_all | solution.py:37
  34.5 0.0 reduce-scatter.5.cloned.1.call-start
  34.6 0.1 copy.17
  34.7 0.1 reshape.218.seeds_ref
  34.9 0.0 copy-start.17
  34.9 1.9 gather_fusion
  36.8 1.1 broadcast_select_fusion.self_ref
  37.9 1.6 convolution_add_fusion.base_ref
  39.5 70.3 %all-to-all-done = bf16[64,8,3200]{2,1,0:T(8,128)(2,1)} async-done(((bf16[64,8,3200]{2,1,0:T(8,128)(2,1)}), bf16[64,8,3200]{2,1,0:T(8,128)(2,1)}, u32[]{:S(2)}, u32[]{:S(2)}) %all-to-all-start) | async-done | bytes 3276832 | tf_op jit(solution)/shard_map/all_to_all | solution.py:37
  109.8 1.2 copy-done.6
  111.0 1.0 copy-done.9
  112.1 7.0 %shard_map.137 = (bf16[256,1024]{1,0:T(8,128)(2,1)}, bf16[256,1024]{1,0:T(8,128)(2,1)S(1)}, bf16[256,768]{1,0:T(8,128)(2,1)S(1)}, bf16[512,1536]{1,0:T(8,128)(2,1)S(1)}, bf16[512,1536]{1,0:T(8,128)(2,1)S(1)}) custom-call(bf16[512,3200]{1,0:T(8,128)(2,1)} %bitcast.1.arrived_ref, s32[4,1,512]{2,1,0:T(1,128)S(1)} %reshape.218.seeds_ref, ...), custom_call_target="tpu_custom_call" | custom-call | flops 2415919104 | bytes 10747904 | tf_op jit(solution)/shard_map/pallas_call | solution.py:178
  119.1 0.0 copy-start.2
  119.1 1.1 copy-done.2
  120.3 1.0 shard_map.138
  121.3 1.7 copy-done.1
  123.0 0.0 reduce-scatter.5.cloned.1.call-update
  123.1 45.4 %all_to_all.30 = bf16[64,8,1536]{2,1,0:T(8,128)(2,1)S(1)} all-to-all(bf16[64,8,1536]{2,1,0:T(8,128)(2,1)S(1)} %bitcast.39), channel_id=1, replica_groups=mesh['z'=8,'x'=4,'c'=2,'rep'=4] {'z','x','c'}, dimensions={0} | all-to-all | bytes 3145728 | tf_op jit(solution)/shard_map/all_to_all | solution.py:37
  168.5 3.7 %fusion.4 = f32[1024,384]{1,0:T(8,128)} fusion(bf16[4,512,1024]{2,1,0:T(8,128)(2,1)} %get-tuple-element.16, bf16[512,1536]{1,0:T(8,128)(2,1)S(1)} %bitcast.42), kind=kOutput, calls=%fused_computation.10 | convolution fusion | flops 402653184 | bytes 3014656 | tf_op jit(solution)/shard_map/dot_general | solution.py:25
  172.2 0.0 copy-done.11
  172.2 3.2 %fusion.12 = f32[1024,384]{1,0:T(8,128)} fusion(bf16[4,512,1024]{2,1,0:T(8,128)(2,1)} %get-tuple-element.16, bf16[512,1536]{1,0:T(8,128)(2,1)S(1)} %bitcast.43), kind=kOutput, calls=%fused_computation.18 | convolution fusion | flops 402653184 | bytes 3014656 | tf_op jit(solution)/shard_map/dot_general | solution.py:25
  175.4 1.0 slice.82
  176.4 0.9 reshape.204
  177.4 0.1 broadcast_in_dim.31
  177.4 2.1 pad_maximum_fusion
  179.5 5.6 %all-to-all-start.2 = ((bf16[32,8,1024]{2,1,0:T(8,128)(2,1)}), bf16[32,8,1024]{2,1,0:T(8,128)(2,1)}, u32[]{:S(2)}, u32[]{:S(2)}) async-start(bf16[32,8,1024]{2,1,0:T(8,128)(2,1)} %pad_maximum_fusion), calls=%async_computation.4 | async-start | bytes 1048576 | tf_op jit(solution)/shard_map/all_to_all | solution.py:37
  185.1 0.2 reduce-scatter.3.cloned.1.call-start
  185.4 0.0 copy-start.13
  185.4 0.0 copy-start.14
  185.4 2.1 fusion.8
  187.5 0.1 copy-done.14
  187.6 2.9 add_convert_fusion.1
  190.5 0.0 reduce-scatter.3.cloned.1.call-update
  190.5 0.0 all-gather.2.cloned.1.call-start
  190.5 11.0 %all-to-all-done.2 = bf16[32,8,1024]{2,1,0:T(8,128)(2,1)} async-done(((bf16[32,8,1024]{2,1,0:T(8,128)(2,1)}), bf16[32,8,1024]{2,1,0:T(8,128)(2,1)}, u32[]{:S(2)}, u32[]{:S(2)}) %all-to-all-start.2) | async-done | bytes 524320 | tf_op jit(solution)/shard_map/all_to_all | solution.py:37
  201.5 1.1 convert_reduce_fusion
  202.7 0.1 broadcast_in_dim.32
  202.7 20.1 %all_to_all.31.earlier_ref = bf16[32,8,1024]{2,1,0:T(8,128)(2,1)S(1)} all-to-all(bf16[32,8,1024]{2,1,0:T(8,128)(2,1)S(1)} %broadcast_in_dim.32), channel_id=1, replica_groups=mesh['z'=8,'x'=4,'c'=2,'rep'=4] {'z','x'}, dimensions={0} | all-to-all | bytes 1048576 | tf_op jit(solution)/shard_map/all_to_all | solution.py:37
  222.8 1.0 reshape.208
  223.8 0.0 all-gather.2.cloned.1.call-update
  223.9 47.7 %all_to_all.32 = bf16[64,8,1536]{2,1,0:T(8,128)(2,1)S(1)} all-to-all(bf16[64,8,1536]{2,1,0:T(8,128)(2,1)} %bitcast.37), channel_id=1, replica_groups=mesh['z'=8,'x'=4,'c'=2,'rep'=4] {'z','x','c'}, dimensions={0} | all-to-all | bytes 3145728 | tf_op jit(solution)/shard_map/all_to_all | solution.py:37
  271.5 2.0 fusion.2
  273.5 0.7 fusion.10
  274.2 0.7 fusion.6
  275.0 1.7 add_convert_fusion
  276.6 4.3 %all-to-all-start.5 = ((bf16[4,256,384]{2,1,0:T(8,128)(2,1)}), bf16[4,256,384]{2,1,0:T(8,128)(2,1)S(1)}, u32[]{:S(2)}, u32[]{:S(2)}) async-start(bf16[4,256,384]{2,1,0:T(8,128)(2,1)} %bitcast.41), calls=%async_computation.7 | async-start | bytes 1572864 | tf_op jit(solution)/shard_map/all_to_all | solution.py:37
  281.0 1.4 convolution_convert_fusion
  282.3 0.6 slice_multiply_fusion
  282.9 8.2 %all-to-all-done.5 = bf16[4,256,384]{2,1,0:T(8,128)(2,1)S(1)} async-done(((bf16[4,256,384]{2,1,0:T(8,128)(2,1)}), bf16[4,256,384]{2,1,0:T(8,128)(2,1)S(1)}, u32[]{:S(2)}, u32[]{:S(2)}) %all-to-all-start.5) | async-done | bytes 786464 | tf_op jit(solution)/shard_map/all_to_all | solution.py:37
  291.1 0.2 reduce_sum.22
  291.3 0.0 reduce-scatter.3.cloned.1.call-done
  291.3 1.7 pad_maximum_fusion.1
  293.0 2.8 convert_multiply_fusion
  295.8 3.3 %fusion.35 = (f32[768,1024]{1,0:T(8,128)}, f32[768,1024]{1,0:T(8,128)}) fusion(f32[1536,1024]{1,0:T(8,128)S(1)} %convert_multiply_fusion), kind=kLoop, calls=%fused_computation.57 | loop fusion | bytes 12582912 | tf_op jit(solution)/shard_map/slice | solution.py:307
  (34 shorter events, 0.1 us)
Async XLA Ops:
  8.0 29.9 %copy-start = (bf16[768,1024]{1,0:T(8,128)(2,1)S(1)}, bf16[768,1024]{1,0:T(8,128)(2,1)}, u32[]{:S(2)}) copy-start(bf16[768,1024]{1,0:T(8,128)(2,1)} %param.14) | copy-start | bytes 4718596
  10.2 1.4 copy-start.3
  19.5 1.8 copy-start.5
  21.3 13.3 %copy-start.16 = (s32[1,64,32]{1,2,0:T(8,128)S(1)}, s32[1,64,32]{1,2,0:T(8,128)}, u32[]{:S(2)}) copy-start(s32[1,64,32]{1,2,0:T(8,128)} %param.13) | copy-start | bytes 24580
  21.3 13.6 %copy-start.18 = (s32[256]{0:T(256)S(1)}, s32[256]{0:T(256)}, u32[]{:S(2)}) copy-start(s32[256]{0:T(256)} %param.10) | copy-start | bytes 3076
  21.3 13.6 %copy-start.4 = (bf16[1024,768]{1,0:T(8,128)(2,1)S(1)}, bf16[1024,768]{1,0:T(8,128)(2,1)}, u32[]{:S(2)}) copy-start(bf16[1024,768]{1,0:T(8,128)(2,1)} %feats_ref.1) | copy-start | bytes 4718596
  21.3 88.6 %all-to-all-start = ((bf16[64,8,3200]{2,1,0:T(8,128)(2,1)}), bf16[64,8,3200]{2,1,0:T(8,128)(2,1)}, u32[]{:S(2)}, u32[]{:S(2)}) async-start(bf16[64,8,3200]{2,1,0:T(8,128)(2,1)} %bitcast.38), calls=%async_computation | async-start | bytes 6553600 | tf_op jit(solution)/shard_map/all_to_all | solution.py:37
  34.5 140.8 %reduce-scatter.5.cloned.1.call-start = ((), (), s32[]{:S(2)}) async-start(), calls=%async_computation.9 | async-start | bytes 3833856 | tf_op jit(solution)/shard_map/reduce_scatter | solution.py:229
  34.9 3.1 %copy-start.17 = (f32[1024]{0:T(1024)S(1)}, f32[1024]{0:T(1024)}, u32[]{:S(2)}) copy-start(f32[1024]{0:T(1024)} %param.16) | copy-start | bytes 12292
  109.8 1.2 copy-start.6
  111.0 1.0 copy-start.9
  119.1 1.1 copy-start.2
  120.3 1.0 copy-start.7
  121.3 1.7 copy-start.1
  168.5 3.7 %copy-start.11 = (bf16[64,8,1536]{2,1,0:T(8,128)(2,1)}, bf16[64,8,1536]{2,1,0:T(8,128)(2,1)S(1)}, u32[]{:S(2)}) copy-start(bf16[64,8,1536]{2,1,0:T(8,128)(2,1)S(1)} %all_to_all.30) | copy-start | bytes 4718596
  175.4 2.0 slice-start
  176.4 9.0 %copy-start.12 = (bf16[64,8,1536]{2,1,0:T(8,128)(2,1)S(1)}, bf16[64,8,1536]{2,1,0:T(8,128)(2,1)}, u32[]{:S(2)}) copy-start(bf16[64,8,1536]{2,1,0:T(8,128)(2,1)} %copy-done.11) | copy-start | bytes 4718596
  179.5 22.0 %all-to-all-start.2 = ((bf16[32,8,1024]{2,1,0:T(8,128)(2,1)}), bf16[32,8,1024]{2,1,0:T(8,128)(2,1)}, u32[]{:S(2)}, u32[]{:S(2)}) async-start(bf16[32,8,1024]{2,1,0:T(8,128)(2,1)} %pad_maximum_fusion), calls=%async_computation.4 | async-start | bytes 1048576 | tf_op jit(solution)/shard_map/all_to_all | solution.py:37
  185.1 106.2 %reduce-scatter.3.cloned.1.call-start = ((), (), s32[]{:S(2)}) async-start(), calls=%async_computation.8 | async-start | bytes 983040 | tf_op jit(solution)/shard_map/reduce_scatter | solution.py:294
  185.4 2.1 copy-start.13
  185.4 2.2 copy-start.14
  190.5 102.5 %all-gather.2.cloned.1.call-start = ((), (), s32[]{:S(2)}) async-start(), calls=%async_computation.10 | async-start | bytes 3538944 | tf_op jit(solution)/shard_map/all_gather | solution.py:245
  222.8 1.0 copy-start.10
  223.8 49.6 %copy-start.15 = (bf16[4,512,1024]{2,1,0:T(8,128)(2,1)S(1)}, bf16[4,512,1024]{2,1,0:T(8,128)(2,1)}, u32[]{:S(2)}) copy-start(bf16[4,512,1024]{2,1,0:T(8,128)(2,1)} %get-tuple-element.16) | copy-start | bytes 12582916
  276.6 4.3 %copy-start.8 = (bf16[256,1024]{1,0:T(8,128)(2,1)S(1)}, bf16[256,1024]{1,0:T(8,128)(2,1)}, u32[]{:S(2)}) copy-start(bf16[256,1024]{1,0:T(8,128)(2,1)} %copy-done.7) | copy-start | bytes 1572868
  276.6 14.5 %all-to-all-start.5 = ((bf16[4,256,384]{2,1,0:T(8,128)(2,1)}), bf16[4,256,384]{2,1,0:T(8,128)(2,1)S(1)}, u32[]{:S(2)}, u32[]{:S(2)}) async-start(bf16[4,256,384]{2,1,0:T(8,128)(2,1)} %bitcast.41), calls=%async_computation.7 | async-start | bytes 1572864 | tf_op jit(solution)/shard_map/all_to_all | solution.py:37
Sparse Core Ops, SparseCore 0:
  123.2 44.9 reduce-scatter.4
  223.9 29.9 all-gather.1
Sparse Core Ops, SparseCore 1:
  190.6 25.0 reduce-scatter.2

commit v3 on v2

--- a/solution.py
+++ b/solution.py
@@ -1,3 +1,5 @@
+import functools
+
 import jax
 import jax.numpy as jnp
 import numpy as np
@@ -8,7 +10,6 @@
 
 DOM = ("z", "x", "c")
 NEAR = ("c", "rep")
-FAR = ("z", "x")
 bf16 = jnp.bfloat16
 f32 = jnp.float32
 
@@ -16,7 +17,6 @@
 STEP = 4
 SPLIT = 4
 EXTRA = 128
-FIRST = 384
 VMEM = pltpu.CompilerParams(vmem_limit_bytes=48 * 1024 * 1024)
 MARGIN = 16
 
@@ -114,8 +114,7 @@
     hidden_ref,
     delta_ref,
     aggregate_ref,
-    first_ref,
-    second_ref,
+    routed_ref,
     pre_ref,
     neigh_ref,
     degree_ref,
@@ -164,11 +163,10 @@
         neigh_ref[here, :] = (delta.astype(f32) / degree_ref[here, 0:1]).astype(bf16)
 
     grad = contract_last(neigh_ref[...], w_neigh_ref[...]).astype(bf16)
-    rest = width - FIRST
     for j in range(SPLIT):
-        routed = contract_first(routing(j), grad).astype(bf16)
-        first_ref[:, j * FIRST : (j + 1) * FIRST] = routed[:, :FIRST]
-        second_ref[:, j * rest : (j + 1) * rest] = routed[:, FIRST:]
+        routed_ref[:, j * width : (j + 1) * width] = contract_first(
+            routing(j), grad
+        ).astype(bf16)
 
 
 def middle(arrived, seeds, base, w_neigh, cotangent):
@@ -181,8 +179,7 @@
             jax.ShapeDtypeStruct((seed_count, hidden), bf16),
             jax.ShapeDtypeStruct((seed_count, hidden), bf16),
             jax.ShapeDtypeStruct((seed_count, width), bf16),
-            jax.ShapeDtypeStruct((sent, SPLIT * FIRST), bf16),
-            jax.ShapeDtypeStruct((sent, SPLIT * (width - FIRST)), bf16),
+            jax.ShapeDtypeStruct((sent, SPLIT * width), bf16),
         ],
         scratch_shapes=[
             pltpu.VMEM((seed_count, hidden), f32),
@@ -213,39 +210,6 @@
         out_ref[b, block:, :] = margin
 
 
-def reduce_everywhere(self_rows, aggregate, delta):
-    near = lax.axis_size(NEAR)
-    far = lax.axis_size(FAR)
-    seeds, width = self_rows.shape
-    hidden = delta.shape[1]
-    block = 2 * width // near
-    piece = block // far
-    terms = pl.pallas_call(
-        terms_kernel,
-        out_shape=jax.ShapeDtypeStruct((near, block + MARGIN, hidden), bf16),
-        compiler_params=VMEM,
-        cost_estimate=cost(4 * seeds * width * hidden, 8 * width * hidden),
-    )(self_rows, aggregate, delta)
-    summed = lax.psum_scatter(
-        terms.reshape(-1, hidden), NEAR, scatter_dimension=0, tiled=True
-    )
-    pieces = jnp.concatenate(
-        [
-            summed[:block].reshape(far, piece, hidden),
-            jnp.broadcast_to(summed[None, block : block + 2], (far, 2, hidden)),
-        ],
-        axis=1,
-    )
-    total = jnp.sum(exchange(pieces, FAR).astype(f32), axis=0)
-    bias_total = total[piece]
-    spread = exchange(
-        jnp.broadcast_to(total.astype(bf16)[None], (far,) + total.shape), FAR
-    )
-    own = spread[:, :piece].reshape(block, hidden)
-    full = lax.all_gather(own, NEAR, axis=0, tiled=True)
-    return full, bias_total, spread
-
-
 def after(value, earlier):
     def kernel(value_ref, earlier_ref, out_ref):
         pass
@@ -257,6 +221,81 @@
         out_shape=jax.ShapeDtypeStruct(value.shape, value.dtype),
         input_output_aliases={0: 0},
     )(value, earlier)
+
+
+def reduce_everywhere(self_rows, aggregate, delta, earlier):
+    near = lax.axis_size(NEAR)
+    seeds, width = self_rows.shape
+    hidden = delta.shape[1]
+    block = 2 * width // near
+    terms = pl.pallas_call(
+        terms_kernel,
+        out_shape=jax.ShapeDtypeStruct((near, block + MARGIN, hidden), bf16),
+        compiler_params=VMEM,
+        cost_estimate=cost(4 * seeds * width * hidden, 8 * width * hidden),
+    )(self_rows, aggregate, delta)
+    summed = lax.psum_scatter(
+        terms.reshape(-1, hidden), NEAR, scatter_dimension=0, tiled=True
+    )
+    part = block // lax.axis_size("x")
+    parts = jnp.concatenate(
+        [
+            summed[:block].reshape(-1, part, hidden),
+            jnp.broadcast_to(summed[None, block : block + 8], (block // part, 8, hidden)),
+        ],
+        axis=1,
+    )
+    line = lax.psum_scatter(
+        parts.reshape(-1, hidden), "x", scatter_dimension=0, tiled=True
+    )
+    lines = lax.all_gather(after(line, earlier), "z", axis=0)
+    total = jnp.sum(lines.astype(f32), axis=0)
+    own = lax.all_gather(total[:part].astype(bf16), "x", axis=0, tiled=True)
+    full = lax.all_gather(own, NEAR, axis=0, tiled=True)
+    return full, total[part]
+
+
+def scaled_kernel(scale, upper_ref, lower_ref, self_ref, neigh_ref):
+    self_ref[...] = upper_ref[...].astype(f32) * scale
+    neigh_ref[...] = lower_ref[...].astype(f32) * scale
+
+
+def scaled_halves(full, scale):
+    rows, hidden = full.shape
+    half = rows // 2
+    steps = 6
+    tall = half // steps
+    spec = pl.BlockSpec((tall, hidden), lambda i: (i, 0))
+    return pl.pallas_call(
+        functools.partial(scaled_kernel, scale),
+        grid=(steps,),
+        in_specs=[spec, pl.BlockSpec((tall, hidden), lambda i: (i + steps, 0))],
+        out_specs=[spec, spec],
+        out_shape=[jax.ShapeDtypeStruct((half, hidden), f32)] * 2,
+        compiler_params=VMEM,
+        cost_estimate=cost(rows * hidden, 6 * rows * hidden),
+    )(full, full)
+
+
+def scatter_kernel(select_ref, grad_ref, out_ref):
+    width = out_ref.shape[1]
+    total = contract_first(select_ref[0], grad_ref[:, :width])
+    for j in range(1, SPLIT):
+        total += contract_first(select_ref[j], grad_ref[:, j * width : (j + 1) * width])
+    out_ref[...] = total.astype(bf16)
+
+
+def scatter_sum(select, slot_grad):
+    _, sent, rows = select.shape
+    width = slot_grad.shape[1] // SPLIT
+    return pl.pallas_call(
+        scatter_kernel,
+        out_shape=jax.ShapeDtypeStruct((rows, width), bf16),
+        compiler_params=VMEM,
+        cost_estimate=cost(
+            2 * SPLIT * sent * rows * width, 2 * (select.size + slot_grad.size)
+        ),
+    )(select, slot_grad)
 
 
 def on_device(
@@ -276,35 +315,24 @@
     seeds = seeds.reshape(SPLIT, 1, sources * s_count)
     self_rows = jnp.take(feats, seed_rows, axis=0)
     base = jnp.dot(self_rows, w_self, preferred_element_type=f32) + bias[None, :]
-    hidden_out, delta, aggregate, first, second = middle(
+    hidden_out, delta, aggregate, routed = middle(
         arrived.reshape(sources * s_count, -1), seeds, base, w_neigh, cotangent
     )
 
-    def back(routed):
-        columns = routed.shape[1] // SPLIT
-        slot_grad = exchange(routed.reshape(sources, s_count, -1), DOM)
-        slot_grad = slot_grad.reshape(sources * s_count, -1)
-        local = sum(
-            contract_first(select[j], slot_grad[:, j * columns : (j + 1) * columns])
-            for j in range(SPLIT)
-        )
-        return local.astype(bf16)
-
-    grads, bias_total, done = reduce_everywhere(self_rows, aggregate, delta)
-    share1 = lax.psum_scatter(back(first), "rep", scatter_dimension=0, tiled=True)
-    local2 = back(after(second, done))
-    shares2 = exchange(local2.reshape(replicas, row_count // replicas, -1), "rep")
-    share2 = jnp.sum(shares2.astype(f32), axis=0).astype(bf16)
-    feat_grads = jnp.concatenate([share1, share2], axis=1)
+    slot_grad = exchange(routed.reshape(sources, s_count, -1), DOM)
+    full, bias_total = reduce_everywhere(self_rows, aggregate, delta, slot_grad)
     self_grad = contract_last(delta, w_self).astype(bf16)
+    local = scatter_sum(select, slot_grad.reshape(sources * s_count, -1))
+    shares = exchange(local.reshape(replicas, row_count // replicas, width), "rep")
+    feat_grads = jnp.sum(shares.astype(f32), axis=0).astype(bf16)
     scale = float(seed_count * lax.axis_size(DOM) * replicas) ** (-0.5)
-    grads = grads.astype(f32) * scale
+    grad_self, grad_neigh = scaled_halves(full, scale)
     return (
         hidden_out,
         self_grad,
         feat_grads,
-        grads[:width],
-        grads[width:],
+        grad_self,
+        grad_neigh,
         bias_total * scale,
     )
 

time: 309 us -> 295 us (0.955)
  waiting for transfers between devices: 89.6 us -> 170 us
  blocking collectives: 113 us -> 32.9 us
  matrix products: 19.9 us -> 1.94 us
  Pallas kernels: 15.9 us -> 28.2 us
  other arithmetic: 9.72 us -> 4.99 us
  local copies, waits for them, and re-layouts: 18.9 us -> 14.4 us
    all_to_all x3 -> x0, blocking collectives: 113 us -> none  [exchange(): return lax.all_to_all(value, axes, split_axis=0, concat_axis=0, tiled=True)]
    reduce_scatter x1, waiting for transfers between devices: 0.01 us -> 38.3 us  [reduce_everywhere(): lax.psum_scatter(terms.reshape(-1, hidden), NEAR, scatter_dimension=0, ti...]
    all_to_all x3, waiting for transfers between devices: 89.5 us -> 123 us  [exchange(): return lax.all_to_all(value, axes, split_axis=0, concat_axis=0, tiled=True)]
    all_gather x0 -> x2, blocking collectives: none -> 32.9 us  [the longest x1 22.2 us: reduce_everywhere(): lines = lax.all_gather(after(line, earlier), 'z', axis=0)]
    dot_general x8 -> x0, matrix products: 17 us -> none  [contract_first(): lax.dot_general(left, right, (((0,), (0,)), ((), ())), preferred_element_...]
    pallas_call x0 -> x2, Pallas kernels: none -> 11.2 us  [the longest x1 7.83 us: scatter_sum(): pl.pallas_call(scatter_kernel, out_shape=jax.ShapeDtypeStruct((rows, widt...]
    all_gather x1, waiting for transfers between devices: 0.01 us -> 8.79 us  [reduce_everywhere(): full = lax.all_gather(own, NEAR, axis=0, tiled=True)]
    unnamed x38 -> x22, local copies, waits for them, and re-layouts: 8.44 us -> 9.29 us
  transfers between devices with their start and end apart: 6 -> 6, of which waited for: 3 -> 5; matrix products, arithmetic and copies ran while one was open for 9% -> 3% of each run, Pallas kernels for 0% -> 3%
where the time goes in v3:
time: 295 us; the launch traced here: 291 us
  waiting for transfers between devices  170 us (58%)
  blocking collectives  32.9 us (11%)
  Pallas kernels  28.2 us (10%)
  starting transfers between devices  24.6 us (8%)
  local copies, waits for them, and re-layouts  14.4 us (5%)
  between operations  14 us (5%)
  other arithmetic  4.99 us (2%)
    all_to_all x3, waiting for transfers between devices, exchange(): return lax.all_to_all(value, axes, split_axis=0, concat_axis=0, tiled=True)  123 us
    reduce_scatter x1, waiting for transfers between devices, reduce_everywhere(): lax.psum_scatter(terms.reshape(-1, hidden), NEAR, scatter_dimension=0, ti...  38.3 us
    all_to_all x3, starting transfers between devices, exchange(): return lax.all_to_all(value, axes, split_axis=0, concat_axis=0, tiled=True)  24.5 us
    all_gather x1, blocking collectives, reduce_everywhere(): lines = lax.all_gather(after(line, earlier), 'z', axis=0)  22.2 us
    all_gather x1, blocking collectives, reduce_everywhere(): own = lax.all_gather(total[:part].astype(bf16), 'x', axis=0, tiled=True)  10.7 us
    unnamed x22, local copies, waits for them, and re-layouts  9.29 us
    all_gather x1, waiting for transfers between devices, reduce_everywhere(): full = lax.all_gather(own, NEAR, axis=0, tiled=True)  8.79 us
    pallas_call x1, Pallas kernels, middle(): pl.pallas_call(middle_kernel, out_shape=[jax.ShapeDtypeStruct((seed_count...  8.22 us
  transfers between devices with their start and end apart: 6, of which 5 were waited for; matrix products, arithmetic and copies ran while one was open for 3% of the time, Pallas kernels for 3%

profile of v3, /device:TPU:1, one launch (start us, length us, event | category | flops | bytes accessed | tf_op | source)
XLA Modules:
  0.0 291.0 jit_solution(87432425818210352)
XLA Ops:
  7.2 0.0 copy-start
  7.2 1.0 reshape_squeeze.6.rows_ref
  8.2 0.8 squeeze.4
  9.0 0.1 add.80
  9.1 0.1 add.81
  9.2 0.1 compare_select_fusion.keys_ref
  9.3 0.0 copy-start.3
  9.3 1.4 copy-done.3
  10.7 7.8 %shard_map.136 = (bf16[4,512,1024]{2,1,0:T(8,128)(2,1)}, bf16[512,3200]{1,0:T(8,128)(2,1)S(1)}) custom-call(s32[16,1,256]{2,1,0:T(1,128)S(1)} %reshape_squeeze.6.rows_ref, s32[16,1,256]{2,1,0:T(1,128)S(1)} %compare_select_fusion.keys_ref, bf16[1024,768]{1,0:T(8,128)(2,1)S(1)} %copy-done.3), custom_call_target="tpu_custom_call" | custom-call | flops 4294967296 | bytes 9043968 | tf_op jit(solution)/shard_map/pallas_call | solution.py:80
  18.6 0.0 copy-start.5
  18.6 1.8 copy-done.5
  20.4 0.0 copy-start.8
  20.4 0.0 copy-start.10
  20.4 0.0 copy-start.4
  20.4 13.3 %all-to-all-start = ((bf16[64,8,3200]{2,1,0:T(8,128)(2,1)}), bf16[64,8,3200]{2,1,0:T(8,128)(2,1)}, u32[]{:S(2)}, u32[]{:S(2)}) async-start(bf16[64,8,3200]{2,1,0:T(8,128)(2,1)} %bitcast.18), calls=%async_computation | async-start | bytes 6553600 | tf_op jit(solution)/shard_map/all_to_all | solution.py:37
  33.7 0.0 reduce-scatter.3.cloned.1.call-start
  33.7 0.0 copy-done.8
  33.7 0.1 copy.17
  33.8 0.1 reshape.209.seeds_ref
  33.9 0.0 copy-done.10
  34.0 0.0 copy-done.4
  34.0 0.0 copy-start.9
  34.0 1.2 gather_fusion
  35.2 0.7 compare_and_fusion
  35.9 0.1 broadcast_select_fusion.self_ref
  36.0 0.0 copy-done
  36.0 0.0 copy-done.9
  36.0 0.6 convolution_add_fusion.base_ref
  36.6 72.3 %all-to-all-done = bf16[64,8,3200]{2,1,0:T(8,128)(2,1)} async-done(((bf16[64,8,3200]{2,1,0:T(8,128)(2,1)}), bf16[64,8,3200]{2,1,0:T(8,128)(2,1)}, u32[]{:S(2)}, u32[]{:S(2)}) %all-to-all-start) | async-done | bytes 3276832 | tf_op jit(solution)/shard_map/all_to_all | solution.py:37
  108.9 0.0 copy-start.6
  108.9 1.4 copy-done.6
  110.3 0.0 copy-start.7
  110.3 1.0 copy-done.7
  111.4 8.2 %shard_map.137 = (bf16[256,1024]{1,0:T(8,128)(2,1)}, bf16[256,1024]{1,0:T(8,128)(2,1)S(1)}, bf16[256,768]{1,0:T(8,128)(2,1)S(1)}, bf16[512,3072]{1,0:T(8,128)(2,1)}) custom-call(bf16[512,3200]{1,0:T(8,128)(2,1)} %bitcast.1.arrived_ref, s32[4,1,512]{2,1,0:T(1,128)S(1)} %reshape.209.seeds_ref, f32[256,1024]{1,0:T(8,128)S(1)} %convolution_add_fusion.base_ref, ...), custom_call_target="tpu_custom_call" | custom-call | flops 2415919104 | bytes 10747904 | tf_op jit(solution)/shard_map/pallas_call | solution.py:176
  119.6 1.0 shard_map.139
  120.6 0.0 copy-start.1
  120.6 1.7 copy-done.1
  122.4 0.0 reduce-scatter.3.cloned.1.call-update
  122.4 6.8 %all-to-all-start.1 = ((bf16[64,8,3072]{2,1,0:T(8,128)(2,1)}), bf16[64,8,3072]{2,1,0:T(8,128)(2,1)}, u32[]{:S(2)}, u32[]{:S(2)}) async-start(bf16[64,8,3072]{2,1,0:T(8,128)(2,1)} %bitcast.20), calls=%async_computation.1 | async-start | bytes 6291456 | tf_op jit(solution)/shard_map/all_to_all | solution.py:37
  129.2 0.0 reduce-scatter.5.cloned.1.call-start
  129.3 38.3 %reduce-scatter.3.cloned.1.call-done = bf16[208,1024]{1,0:T(8,128)(2,1)} async-done(((bf16[1664,1024]{1,0:T(8,128)(2,1)}), bf16[208,1024]{1,0:T(8,128)(2,1)}) %reduce-scatter.3.cloned.1.call-update) | async-done | bytes 426000 | tf_op jit(solution)/shard_map/reduce_scatter | solution.py:237
  167.6 0.7 slice.20
  168.3 1.0 slice.19
  169.3 0.8 pad_maximum_fusion
  170.1 0.0 reduce-scatter.5.cloned.1.call-update
  170.2 0.0 all-gather.3.cloned.1.call-start
  170.2 31.7 %all-to-all-done.1.earlier_ref = bf16[64,8,3072]{2,1,0:T(8,128)(2,1)} async-done(((bf16[64,8,3072]{2,1,0:T(8,128)(2,1)}), bf16[64,8,3072]{2,1,0:T(8,128)(2,1)}, u32[]{:S(2)}, u32[]{:S(2)}) %all-to-all-start.1) | async-done | bytes 3145760 | tf_op jit(solution)/shard_map/all_to_all | solution.py:37
  201.9 0.0 reduce-scatter.5.cloned.1.call-done.value_ref
  201.9 22.2 %all-gather = bf16[448,1024]{1,0:T(8,128)(2,1)S(1)} all-gather(bf16[56,1024]{1,0:T(8,128)(2,1)} %shard_map.140), channel_id=2, replica_groups=mesh['z'=8,'x'=4,'c'=2,'rep'=4] {'z'}, dimensions={0}, use_global_device_ids=true | all-gather | bytes 1032192 | tf_op jit(solution)/shard_map/all_gather | solution.py:251
  224.1 0.1 convert_reduce_fusion
  224.3 10.7 %all_gather.14 = bf16[192,1024]{1,0:T(8,128)(2,1)} all-gather(bf16[48,1024]{1,0:T(8,128)(2,1)S(1)} %slice.25), channel_id=1, replica_groups=mesh['z'=8,'x'=4,'c'=2,'rep'=4] {'x'}, dimensions={0}, use_global_device_ids=true | all-gather | bytes 491520 | tf_op jit(solution)/shard_map/all_gather | solution.py:253
  235.0 0.0 all-gather.3.cloned.1.call-update
  235.1 7.8 %shard_map.138 = bf16[1024,768]{1,0:T(8,128)(2,1)} custom-call(bf16[4,512,1024]{2,1,0:T(8,128)(2,1)} %get-tuple-element.17.select_ref, bf16[512,3072]{1,0:T(8,128)(2,1)} %bitcast.5.grad_ref), custom_call_target="tpu_custom_call" | custom-call | flops 3221225472 | bytes 7340032 | tf_op jit(solution)/shard_map/pallas_call | solution.py:291
  242.9 4.4 %all-to-all-start.2 = ((bf16[4,256,768]{2,1,0:T(8,128)(2,1)}), bf16[4,256,768]{2,1,0:T(8,128)(2,1)}, u32[]{:S(2)}, u32[]{:S(2)}) async-start(bf16[4,256,768]{2,1,0:T(8,128)(2,1)} %bitcast.6), calls=%async_computation.2 | async-start | bytes 3145728 | tf_op jit(solution)/shard_map/all_to_all | solution.py:37
  247.3 1.4 convolution_convert_fusion
  248.6 18.8 %all-to-all-done.2 = bf16[4,256,768]{2,1,0:T(8,128)(2,1)} async-done(((bf16[4,256,768]{2,1,0:T(8,128)(2,1)}), bf16[4,256,768]{2,1,0:T(8,128)(2,1)}, u32[]{:S(2)}, u32[]{:S(2)}) %all-to-all-start.2) | async-done | bytes 1572896 | tf_op jit(solution)/shard_map/all_to_all | solution.py:37
  267.4 2.5 reduce_sum.21
  269.9 0.6 slice_multiply_fusion
  270.5 8.8 %all-gather.3.cloned.1.call-done.upper_ref.lower_ref = bf16[1536,1024]{1,0:T(8,128)(2,1)} async-done(((bf16[192,1024]{1,0:T(8,128)(2,1)}), bf16[1536,1024]{1,0:T(8,128)(2,1)}) %all-gather.3.cloned.1.call-update) | async-done | bytes 3145744 | tf_op jit(solution)/shard_map/all_gather | solution.py:254
  279.3 0.0 copy-start.2
  279.3 1.9 copy-done.2
  281.2 3.3 %shard_map.141 = (f32[768,1024]{1,0:T(8,128)}, f32[768,1024]{1,0:T(8,128)}) custom-call(bf16[1536,1024]{1,0:T(8,128)(2,1)S(1)} %copy-done.2, bf16[1536,1024]{1,0:T(8,128)(2,1)S(1)} %copy-done.2), custom_call_target="tpu_custom_call" | custom-call | flops 1572864 | bytes 9437184 | tf_op jit(solution)/shard_map/pallas_call | solution.py:269
  (6 shorter events, 0.0 us)
Async XLA Ops:
  7.2 28.8 %copy-start = (bf16[768,1024]{1,0:T(8,128)(2,1)S(1)}, bf16[768,1024]{1,0:T(8,128)(2,1)}, u32[]{:S(2)}) copy-start(bf16[768,1024]{1,0:T(8,128)(2,1)} %param.14) | copy-start | bytes 4718596
  9.3 1.4 copy-start.3
  18.6 1.8 copy-start.5
  20.4 13.3 %copy-start.8 = (s32[1,64,32]{1,2,0:T(8,128)S(1)}, s32[1,64,32]{1,2,0:T(8,128)}, u32[]{:S(2)}) copy-start(s32[1,64,32]{1,2,0:T(8,128)} %param.13) | copy-start | bytes 24580
  20.4 13.6 %copy-start.10 = (s32[256]{0:T(256)S(1)}, s32[256]{0:T(256)}, u32[]{:S(2)}) copy-start(s32[256]{0:T(256)} %param.10) | copy-start | bytes 3076
  20.4 13.6 %copy-start.4 = (bf16[1024,768]{1,0:T(8,128)(2,1)S(1)}, bf16[1024,768]{1,0:T(8,128)(2,1)}, u32[]{:S(2)}) copy-start(bf16[1024,768]{1,0:T(8,128)(2,1)} %feats_ref.1) | copy-start | bytes 4718596
  20.4 88.6 %all-to-all-start = ((bf16[64,8,3200]{2,1,0:T(8,128)(2,1)}), bf16[64,8,3200]{2,1,0:T(8,128)(2,1)}, u32[]{:S(2)}, u32[]{:S(2)}) async-start(bf16[64,8,3200]{2,1,0:T(8,128)(2,1)} %bitcast.18), calls=%async_computation | async-start | bytes 6553600 | tf_op jit(solution)/shard_map/all_to_all | solution.py:37
  33.7 133.9 %reduce-scatter.3.cloned.1.call-start = ((), (), s32[]{:S(2)}) async-start(), calls=%async_computation.5 | async-start | bytes 3833856 | tf_op jit(solution)/shard_map/reduce_scatter | solution.py:237
  34.0 2.0 copy-start.9
  108.9 1.4 copy-start.6
  110.3 1.0 copy-start.7
  120.6 1.8 copy-start.1
  122.4 79.5 %all-to-all-start.1 = ((bf16[64,8,3072]{2,1,0:T(8,128)(2,1)}), bf16[64,8,3072]{2,1,0:T(8,128)(2,1)}, u32[]{:S(2)}, u32[]{:S(2)}) async-start(bf16[64,8,3072]{2,1,0:T(8,128)(2,1)} %bitcast.20), calls=%async_computation.1 | async-start | bytes 6291456 | tf_op jit(solution)/shard_map/all_to_all | solution.py:37
  129.2 72.7 %reduce-scatter.5.cloned.1.call-start = ((), (), s32[]{:S(2)}) async-start(), calls=%async_computation.6 | async-start | bytes 573440 | tf_op jit(solution)/shard_map/reduce_scatter | solution.py:248
  170.2 109.1 %all-gather.3.cloned.1.call-start = ((), (), s32[]{:S(2)}) async-start(), calls=%async_computation.7 | async-start | bytes 3538944 | tf_op jit(solution)/shard_map/all_gather | solution.py:254
  242.9 24.5 %all-to-all-start.2 = ((bf16[4,256,768]{2,1,0:T(8,128)(2,1)}), bf16[4,256,768]{2,1,0:T(8,128)(2,1)}, u32[]{:S(2)}, u32[]{:S(2)}) async-start(bf16[4,256,768]{2,1,0:T(8,128)(2,1)} %bitcast.6), calls=%async_computation.2 | async-start | bytes 3145728 | tf_op jit(solution)/shard_map/all_to_all | solution.py:37
  279.3 1.9 copy-start.2
Sparse Core Ops, SparseCore 0:
  122.5 45.0 reduce-scatter.2
  170.7 25.7 reduce-scatter.4
  235.2 44.0 all-gather.2

commit v4 on v3

--- a/solution.py
+++ b/solution.py
@@ -17,7 +17,7 @@
 STEP = 4
 SPLIT = 4
 EXTRA = 128
-VMEM = pltpu.CompilerParams(vmem_limit_bytes=48 * 1024 * 1024)
+VMEM = pltpu.CompilerParams(vmem_limit_bytes=60 * 1024 * 1024)
 MARGIN = 16
 
 
@@ -35,6 +35,10 @@
 
 def exchange(value, axes):
     return lax.all_to_all(value, axes, split_axis=0, concat_axis=0, tiled=True)
+
+
+def spread(value, axes):
+    return jnp.broadcast_to(value[None], (lax.axis_size(axes),) + value.shape)
 
 
 def cost(flops, bytes_accessed):
@@ -237,43 +241,62 @@
     summed = lax.psum_scatter(
         terms.reshape(-1, hidden), NEAR, scatter_dimension=0, tiled=True
     )
-    part = block // lax.axis_size("x")
+    height = lax.axis_size("z")
+    part = block // height
     parts = jnp.concatenate(
         [
-            summed[:block].reshape(-1, part, hidden),
-            jnp.broadcast_to(summed[None, block : block + 8], (block // part, 8, hidden)),
+            summed[:block].reshape(height, part, hidden),
+            jnp.broadcast_to(summed[None, block : block + 8], (height, 8, hidden)),
         ],
         axis=1,
     )
     line = lax.psum_scatter(
-        parts.reshape(-1, hidden), "x", scatter_dimension=0, tiled=True
-    )
-    lines = lax.all_gather(after(line, earlier), "z", axis=0)
+        parts.reshape(-1, hidden), "z", scatter_dimension=0, tiled=True
+    )
+    lines = exchange(spread(after(line, earlier), "x"), "x")
     total = jnp.sum(lines.astype(f32), axis=0)
-    own = lax.all_gather(total[:part].astype(bf16), "x", axis=0, tiled=True)
-    full = lax.all_gather(own, NEAR, axis=0, tiled=True)
-    return full, total[part]
-
-
-def scaled_kernel(scale, upper_ref, lower_ref, self_ref, neigh_ref):
-    self_ref[...] = upper_ref[...].astype(f32) * scale
-    neigh_ref[...] = lower_ref[...].astype(f32) * scale
-
-
-def scaled_halves(full, scale):
-    rows, hidden = full.shape
-    half = rows // 2
-    steps = 6
-    tall = half // steps
-    spec = pl.BlockSpec((tall, hidden), lambda i: (i, 0))
+    own = exchange(spread(total.astype(bf16), "z"), "z")
+    margin = jnp.concatenate([own[0, part:]] * (MARGIN // 8), axis=0)
+    own = jnp.concatenate([own[:, :part].reshape(block, hidden), margin], axis=0)
+    return lax.all_gather(own, NEAR, axis=0, tiled=True)
+
+
+def scaled_kernel(scale, upper_ref, lower_ref, self_ref, neigh_ref, bias_ref):
+    block = self_ref.shape[0]
+    self_ref[...] = upper_ref[:block, :].astype(f32) * scale
+    neigh_ref[...] = lower_ref[:block, :].astype(f32) * scale
+
+    @pl.when(pl.program_id(0) == 0)
+    def _():
+        bias_ref[...] = upper_ref[block:, :].astype(f32) * scale
+
+
+def scaled_parts(full, width, scale):
+    hidden = full.shape[1]
+    near = lax.axis_size(NEAR)
+    tall = full.shape[0] // near
+    half = near // 2
+    block = width // half
+    grad_spec = pl.BlockSpec((block, hidden), lambda i: (i, 0))
     return pl.pallas_call(
         functools.partial(scaled_kernel, scale),
-        grid=(steps,),
-        in_specs=[spec, pl.BlockSpec((tall, hidden), lambda i: (i + steps, 0))],
-        out_specs=[spec, spec],
-        out_shape=[jax.ShapeDtypeStruct((half, hidden), f32)] * 2,
-        compiler_params=VMEM,
-        cost_estimate=cost(rows * hidden, 6 * rows * hidden),
+        grid=(half,),
+        in_specs=[
+            pl.BlockSpec((tall, hidden), lambda i: (i, 0)),
+            pl.BlockSpec((tall, hidden), lambda i: (i + half, 0)),
+        ],
+        out_specs=[
+            grad_spec,
+            grad_spec,
+            pl.BlockSpec((MARGIN, hidden), lambda i: (0, 0)),
+        ],
+        out_shape=[
+            jax.ShapeDtypeStruct((width, hidden), f32),
+            jax.ShapeDtypeStruct((width, hidden), f32),
+            jax.ShapeDtypeStruct((MARGIN, hidden), f32),
+        ],
+        compiler_params=VMEM,
+        cost_estimate=cost(full.size, 6 * full.size),
     )(full, full)
 
 
@@ -320,20 +343,20 @@
     )
 
     slot_grad = exchange(routed.reshape(sources, s_count, -1), DOM)
-    full, bias_total = reduce_everywhere(self_rows, aggregate, delta, slot_grad)
+    full = reduce_everywhere(self_rows, aggregate, delta, slot_grad)
     self_grad = contract_last(delta, w_self).astype(bf16)
     local = scatter_sum(select, slot_grad.reshape(sources * s_count, -1))
     shares = exchange(local.reshape(replicas, row_count // replicas, width), "rep")
     feat_grads = jnp.sum(shares.astype(f32), axis=0).astype(bf16)
     scale = float(seed_count * lax.axis_size(DOM) * replicas) ** (-0.5)
-    grad_self, grad_neigh = scaled_halves(full, scale)
+    grad_self, grad_neigh, grad_bias = scaled_parts(full, width, scale)
     return (
         hidden_out,
         self_grad,
         feat_grads,
         grad_self,
         grad_neigh,
-        bias_total * scale,
+        grad_bias[0],
     )
 
 

time: 295 us -> 297 us (level)
  Pallas kernels: 28.2 us -> 35.8 us
  waiting for transfers between devices: 170 us -> 177 us
  local copies, waits for them, and re-layouts: 14.4 us -> 8.65 us
  blocking collectives: 32.9 us -> 27.3 us
    all_gather x2 -> x0, blocking collectives: 32.9 us -> none  [the longest x1 22.2 us: reduce_everywhere(): lines = lax.all_gather(after(line, earlier), 'z', axis=0)]
    all_to_all x0 -> x2, blocking collectives: none -> 27.3 us  [exchange(): return lax.all_to_all(value, axes, split_axis=0, concat_axis=0, tiled=True)]
    all_to_all x3, waiting for transfers between devices: 123 us -> 135 us  [exchange(): return lax.all_to_all(value, axes, split_axis=0, concat_axis=0, tiled=True)]
    unnamed x22 -> x12, local copies, waits for them, and re-layouts: 9.29 us -> 0.04 us
    all_gather x1, waiting for transfers between devices: 8.79 us -> 0.01 us  [reduce_everywhere(): return lax.all_gather(own, NEAR, axis=0, tiled=True)]
    reduce_scatter x1, waiting for transfers between devices: 0.01 us -> 3.49 us  [reduce_everywhere(): lax.psum_scatter(parts.reshape(-1, hidden), 'z', scatter_dimension=0, til...]
    pallas_call x1, Pallas kernels: 1.01 us -> 4.06 us  [reduce_everywhere(): pl.pallas_call(terms_kernel, out_shape=jax.ShapeDtypeStruct((near, block...]
where the time goes in v4:
time: 297 us; the launch traced here: 295 us
  waiting for transfers between devices  177 us (60%)
  Pallas kernels  35.8 us (12%)
  blocking collectives  27.3 us (9%)
  starting transfers between devices  24 us (8%)
  between operations  13.9 us (5%)
  local copies, waits for them, and re-layouts  8.65 us (3%)
  matrix products  3.98 us (1%)
  other arithmetic  3.61 us (1%)
    all_to_all x3, waiting for transfers between devices, exchange(): return lax.all_to_all(value, axes, split_axis=0, concat_axis=0, tiled=True)  135 us
    reduce_scatter x1, waiting for transfers between devices, reduce_everywhere(): lax.psum_scatter(terms.reshape(-1, hidden), NEAR, scatter_dimension=0, ti...  38.3 us
    all_to_all x2, blocking collectives, exchange(): return lax.all_to_all(value, axes, split_axis=0, concat_axis=0, tiled=True)  27.3 us
    all_to_all x3, starting transfers between devices, exchange(): return lax.all_to_all(value, axes, split_axis=0, concat_axis=0, tiled=True)  23.9 us
    pallas_call x1, Pallas kernels, select_and_sum(): pl.pallas_call(select_kernel, grid=(groups // STEP,), in_specs=[pl.BlockS...  9.67 us
    pallas_call x1, Pallas kernels, middle(): pl.pallas_call(middle_kernel, out_shape=[jax.ShapeDtypeStruct((seed_count...  9.13 us
    pallas_call x1, Pallas kernels, scatter_sum(): pl.pallas_call(scatter_kernel, out_shape=jax.ShapeDtypeStruct((rows, widt...  7.83 us
  transfers between devices with their start and end apart: 6, of which 5 were waited for; matrix products, arithmetic and copies ran while one was open for 3% of the time, Pallas kernels for 3%

profile of v4, /device:TPU:1, one launch (start us, length us, event | category | flops | bytes accessed | tf_op | source)
XLA Modules:
  0.0 294.6 jit_solution(5740705888858240502)
XLA Ops:
  7.2 0.0 copy-start
  7.2 1.6 reshape_squeeze.6.rows_ref
  8.8 0.8 squeeze.9
  9.6 0.1 add.80
  9.7 0.1 add.81
  9.8 0.7 compare_select_fusion.keys_ref
  10.5 9.7 %shard_map.136 = (bf16[4,512,1024]{2,1,0:T(8,128)(2,1)}, bf16[512,3200]{1,0:T(8,128)(2,1)}) custom-call(s32[16,1,256]{2,1,0:T(1,128)} %reshape_squeeze.6.rows_ref, s32[16,1,256]{2,1,0:T(1,128)} %compare_select_fusion.keys_ref, bf16[1024,768]{1,0:T(8,128)(2,1)} %feats_ref.1), custom_call_target="tpu_custom_call" | custom-call | flops 4294967296 | bytes 9043968 | tf_op jit(solution)/shard_map/pallas_call | solution.py:84
  20.2 0.0 copy-start.3
  20.2 0.0 copy-start.5
  20.2 0.0 copy-start.1
  20.2 13.3 %all-to-all-start = ((bf16[64,8,3200]{2,1,0:T(8,128)(2,1)}), bf16[64,8,3200]{2,1,0:T(8,128)(2,1)}, u32[]{:S(2)}, u32[]{:S(2)}) async-start(bf16[64,8,3200]{2,1,0:T(8,128)(2,1)} %bitcast.19), calls=%async_computation | async-start | bytes 6553600 | tf_op jit(solution)/shard_map/all_to_all | solution.py:37
  33.5 0.0 reduce-scatter.3.cloned.1.call-start
  33.6 0.0 copy-done.3
  33.6 0.1 copy.19
  33.7 0.7 reshape.211.seeds_ref
  34.4 0.0 copy-done.5
  34.4 0.0 copy-done.1
  34.4 0.0 copy-start.4
  34.4 1.2 gather_fusion
  35.6 0.1 broadcast_select_fusion.self_ref
  35.7 0.0 copy-done
  35.8 0.0 copy-done.4
  35.8 0.0 copy-start.2
  35.8 1.5 convolution_add_fusion.base_ref
  37.3 71.5 %all-to-all-done = bf16[64,8,3200]{2,1,0:T(8,128)(2,1)} async-done(((bf16[64,8,3200]{2,1,0:T(8,128)(2,1)}), bf16[64,8,3200]{2,1,0:T(8,128)(2,1)}, u32[]{:S(2)}, u32[]{:S(2)}) %all-to-all-start) | async-done | bytes 3276832 | tf_op jit(solution)/shard_map/all_to_all | solution.py:37
  108.8 9.1 %shard_map.137 = (bf16[256,1024]{1,0:T(8,128)(2,1)}, bf16[256,1024]{1,0:T(8,128)(2,1)}, bf16[256,768]{1,0:T(8,128)(2,1)}, bf16[512,3072]{1,0:T(8,128)(2,1)}) custom-call(bf16[512,3200]{1,0:T(8,128)(2,1)} %bitcast.1.arrived_ref, s32[4,1,512]{2,1,0:T(1,128)} %reshape.211.seeds_ref, f32[256,1024]{1,0:T(8,128)} %convolution_add_fusion.base_ref, ...), custom_call_target="tpu_custom_call" | custom-call | flops 2415919104 | bytes 10747904 | tf_op jit(solution)/shard_map/pallas_call | solution.py:180
  117.9 0.0 copy-done.2
  117.9 4.1 %shard_map.139 = bf16[8,208,1024]{2,1,0:T(8,128)(2,1)} custom-call(bf16[256,768]{1,0:T(8,128)(2,1)} %copy-done.2, bf16[256,768]{1,0:T(8,128)(2,1)} %get-tuple-element.20.aggregate_ref, bf16[256,1024]{1,0:T(8,128)(2,1)} %get-tuple-element.17.delta_ref), custom_call_target="tpu_custom_call" | custom-call | flops 805306368 | bytes 6291456 | tf_op jit(solution)/shard_map/pallas_call | solution.py:235
  122.0 0.0 reduce-scatter.3.cloned.1.call-update
  122.0 6.8 %all-to-all-start.1 = ((bf16[64,8,3072]{2,1,0:T(8,128)(2,1)}), bf16[64,8,3072]{2,1,0:T(8,128)(2,1)}, u32[]{:S(2)}, u32[]{:S(2)}) async-start(bf16[64,8,3072]{2,1,0:T(8,128)(2,1)} %bitcast.20), calls=%async_computation.1 | async-start | bytes 6291456 | tf_op jit(solution)/shard_map/all_to_all | solution.py:37
  128.8 0.0 reduce-scatter.5.cloned.1.call-start
  128.9 38.3 %reduce-scatter.3.cloned.1.call-done = bf16[208,1024]{1,0:T(8,128)(2,1)} async-done(((bf16[1664,1024]{1,0:T(8,128)(2,1)}), bf16[208,1024]{1,0:T(8,128)(2,1)}) %reduce-scatter.3.cloned.1.call-update) | async-done | bytes 426000 | tf_op jit(solution)/shard_map/reduce_scatter | solution.py:241
  167.2 0.7 slice.23
  167.9 1.0 slice.22
  169.0 0.8 pad_maximum_fusion
  169.8 0.0 reduce-scatter.5.cloned.1.call-update
  169.8 0.0 all-gather.2.cloned.1.call-start
  169.9 34.6 %all-to-all-done.1.earlier_ref = bf16[64,8,3072]{2,1,0:T(8,128)(2,1)} async-done(((bf16[64,8,3072]{2,1,0:T(8,128)(2,1)}), bf16[64,8,3072]{2,1,0:T(8,128)(2,1)}, u32[]{:S(2)}, u32[]{:S(2)}) %all-to-all-start.1) | async-done | bytes 3145760 | tf_op jit(solution)/shard_map/all_to_all | solution.py:37
  204.4 3.5 %reduce-scatter.5.cloned.1.call-done.value_ref = bf16[32,1024]{1,0:T(8,128)(2,1)} async-done(((bf16[256,1024]{1,0:T(8,128)(2,1)}), bf16[32,1024]{1,0:T(8,128)(2,1)}) %reduce-scatter.5.cloned.1.call-update) | async-done | bytes 65552 | tf_op jit(solution)/shard_map/reduce_scatter | solution.py:253
  207.9 0.9 broadcast_in_dim.38
  208.8 10.1 %all_to_all.25 = bf16[4,32,1024]{2,1,0:T(8,128)(2,1)S(1)} all-to-all(bf16[4,32,1024]{2,1,0:T(8,128)(2,1)S(1)} %broadcast_in_dim.38), channel_id=1, replica_groups=mesh['z'=8,'x'=4,'c'=2,'rep'=4] {'x'}, dimensions={0} | all-to-all | bytes 524288 | tf_op jit(solution)/shard_map/all_to_all | solution.py:37
  218.9 0.1 broadcast_in_dim.39
  219.0 17.3 %all_to_all.26 = bf16[8,32,1024]{2,1,0:T(8,128)(2,1)S(1)} all-to-all(bf16[8,32,1024]{2,1,0:T(8,128)(2,1)S(1)} %broadcast_in_dim.39), channel_id=1, replica_groups=mesh['z'=8,'x'=4,'c'=2,'rep'=4] {'z'}, dimensions={0} | all-to-all | bytes 1048576 | tf_op jit(solution)/shard_map/all_to_all | solution.py:37
  236.3 0.8 pad_maximum_fusion.1
  237.1 0.0 all-gather.2.cloned.1.call-update
  237.1 7.8 %shard_map.138 = bf16[1024,768]{1,0:T(8,128)(2,1)} custom-call(bf16[4,512,1024]{2,1,0:T(8,128)(2,1)} %get-tuple-element.18.select_ref, bf16[512,3072]{1,0:T(8,128)(2,1)} %bitcast.5.grad_ref), custom_call_target="tpu_custom_call" | custom-call | flops 3221225472 | bytes 7340032 | tf_op jit(solution)/shard_map/pallas_call | solution.py:314
  244.9 3.8 %all-to-all-start.2 = ((bf16[4,256,768]{2,1,0:T(8,128)(2,1)}), bf16[4,256,768]{2,1,0:T(8,128)(2,1)S(1)}, u32[]{:S(2)}, u32[]{:S(2)}) async-start(bf16[4,256,768]{2,1,0:T(8,128)(2,1)} %bitcast.22), calls=%async_computation.2 | async-start | bytes 3145728 | tf_op jit(solution)/shard_map/all_to_all | solution.py:37
  248.7 2.4 convolution_convert_fusion
  251.1 29.4 %all-to-all-done.2 = bf16[4,256,768]{2,1,0:T(8,128)(2,1)S(1)} async-done(((bf16[4,256,768]{2,1,0:T(8,128)(2,1)}), bf16[4,256,768]{2,1,0:T(8,128)(2,1)S(1)}, u32[]{:S(2)}, u32[]{:S(2)}) %all-to-all-start.2) | async-done | bytes 1572896 | tf_op jit(solution)/shard_map/all_to_all | solution.py:37
  280.6 1.1 reduce_sum.24
  281.6 0.0 all-gather.2.cloned.1.call-done.upper_ref.lower_ref
  281.6 5.1 %shard_map.141 = (f32[768,1024]{1,0:T(8,128)}, f32[768,1024]{1,0:T(8,128)}, f32[16,1024]{1,0:T(8,128)}) custom-call(bf16[1664,1024]{1,0:T(8,128)(2,1)} %all-gather.2.cloned.1.call-done.upper_ref.lower_ref, bf16[1664,1024]{1,0:T(8,128)(2,1)} %all-gather.2.cloned.1.call-done.upper_ref.lower_ref), custom_call_target="tpu_custom_call" | custom-call | flops 1703936 | bytes 10223616 | tf_op jit(solution)/shard_map/pallas_call | solution.py:281
  286.7 1.4 slice.19
  (9 shorter events, 0.1 us)
Async XLA Ops:
  7.2 28.6 %copy-start = (bf16[768,1024]{1,0:T(8,128)(2,1)S(1)}, bf16[768,1024]{1,0:T(8,128)(2,1)}, u32[]{:S(2)}) copy-start(bf16[768,1024]{1,0:T(8,128)(2,1)} %param.14) | copy-start | bytes 4718596
  20.2 13.4 %copy-start.3 = (s32[1,64,32]{1,2,0:T(8,128)S(1)}, s32[1,64,32]{1,2,0:T(8,128)}, u32[]{:S(2)}) copy-start(s32[1,64,32]{1,2,0:T(8,128)} %param.13) | copy-start | bytes 24580
  20.2 14.2 %copy-start.5 = (s32[256]{0:T(256)S(1)}, s32[256]{0:T(256)}, u32[]{:S(2)}) copy-start(s32[256]{0:T(256)} %param.10) | copy-start | bytes 3076
  20.2 14.2 %copy-start.1 = (bf16[1024,768]{1,0:T(8,128)(2,1)S(1)}, bf16[1024,768]{1,0:T(8,128)(2,1)}, u32[]{:S(2)}) copy-start(bf16[1024,768]{1,0:T(8,128)(2,1)} %feats_ref.1) | copy-start | bytes 4718596
  20.2 88.6 %all-to-all-start = ((bf16[64,8,3200]{2,1,0:T(8,128)(2,1)}), bf16[64,8,3200]{2,1,0:T(8,128)(2,1)}, u32[]{:S(2)}, u32[]{:S(2)}) async-start(bf16[64,8,3200]{2,1,0:T(8,128)(2,1)} %bitcast.19), calls=%async_computation | async-start | bytes 6553600 | tf_op jit(solution)/shard_map/all_to_all | solution.py:37
  33.5 133.7 %reduce-scatter.3.cloned.1.call-start = ((), (), s32[]{:S(2)}) async-start(), calls=%async_computation.7 | async-start | bytes 3833856 | tf_op jit(solution)/shard_map/reduce_scatter | solution.py:241
  34.4 1.3 copy-start.4
  35.8 82.2 %copy-start.2 = (bf16[256,768]{1,0:T(8,128)(2,1)}, bf16[256,768]{1,0:T(8,128)(2,1)S(1)}, u32[]{:S(2)}) copy-start(bf16[256,768]{1,0:T(8,128)(2,1)S(1)} %broadcast_select_fusion.self_ref) | copy-start | bytes 1179652
  122.0 82.4 %all-to-all-start.1 = ((bf16[64,8,3072]{2,1,0:T(8,128)(2,1)}), bf16[64,8,3072]{2,1,0:T(8,128)(2,1)}, u32[]{:S(2)}, u32[]{:S(2)}) async-start(bf16[64,8,3072]{2,1,0:T(8,128)(2,1)} %bitcast.20), calls=%async_computation.1 | async-start | bytes 6291456 | tf_op jit(solution)/shard_map/all_to_all | solution.py:37
  128.8 79.1 %reduce-scatter.5.cloned.1.call-start = ((), (), s32[]{:S(2)}) async-start(), calls=%async_computation.8 | async-start | bytes 589824 | tf_op jit(solution)/shard_map/reduce_scatter | solution.py:253
  169.8 111.8 %all-gather.2.cloned.1.call-start = ((), (), s32[]{:S(2)}) async-start(), calls=%async_computation.9 | async-start | bytes 3833856 | tf_op jit(solution)/shard_map/all_gather | solution.py:261
  244.9 35.6 %all-to-all-start.2 = ((bf16[4,256,768]{2,1,0:T(8,128)(2,1)}), bf16[4,256,768]{2,1,0:T(8,128)(2,1)S(1)}, u32[]{:S(2)}, u32[]{:S(2)}) async-start(bf16[4,256,768]{2,1,0:T(8,128)(2,1)} %bitcast.22), calls=%async_computation.2 | async-start | bytes 3145728 | tf_op jit(solution)/shard_map/all_to_all | solution.py:37
Sparse Core Ops, SparseCore 0:
  122.1 45.0 reduce-scatter.2
  170.3 37.6 reduce-scatter.4
  237.2 43.5 all-gather.1

commit v5 on v4

v5 whole, which is shorter than its diff:
```python
import functools

import jax
import jax.numpy as jnp
import numpy as np
from jax import lax
from jax.experimental import pallas as pl
from jax.experimental.pallas import tpu as pltpu
from jax.sharding import Mesh, PartitionSpec as P

DOM = ("z", "x", "c")
NEAR = ("c", "rep")
FAR = ("x", "z")
bf16 = jnp.bfloat16
f32 = jnp.float32

GROUP = 4
STEP = 4
SPLIT = 4
EXTRA = 128
VMEM = pltpu.CompilerParams(vmem_limit_bytes=60 * 1024 * 1024)
MARGIN = 16


def contract_first(left, right):
    return lax.dot_general(
        left, right, (((0,), (0,)), ((), ())), preferred_element_type=f32
    )


def contract_last(left, right):
    return lax.dot_general(
        left, right, (((1,), (1,)), ((), ())), preferred_element_type=f32
    )


def exchange(value, axes):
    return lax.all_to_all(value, axes, split_axis=0, concat_axis=0, tiled=True)


def spread(value, axes):
    return jnp.broadcast_to(value[None], (lax.axis_size(axes),) + value.shape)


def cost(flops, bytes_accessed):
    return pl.CostEstimate(flops=flops, bytes_accessed=bytes_accessed, transcendentals=0)


def select_kernel(rows_ref, slots_ref, feats_ref, select_ref, partial_ref):
    row_count, width = feats_ref.shape
    dests, entry_cap = rows_ref.shape
    entries = GROUP * entry_cap
    part = select_ref.shape[1] // STEP
    s_count = part // GROUP
    slots = SPLIT * part
    named = slots_ref[...]
    place = lax.broadcasted_iota(jnp.int32, named.shape, 0) % GROUP * s_count
    keys = named // s_count * part + place + named % s_count
    keys = jnp.where(named < SPLIT * s_count, keys, -1)
    row_ids = lax.broadcasted_iota(jnp.int32, (row_count, entries), 0)
    slot_ids = lax.broadcasted_iota(jnp.int32, (slots, entries), 0)
    lanes = lax.broadcasted_iota(jnp.int32, (part, EXTRA), 1)

    def side_by_side(values, step):
        first = step * GROUP
        return jnp.concatenate(
            [values[first + i : first + i + 1] for i in range(GROUP)], axis=1
        )

    for step in range(STEP):
        here = slice(step * part, (step + 1) * part)
        by_row = jnp.where(row_ids == side_by_side(rows_ref[...], step), 1.0, 0.0)
        hits = jnp.where(slot_ids == side_by_side(keys, step), 1.0, 0.0)
        chosen = contract_last(hits.astype(bf16), by_row.astype(bf16)).astype(bf16)
        count = jnp.sum(hits, axis=1, keepdims=True)
        tail = jnp.zeros((part, EXTRA), f32)
        for j in range(SPLIT):
            select_ref[j, here, :] = chosen[j * part : (j + 1) * part]
            tail = jnp.where(lanes == j, count[j * part : (j + 1) * part], tail)
        partial_ref[here, SPLIT * width :] = tail.astype(bf16)
    for j in range(SPLIT):
        partial_ref[:, j * width : (j + 1) * width] = jnp.dot(
            select_ref[j], feats_ref[...], preferred_element_type=f32
        ).astype(bf16)


def select_and_sum(feats, edge_rows, edge_slots, slot_cap):
    dests, entry_cap = edge_rows.shape
    row_count, width = feats.shape
    s_count = slot_cap // SPLIT
    sent = dests * s_count
    steps = dests // (GROUP * STEP)
    wide = SPLIT * width + EXTRA
    edge_spec = pl.BlockSpec((GROUP * STEP, entry_cap), lambda i: (i, 0))
    return pl.pallas_call(
        select_kernel,
        grid=(steps,),
        in_specs=[
            edge_spec,
            edge_spec,
            pl.BlockSpec((row_count, width), lambda i: (0, 0)),
        ],
        out_specs=[
            pl.BlockSpec((SPLIT, sent // steps, row_count), lambda i: (0, i, 0)),
            pl.BlockSpec((sent // steps, wide), lambda i: (i, 0)),
        ],
        out_shape=[
            jax.ShapeDtypeStruct((SPLIT, sent, row_count), bf16),
            jax.ShapeDtypeStruct((sent, wide), bf16),
        ],
        compiler_params=VMEM,
        cost_estimate=cost(
            2 * SPLIT * sent * row_count * (width + GROUP * entry_cap),
            2 * (row_count * width + sent * (SPLIT * row_count + wide)),
        ),
    )(edge_rows, edge_slots, feats)


def middle_kernel(
    arrived_any,
    seeds_ref,
    base_ref,
    w_neigh_ref,
    cotangent_ref,
    self_ref,
    hidden_ref,
    delta_ref,
    routed_any,
    terms_any,
    arrived_ref,
    routed_ref,
    terms_ref,
    aggregate_ref,
    pre_ref,
    neigh_ref,
    degree_ref,
    in_sems,
    out_sems,
):
    seed_count = base_ref.shape[0]
    width = w_neigh_ref.shape[0]
    sent = seeds_ref.shape[2]
    near, tall, hidden = terms_ref.shape
    block = tall - MARGIN
    ids = lax.broadcasted_iota(jnp.int32, (seed_count, sent), 0)
    lanes = lax.broadcasted_iota(jnp.int32, (seed_count, EXTRA), 1)

    def columns(j):
        return slice(j * width, (j + 1) * width if j < SPLIT else j * width + EXTRA)

    def routing(j):
        return jnp.where(ids == seeds_ref[j], 1.0, 0.0).astype(bf16)

    loads = [
        pltpu.make_async_copy(
            arrived_any.at[:, columns(j)], arrived_ref.at[:, columns(j)], in_sems.at[j]
        )
        for j in range(SPLIT + 1)
    ]
    loads[SPLIT].start()
    for j in range(SPLIT):
        loads[j].start()

    total = jnp.zeros((seed_count, width), f32)
    counts = jnp.zeros((seed_count, EXTRA), f32)
    loads[SPLIT].wait()
    for j in range(SPLIT):
        route = routing(j)
        loads[j].wait()
        total += jnp.dot(route, arrived_ref[:, columns(j)], preferred_element_type=f32)
        found = jnp.dot(
            route, arrived_ref[:, columns(SPLIT)], preferred_element_type=f32
        )
        counts += jnp.where(lanes == j, found, 0.0)
    degree = jnp.maximum(jnp.sum(counts, axis=1, keepdims=True), 1.0)
    degree_ref[...] = jnp.broadcast_to(degree, (seed_count, EXTRA))
    aggregate_ref[...] = (total / degree).astype(bf16)
    pre_ref[...] = base_ref[...] + jnp.dot(
        aggregate_ref[...], w_neigh_ref[...], preferred_element_type=f32
    )

    rows = 16
    slope = (2.0 / np.pi) ** 0.5

    @pl.loop(0, seed_count // rows)
    def _(i):
        here = pl.ds(pl.multiple_of(i * rows, rows), rows)
        pre = pre_ref[here, :]
        square = pre * pre
        bend = jnp.tanh(slope * pre * (1.0 + 0.044715 * square))
        half = 0.5 * (1.0 + bend)
        hidden_ref[here, :] = (pre * half).astype(bf16)
        steep = half + 0.5 * pre * (1.0 - bend * bend) * (
            slope * (1.0 + 3 * 0.044715 * square)
        )
        delta = (cotangent_ref[here, :].astype(f32) * steep).astype(bf16)
        delta_ref[here, :] = delta
        neigh_ref[here, :] = (delta.astype(f32) / degree_ref[here, 0:1]).astype(bf16)

    copies = []

    def send(source, target):
        copy = pltpu.make_async_copy(source, target, out_sems.at[len(copies)])
        copy.start()
        copies.append(copy)

    grad = contract_last(neigh_ref[...], w_neigh_ref[...]).astype(bf16)
    for j in range(SPLIT):
        routed_ref[:, columns(j)] = contract_first(routing(j), grad).astype(bf16)
        send(routed_ref.at[:, columns(j)], routed_any.at[:, columns(j)])

    delta = delta_ref[...]
    column = jnp.sum(delta.astype(f32), axis=0, keepdims=True)
    first = lax.broadcasted_iota(jnp.int32, (MARGIN, hidden), 0) == 0
    margin = jnp.where(first, column, 0.0).astype(bf16)
    half = near // 2
    for side, left in enumerate((self_ref, aggregate_ref)):
        product = contract_first(left[...], delta).astype(bf16)
        mine = slice(side * half, (side + 1) * half)
        for b in range(half):
            terms_ref[side * half + b, :block, :] = product[b * block : (b + 1) * block]
            terms_ref[side * half + b, block:, :] = margin
        send(terms_ref.at[mine], terms_any.at[mine])
    for copy in copies:
        copy.wait()


def middle(arrived, seeds, base, w_neigh, cotangent, self_rows):
    sent, wide = arrived.shape
    seed_count, hidden = base.shape
    width = w_neigh.shape[0]
    near = lax.axis_size(NEAR)
    terms = (near, 2 * width // near + MARGIN, hidden)
    vmem = pl.BlockSpec(memory_space=pltpu.VMEM)
    hbm = pl.BlockSpec(memory_space=pltpu.HBM)
    return pl.pallas_call(
        middle_kernel,
        in_specs=[hbm] + [vmem] * 5,
        out_specs=[vmem, vmem, hbm, hbm],
        out_shape=[
            jax.ShapeDtypeStruct((seed_count, hidden), bf16),
            jax.ShapeDtypeStruct((seed_count, hidden), bf16),
            jax.ShapeDtypeStruct((sent, SPLIT * width), bf16),
            jax.ShapeDtypeStruct(terms, bf16),
        ],
        scratch_shapes=[
            pltpu.VMEM((sent, wide), bf16),
            pltpu.VMEM((sent, SPLIT * width), bf16),
            pltpu.VMEM(terms, bf16),
            pltpu.VMEM((seed_count, width), bf16),
            pltpu.VMEM((seed_count, hidden), f32),
            pltpu.VMEM((seed_count, hidden), bf16),
            pltpu.VMEM((seed_count, EXTRA), f32),
            pltpu.SemaphoreType.DMA((SPLIT + 1,)),
            pltpu.SemaphoreType.DMA((SPLIT + 2,)),
        ],
        compiler_params=pltpu.CompilerParams(vmem_limit_bytes=40 * 1024 * 1024),
        cost_estimate=cost(
            4 * seed_count * width * (SPLIT * sent + 2 * hidden),
            2 * (2 * arrived.size + 3 * w_neigh.size + 5 * base.size),
        ),
    )(arrived, seeds, base, w_neigh, cotangent, self_rows)


def after(value, earlier):
    def kernel(value_ref, earlier_ref, out_ref):
        pass

    return pl.pallas_call(
        kernel,
        in_specs=[pl.BlockSpec(memory_space=pl.ANY)] * 2,
        out_specs=pl.BlockSpec(memory_space=pl.ANY),
        out_shape=jax.ShapeDtypeStruct(value.shape, value.dtype),
        input_output_aliases={0: 0},
    )(value, earlier)


def reduce_everywhere(terms, earlier, meanwhile):
    _, tall, hidden = terms.shape
    block = tall - MARGIN
    part = block // lax.axis_size("x")
    piece = part // lax.axis_size("z")
    summed = lax.psum_scatter(
        terms.reshape(-1, hidden), NEAR, scatter_dimension=0, tiled=True
    )
    parts = summed[:block].reshape(-1, part, hidden)
    margin = summed[None, block : block + 8]
    parts = jnp.concatenate([parts, jnp.repeat(margin, block // part, axis=0)], axis=1)
    line = lax.psum_scatter(
        parts.reshape(-1, hidden), "x", scatter_dimension=0, tiled=True
    )
    line = after(line, earlier)
    pieces = line[:part].reshape(-1, piece, hidden)
    margin = line[None, part : part + 2]
    pieces = jnp.concatenate([pieces, jnp.repeat(margin, part // piece, axis=0)], axis=1)
    total = jnp.sum(exchange(pieces, "z").astype(f32), axis=0).astype(bf16)
    own = exchange(spread(total, FAR), FAR)
    margin = jnp.concatenate([own[0, piece:]] * (MARGIN // 2), axis=0)
    own = jnp.concatenate([own[:, :piece].reshape(block, hidden), margin], axis=0)
    return lax.all_gather(after(own, meanwhile), NEAR, axis=0, tiled=True)


def scaled_kernel(scale, upper_ref, lower_ref, self_ref, neigh_ref, bias_ref):
    block = self_ref.shape[0]
    self_ref[...] = upper_ref[:block, :].astype(f32) * scale
    neigh_ref[...] = lower_ref[:block, :].astype(f32) * scale

    @pl.when(pl.program_id(0) == 0)
    def _():
        bias_ref[...] = upper_ref[block : block + MARGIN, :].astype(f32)[0:1] * scale


def scaled_parts(full, width, scale):
    hidden = full.shape[1]
    near = lax.axis_size(NEAR)
    tall = full.shape[0] // near
    half = near // 2
    block = width // half
    grad_spec = pl.BlockSpec((block, hidden), lambda i: (i, 0))
    return pl.pallas_call(
        functools.partial(scaled_kernel, scale),
        grid=(half,),
        in_specs=[
            pl.BlockSpec((tall, hidden), lambda i: (i, 0)),
            pl.BlockSpec((tall, hidden), lambda i: (i + half, 0)),
        ],
        out_specs=[
            grad_spec,
            grad_spec,
            pl.BlockSpec((1, hidden), lambda i: (0, 0)),
        ],
        out_shape=[
            jax.ShapeDtypeStruct((width, hidden), f32),
            jax.ShapeDtypeStruct((width, hidden), f32),
            jax.ShapeDtypeStruct((1, hidden), f32),
        ],
        compiler_params=VMEM,
        cost_estimate=cost(full.size, 6 * full.size),
    )(full, full)


def scatter_kernel(select_ref, grad_ref, out_ref):
    width = out_ref.shape[1]
    total = contract_first(select_ref[0], grad_ref[:, :width])
    for j in range(1, SPLIT):
        total += contract_first(select_ref[j], grad_ref[:, j * width : (j + 1) * width])
    out_ref[...] = total.astype(bf16)


def scatter_sum(select, slot_grad):
    _, sent, rows = select.shape
    width = slot_grad.shape[1] // SPLIT
    return pl.pallas_call(
        scatter_kernel,
        out_shape=jax.ShapeDtypeStruct((rows, width), bf16),
        compiler_params=VMEM,
        cost_estimate=cost(
            2 * SPLIT * sent * rows * width, 2 * (select.size + slot_grad.size)
        ),
    )(select, slot_grad)


def on_device(
    feats, seed_rows, edge_rows, edge_slots, slot_seeds, w_self, w_neigh, bias, cotangent
):
    edge_rows = edge_rows[0]
    edge_slots = edge_slots[0]
    slot_seeds = slot_seeds[0]
    sources, slot_cap = slot_seeds.shape
    s_count = slot_cap // SPLIT
    seed_count = seed_rows.shape[0]
    width = feats.shape[1]
    replicas = lax.axis_size("rep")
    select, partial_value = select_and_sum(feats, edge_rows, edge_slots, slot_cap)
    arrived = exchange(partial_value.reshape(sources, s_count, -1), DOM)
    seeds = slot_seeds.reshape(sources, SPLIT, s_count).transpose(1, 0, 2)
    seeds = seeds.reshape(SPLIT, 1, sources * s_count)
    self_rows = jnp.take(feats, seed_rows, axis=0)
    base = jnp.dot(self_rows, w_self, preferred_element_type=f32) + bias[None, :]
    hidden_out, delta, routed, terms = middle(
        arrived.reshape(sources * s_count, -1), seeds, base, w_neigh, cotangent, self_rows
    )

    slot_grad = exchange(routed.reshape(sources, s_count, -1), DOM)
    self_grad = contract_last(delta, w_self).astype(bf16)
    local = scatter_sum(select, slot_grad.reshape(sources * s_count, -1))
    feat_grads = lax.psum_scatter(local, "rep", scatter_dimension=0, tiled=True)
    full = reduce_everywhere(terms, slot_grad, feat_grads)
    scale = float(seed_count * lax.axis_size(DOM) * replicas) ** (-0.5)
    grad_self, grad_neigh, grad_bias = scaled_parts(full, width, scale)
    return (
        hidden_out,
        self_grad,
        feat_grads,
        grad_self,
        grad_neigh,
        grad_bias.reshape(-1),
    )


def solution(mesh):
    fine = Mesh(
        np.asarray(mesh.devices).reshape(8, 4, 2, 4), ("z", "x", "c", "rep")
    )
    every = DOM + ("rep",)
    in_specs = (
        P(DOM, None),
        P(every),
        P(every, None, None),
        P(every, None, None),
        P(every, None, None),
        P(),
        P(),
        P(),
        P(every, None),
    )
    out_specs = (P(every, None), P(every, None), P(every, None), P(), P(), P())
    return jax.shard_map(
        on_device, mesh=fine, in_specs=in_specs, out_specs=out_specs, check_vma=False
    )
```

time: 297 us -> 290 us (0.976)
  local copies, waits for them, and re-layouts: 8.65 us -> 13.3 us
  waiting for transfers between devices: 177 us -> 173 us
  blocking collectives: 27.3 us -> 31 us
  starting transfers between devices: 24 us -> 20.5 us
    all_to_all x3 -> x2, waiting for transfers between devices: 135 us -> 104 us  [exchange(): return lax.all_to_all(value, axes, split_axis=0, concat_axis=0, tiled=True)]
    all_gather x1, waiting for transfers between devices: 0.01 us -> 31 us  [reduce_everywhere(): return lax.all_gather(after(own, meanwhile), NEAR, axis=0, tiled=True)]
    unnamed x12 -> x22, local copies, waits for them, and re-layouts: 0.04 us -> 5.64 us
    all_to_all x3 -> x2, starting transfers between devices: 23.9 us -> 20.1 us  [exchange(): return lax.all_to_all(value, axes, split_axis=0, concat_axis=0, tiled=True)]
    all_to_all x2, blocking collectives: 27.3 us -> 31 us  [exchange(): return lax.all_to_all(value, axes, split_axis=0, concat_axis=0, tiled=True)]
    reduce_scatter x1 -> x2, waiting for transfers between devices: 3.49 us -> 0.02 us  [the longest x1 0.02 us: reduce_everywhere(): lax.psum_scatter(parts.reshape(-1, hidden), 'x', scatter_dimension=0, til...]
    pallas_call x3 -> x2, Pallas kernels: 22.9 us -> 20.6 us  [the longest x1 10.5 us: middle(): pl.pallas_call(middle_kernel, in_specs=[hbm] + [vmem] * 5, out_specs=[vme...]
  transfers between devices with their start and end apart: 6 -> 6, of which waited for: 5 -> 4; matrix products, arithmetic and copies ran while one was open for 3% -> 4% of each run, Pallas kernels for 3% -> 3%
where the time goes in v5:
time: 290 us; the launch traced here: 289 us
  waiting for transfers between devices  173 us (60%)
  Pallas kernels  33.5 us (12%)
  blocking collectives  31 us (11%)
  starting transfers between devices  20.5 us (7%)
  between operations  14 us (5%)
  local copies, waits for them, and re-layouts  13.3 us (5%)
    all_to_all x2, waiting for transfers between devices, exchange(): return lax.all_to_all(value, axes, split_axis=0, concat_axis=0, tiled=True)  104 us
    reduce_scatter x1, waiting for transfers between devices, reduce_everywhere(): lax.psum_scatter(terms.reshape(-1, hidden), NEAR, scatter_dimension=0, ti...  38.3 us
    all_gather x1, waiting for transfers between devices, reduce_everywhere(): return lax.all_gather(after(own, meanwhile), NEAR, axis=0, tiled=True)  31 us
    all_to_all x2, blocking collectives, exchange(): return lax.all_to_all(value, axes, split_axis=0, concat_axis=0, tiled=True)  31 us
    all_to_all x2, starting transfers between devices, exchange(): return lax.all_to_all(value, axes, split_axis=0, concat_axis=0, tiled=True)  20.1 us
    pallas_call x1, Pallas kernels, middle(): pl.pallas_call(middle_kernel, in_specs=[hbm] + [vmem] * 5, out_specs=[vme...  10.5 us
    pallas_call x1, Pallas kernels, select_and_sum(): pl.pallas_call(select_kernel, grid=(steps,), in_specs=[edge_spec, edge_sp...  10.1 us
    pallas_call x1, Pallas kernels, scatter_sum(): pl.pallas_call(scatter_kernel, out_shape=jax.ShapeDtypeStruct((rows, widt...  7.83 us
  transfers between devices with their start and end apart: 6, of which 4 were waited for; matrix products, arithmetic and copies ran while one was open for 4% of the time, Pallas kernels for 3%

profile of v5, /device:TPU:1, one launch (start us, length us, event | category | flops | bytes accessed | tf_op | source)
XLA Modules:
  0.0 289.2 jit_solution(6112700473920269996)
XLA Ops:
  7.2 0.0 copy-start
  7.2 10.1 %shard_map.136 = (bf16[4,512,1024]{2,1,0:T(8,128)(2,1)}, bf16[512,3200]{1,0:T(8,128)(2,1)}) custom-call(s32[64,64]{1,0:T(8,128)} %bitcast.27, s32[64,64]{1,0:T(8,128)} %bitcast.28, bf16[1024,768]{1,0:T(8,128)(2,1)} %feats_ref.1), custom_call_target="tpu_custom_call" | custom-call | flops 4294967296 | bytes 9043968 | tf_op jit(solution)/shard_map/pallas_call | solution.py:95
  17.3 0.0 copy-start.8
  17.3 0.0 copy-start.10
  17.3 0.0 copy-start.7
  17.3 13.3 %all-to-all-start = ((bf16[64,8,3200]{2,1,0:T(8,128)(2,1)}), bf16[64,8,3200]{2,1,0:T(8,128)(2,1)}, u32[]{:S(2)}, u32[]{:S(2)}) async-start(bf16[64,8,3200]{2,1,0:T(8,128)(2,1)} %bitcast.21), calls=%async_computation | async-start | bytes 6553600 | tf_op jit(solution)/shard_map/all_to_all | solution.py:38
  30.6 0.0 reduce-scatter.6.cloned.1.call-start
  30.7 0.0 copy-done.8
  30.7 0.1 copy.18
  30.8 0.1 reshape.80.seeds_ref
  30.9 0.0 copy-done.10
  30.9 0.0 copy-done.7
  30.9 0.0 copy-start.9
  30.9 1.2 gather_fusion
  32.1 0.7 compare_and_fusion
  32.8 0.1 broadcast_select_fusion.self_ref
  32.9 0.0 copy-done
  32.9 0.0 copy-done.9
  33.0 0.0 copy-start.4
  33.0 0.6 convolution_add_fusion.base_ref
  33.6 72.3 %all-to-all-done = bf16[64,8,3200]{2,1,0:T(8,128)(2,1)} async-done(((bf16[64,8,3200]{2,1,0:T(8,128)(2,1)}), bf16[64,8,3200]{2,1,0:T(8,128)(2,1)}, u32[]{:S(2)}, u32[]{:S(2)}) %all-to-all-start) | async-done | bytes 3276832 | tf_op jit(solution)/shard_map/all_to_all | solution.py:38
  105.9 0.0 copy-done.4
  105.9 0.0 copy-start.3
  105.9 1.4 copy-done.3
  107.3 10.5 %shard_map.137 = (bf16[256,1024]{1,0:T(8,128)(2,1)}, bf16[256,1024]{1,0:T(8,128)(2,1)S(1)}, bf16[512,3072]{1,0:T(8,128)(2,1)S(1)}, bf16[8,208,1024]{2,1,0:T(8,128)(2,1)S(1)}) custom-call(bf16[512,3200]{1,0:T(8,128)(2,1)} %bitcast.3.arrived_any, s32[4,1,512]{2,1,0:T(1,128)S(1)} %reshape.80.seeds_ref, f32[256,1024]{1,0:T(8,128)S(1)} %convolution_add_fusion.base_ref, ...), custom_call_target="tpu_custom_call" | custom-call | flops 3221225472 | bytes 13893632 | tf_op jit(solution)/shard_map/pallas_call | solution.py:236
  117.8 0.0 copy-start.1
  117.8 1.7 copy-done.1
  119.6 0.0 copy-start.2
  119.6 1.7 copy-done.2
  121.2 0.0 copy-start.5
  121.2 0.8 copy-done.5
  122.0 0.0 reduce-scatter.6.cloned.1.call-update
  122.0 6.8 %all-to-all-start.1 = ((bf16[64,8,3072]{2,1,0:T(8,128)(2,1)}), bf16[64,8,3072]{2,1,0:T(8,128)(2,1)}, u32[]{:S(2)}, u32[]{:S(2)}) async-start(bf16[64,8,3072]{2,1,0:T(8,128)(2,1)} %bitcast.20), calls=%async_computation.1 | async-start | bytes 6291456 | tf_op jit(solution)/shard_map/all_to_all | solution.py:38
  128.9 0.0 reduce-scatter.8.cloned.1.call-start
  128.9 38.3 %reduce-scatter.6.cloned.1.call-done = bf16[208,1024]{1,0:T(8,128)(2,1)} async-done(((bf16[1664,1024]{1,0:T(8,128)(2,1)}), bf16[208,1024]{1,0:T(8,128)(2,1)}) %reduce-scatter.6.cloned.1.call-update) | async-done | bytes 426000 | tf_op jit(solution)/shard_map/reduce_scatter | solution.py:283
  167.2 0.7 slice.27
  167.9 1.0 slice.26
  169.0 0.8 pad_maximum_fusion
  169.8 0.0 reduce-scatter.8.cloned.1.call-update
  169.8 0.2 reduce-scatter.4.cloned.1.call-start
  170.1 31.5 %all-to-all-done.1.earlier_ref = bf16[64,8,3072]{2,1,0:T(8,128)(2,1)} async-done(((bf16[64,8,3072]{2,1,0:T(8,128)(2,1)}), bf16[64,8,3072]{2,1,0:T(8,128)(2,1)}, u32[]{:S(2)}, u32[]{:S(2)}) %all-to-all-start.1) | async-done | bytes 3145760 | tf_op jit(solution)/shard_map/all_to_all | solution.py:38
  201.6 7.8 %shard_map.138 = bf16[1024,768]{1,0:T(8,128)(2,1)} custom-call(bf16[4,512,1024]{2,1,0:T(8,128)(2,1)} %get-tuple-element.18.select_ref, bf16[512,3072]{1,0:T(8,128)(2,1)} %bitcast.7.grad_ref), custom_call_target="tpu_custom_call" | custom-call | flops 3221225472 | bytes 7340032 | tf_op jit(solution)/shard_map/pallas_call | solution.py:353
  209.4 0.0 reduce-scatter.4.cloned.1.call-update
  209.4 0.0 all-gather.2.cloned.1.call-start
  209.5 0.0 reduce-scatter.8.cloned.1.call-done.value_ref
  209.5 0.7 slice.29
  210.2 0.9 slice.28
  211.2 0.1 pad_maximum_fusion.1
  211.3 14.0 %all_to_all.20 = bf16[8,8,1024]{2,1,0:T(8,128)(2,1)S(1)} all-to-all(bf16[8,8,1024]{2,1,0:T(8,128)(2,1)S(1)} %pad_maximum_fusion.1), channel_id=1, replica_groups=mesh['z'=8,'x'=4,'c'=2,'rep'=4] {'z'}, dimensions={0} | all-to-all | bytes 262144 | tf_op jit(solution)/shard_map/all_to_all | solution.py:38
  225.3 0.1 broadcast_in_dim.26
  225.4 17.0 %all_to_all.21 = bf16[32,8,1024]{2,1,0:T(8,128)(2,1)S(1)} all-to-all(bf16[32,8,1024]{2,1,0:T(8,128)(2,1)S(1)} %broadcast_in_dim.26), channel_id=1, replica_groups=mesh['z'=8,'x'=4,'c'=2,'rep'=4] {'x','z'}, dimensions={0} | all-to-all | bytes 1048576 | tf_op jit(solution)/shard_map/all_to_all | solution.py:38
  242.4 0.0 copy-start.6
  242.4 0.1 reshape.69
  242.5 2.6 concatenate.11.value_ref
  245.2 0.0 reduce-scatter.4.cloned.1.call-done.earlier_ref
  245.2 0.0 all-gather.2.cloned.1.call-update
  245.2 0.0 copy-done.6
  245.2 1.4 convolution_convert_fusion
  246.6 31.0 %all-gather.2.cloned.1.call-done.upper_ref.lower_ref = bf16[1664,1024]{1,0:T(8,128)(2,1)} async-done(((bf16[208,1024]{1,0:T(8,128)(2,1)}), bf16[1664,1024]{1,0:T(8,128)(2,1)}) %all-gather.2.cloned.1.call-update) | async-done | bytes 3407888 | tf_op jit(solution)/shard_map/all_gather | solution.py:300
  277.6 5.1 %shard_map.141 = (f32[768,1024]{1,0:T(8,128)}, f32[768,1024]{1,0:T(8,128)}, f32[1,1024]{1,0:T(1,128)}) custom-call(bf16[1664,1024]{1,0:T(8,128)(2,1)} %all-gather.2.cloned.1.call-done.upper_ref.lower_ref, bf16[1664,1024]{1,0:T(8,128)(2,1)} %all-gather.2.cloned.1.call-done.upper_ref.lower_ref), custom_call_target="tpu_custom_call" | custom-call | flops 1703936 | bytes 10223616 | tf_op jit(solution)/shard_map/pallas_call | solution.py:320
  (9 shorter events, 0.1 us)
Async XLA Ops:
  7.2 25.8 %copy-start = (bf16[768,1024]{1,0:T(8,128)(2,1)S(1)}, bf16[768,1024]{1,0:T(8,128)(2,1)}, u32[]{:S(2)}) copy-start(bf16[768,1024]{1,0:T(8,128)(2,1)} %param.14) | copy-start | bytes 4718596
  17.3 13.4 %copy-start.8 = (s32[1,64,32]{1,2,0:T(8,128)S(1)}, s32[1,64,32]{1,2,0:T(8,128)}, u32[]{:S(2)}) copy-start(s32[1,64,32]{1,2,0:T(8,128)} %param.13) | copy-start | bytes 24580
  17.3 13.6 %copy-start.10 = (s32[256]{0:T(256)S(1)}, s32[256]{0:T(256)}, u32[]{:S(2)}) copy-start(s32[256]{0:T(256)} %param.10) | copy-start | bytes 3076
  17.3 13.6 %copy-start.7 = (bf16[1024,768]{1,0:T(8,128)(2,1)S(1)}, bf16[1024,768]{1,0:T(8,128)(2,1)}, u32[]{:S(2)}) copy-start(bf16[1024,768]{1,0:T(8,128)(2,1)} %feats_ref.1) | copy-start | bytes 4718596
  17.3 88.6 %all-to-all-start = ((bf16[64,8,3200]{2,1,0:T(8,128)(2,1)}), bf16[64,8,3200]{2,1,0:T(8,128)(2,1)}, u32[]{:S(2)}, u32[]{:S(2)}) async-start(bf16[64,8,3200]{2,1,0:T(8,128)(2,1)} %bitcast.21), calls=%async_computation | async-start | bytes 6553600 | tf_op jit(solution)/shard_map/all_to_all | solution.py:38
  30.6 136.6 %reduce-scatter.6.cloned.1.call-start = ((), (), s32[]{:S(2)}) async-start(), calls=%async_computation.8 | async-start | bytes 3833856 | tf_op jit(solution)/shard_map/reduce_scatter | solution.py:283
  30.9 2.0 copy-start.9
  33.0 72.9 %copy-start.4 = (bf16[256,1024]{1,0:T(8,128)(2,1)S(1)}, bf16[256,1024]{1,0:T(8,128)(2,1)}, u32[]{:S(2)}) copy-start(bf16[256,1024]{1,0:T(8,128)(2,1)} %cotangent_ref.1) | copy-start | bytes 1572868
  105.9 1.4 copy-start.3
  117.8 1.7 copy-start.1
  119.6 1.7 copy-start.2
  121.2 0.8 copy-start.5
  122.0 79.5 %all-to-all-start.1 = ((bf16[64,8,3072]{2,1,0:T(8,128)(2,1)}), bf16[64,8,3072]{2,1,0:T(8,128)(2,1)}, u32[]{:S(2)}, u32[]{:S(2)}) async-start(bf16[64,8,3072]{2,1,0:T(8,128)(2,1)} %bitcast.20), calls=%async_computation.1 | async-start | bytes 6291456 | tf_op jit(solution)/shard_map/all_to_all | solution.py:38
  128.9 80.6 %reduce-scatter.8.cloned.1.call-start = ((), (), s32[]{:S(2)}) async-start(), calls=%async_computation.9 | async-start | bytes 573440 | tf_op jit(solution)/shard_map/reduce_scatter | solution.py:289
  169.8 75.3 %reduce-scatter.4.cloned.1.call-start = ((), (), s32[]{:S(2)}) async-start(), calls=%async_computation.7 | async-start | bytes 1966080 | tf_op jit(solution)/shard_map/reduce_scatter | solution.py:387
  209.4 68.2 %all-gather.2.cloned.1.call-start = ((), (), s32[]{:S(2)}) async-start(), calls=%async_computation.10 | async-start | bytes 3833856 | tf_op jit(solution)/shard_map/all_gather | solution.py:300
  242.4 2.8 copy-start.6
Sparse Core Ops, SparseCore 0:
  122.2 45.0 reduce-scatter.5
  169.9 25.9 reduce-scatter.7
  209.6 24.5 reduce-scatter.3
  245.3 32.2 all-gather.1

commit v6 on v5

--- a/solution.py
+++ b/solution.py
@@ -78,10 +78,11 @@
             select_ref[j, here, :] = chosen[j * part : (j + 1) * part]
             tail = jnp.where(lanes == j, count[j * part : (j + 1) * part], tail)
         partial_ref[here, SPLIT * width :] = tail.astype(bf16)
+    height = STEP * part
+    chosen = select_ref[...].reshape(SPLIT * height, row_count)
+    sums = jnp.dot(chosen, feats_ref[...], preferred_element_type=f32).astype(bf16)
     for j in range(SPLIT):
-        partial_ref[:, j * width : (j + 1) * width] = jnp.dot(
-            select_ref[j], feats_ref[...], preferred_element_type=f32
-        ).astype(bf16)
+        partial_ref[:, j * width : (j + 1) * width] = sums[j * height : (j + 1) * height]
 
 
 def select_and_sum(feats, edge_rows, edge_slots, slot_cap):
@@ -119,19 +120,26 @@
 def middle_kernel(
     arrived_any,
     seeds_ref,
+    base_any,
+    w_neigh_any,
+    cotangent_any,
+    turned_any,
+    self_any,
+    hidden_any,
+    delta_any,
+    routed_any,
+    terms_any,
+    arrived_ref,
     base_ref,
     w_neigh_ref,
     cotangent_ref,
+    turned_ref,
     self_ref,
     hidden_ref,
     delta_ref,
-    routed_any,
-    terms_any,
-    arrived_ref,
     routed_ref,
     terms_ref,
     aggregate_ref,
-    pre_ref,
     neigh_ref,
     degree_ref,
     in_sems,
@@ -148,25 +156,27 @@
     def columns(j):
         return slice(j * width, (j + 1) * width if j < SPLIT else j * width + EXTRA)
 
-    def routing(j):
-        return jnp.where(ids == seeds_ref[j], 1.0, 0.0).astype(bf16)
-
-    loads = [
-        pltpu.make_async_copy(
-            arrived_any.at[:, columns(j)], arrived_ref.at[:, columns(j)], in_sems.at[j]
-        )
-        for j in range(SPLIT + 1)
-    ]
-    loads[SPLIT].start()
-    for j in range(SPLIT):
-        loads[j].start()
+    loads = []
+
+    def load(source, target):
+        copy = pltpu.make_async_copy(source, target, in_sems.at[len(loads)])
+        copy.start()
+        loads.append(copy)
+
+    for j in (SPLIT, *range(SPLIT)):
+        load(arrived_any.at[:, columns(j)], arrived_ref.at[:, columns(j)])
+    load(w_neigh_any, w_neigh_ref)
+    load(base_any, base_ref)
+    load(cotangent_any, cotangent_ref)
+    load(turned_any, turned_ref)
+    load(self_any, self_ref)
 
     total = jnp.zeros((seed_count, width), f32)
     counts = jnp.zeros((seed_count, EXTRA), f32)
-    loads[SPLIT].wait()
+    loads[0].wait()
     for j in range(SPLIT):
-        route = routing(j)
-        loads[j].wait()
+        route = jnp.where(ids == seeds_ref[j], 1.0, 0.0).astype(bf16)
+        loads[1 + j].wait()
         total += jnp.dot(route, arrived_ref[:, columns(j)], preferred_element_type=f32)
         found = jnp.dot(
             route, arrived_ref[:, columns(SPLIT)], preferred_element_type=f32
@@ -175,7 +185,9 @@
     degree = jnp.maximum(jnp.sum(counts, axis=1, keepdims=True), 1.0)
     degree_ref[...] = jnp.broadcast_to(degree, (seed_count, EXTRA))
     aggregate_ref[...] = (total / degree).astype(bf16)
-    pre_ref[...] = base_ref[...] + jnp.dot(
+    for later in loads[1 + SPLIT :]:
+        later.wait()
+    base_ref[...] += jnp.dot(
         aggregate_ref[...], w_neigh_ref[...], preferred_element_type=f32
     )
 
@@ -185,7 +197,7 @@
     @pl.loop(0, seed_count // rows)
     def _(i):
         here = pl.ds(pl.multiple_of(i * rows, rows), rows)
-        pre = pre_ref[here, :]
+        pre = base_ref[here, :]
         square = pre * pre
         bend = jnp.tanh(slope * pre * (1.0 + 0.044715 * square))
         half = 0.5 * (1.0 + bend)
@@ -206,16 +218,24 @@
 
     grad = contract_last(neigh_ref[...], w_neigh_ref[...]).astype(bf16)
     for j in range(SPLIT):
-        routed_ref[:, columns(j)] = contract_first(routing(j), grad).astype(bf16)
+        routed_ref[:, columns(j)] = jnp.dot(
+            turned_ref[j], grad, preferred_element_type=f32
+        ).astype(bf16)
         send(routed_ref.at[:, columns(j)], routed_any.at[:, columns(j)])
 
+    send(hidden_ref, hidden_any)
+    send(delta_ref, delta_any)
     delta = delta_ref[...]
     column = jnp.sum(delta.astype(f32), axis=0, keepdims=True)
     first = lax.broadcasted_iota(jnp.int32, (MARGIN, hidden), 0) == 0
     margin = jnp.where(first, column, 0.0).astype(bf16)
     half = near // 2
-    for side, left in enumerate((self_ref, aggregate_ref)):
-        product = contract_first(left[...], delta).astype(bf16)
+    products = (
+        jnp.dot(self_ref[...], delta, preferred_element_type=f32),
+        contract_first(aggregate_ref[...], delta),
+    )
+    for side, product in enumerate(products):
+        product = product.astype(bf16)
         mine = slice(side * half, (side + 1) * half)
         for b in range(half):
             terms_ref[side * half + b, :block, :] = product[b * block : (b + 1) * block]
@@ -225,41 +245,39 @@
         copy.wait()
 
 
-def middle(arrived, seeds, base, w_neigh, cotangent, self_rows):
+def middle(arrived, seeds, base, w_neigh, cotangent, turned, self_turned):
     sent, wide = arrived.shape
     seed_count, hidden = base.shape
     width = w_neigh.shape[0]
     near = lax.axis_size(NEAR)
     terms = (near, 2 * width // near + MARGIN, hidden)
-    vmem = pl.BlockSpec(memory_space=pltpu.VMEM)
     hbm = pl.BlockSpec(memory_space=pltpu.HBM)
+    loaded = (arrived, base, w_neigh, cotangent, turned, self_turned)
+    results = [
+        jax.ShapeDtypeStruct((seed_count, hidden), bf16),
+        jax.ShapeDtypeStruct((seed_count, hidden), bf16),
+        jax.ShapeDtypeStruct((sent, SPLIT * width), bf16),
+        jax.ShapeDtypeStruct(terms, bf16),
+    ]
     return pl.pallas_call(
         middle_kernel,
-        in_specs=[hbm] + [vmem] * 5,
-        out_specs=[vmem, vmem, hbm, hbm],
-        out_shape=[
-            jax.ShapeDtypeStruct((seed_count, hidden), bf16),
-            jax.ShapeDtypeStruct((seed_count, hidden), bf16),
-            jax.ShapeDtypeStruct((sent, SPLIT * width), bf16),
-            jax.ShapeDtypeStruct(terms, bf16),
-        ],
-        scratch_shapes=[
-            pltpu.VMEM((sent, wide), bf16),
-            pltpu.VMEM((sent, SPLIT * width), bf16),
-            pltpu.VMEM(terms, bf16),
+        in_specs=[hbm, pl.BlockSpec(memory_space=pltpu.VMEM)] + [hbm] * 5,
+        out_specs=[hbm] * 4,
+        out_shape=results,
+        scratch_shapes=[pltpu.VMEM(one.shape, one.dtype) for one in (*loaded, *results)]
+        + [
             pltpu.VMEM((seed_count, width), bf16),
-            pltpu.VMEM((seed_count, hidden), f32),
             pltpu.VMEM((seed_count, hidden), bf16),
             pltpu.VMEM((seed_count, EXTRA), f32),
-            pltpu.SemaphoreType.DMA((SPLIT + 1,)),
-            pltpu.SemaphoreType.DMA((SPLIT + 2,)),
-        ],
-        compiler_params=pltpu.CompilerParams(vmem_limit_bytes=40 * 1024 * 1024),
+            pltpu.SemaphoreType.DMA((SPLIT + 6,)),
+            pltpu.SemaphoreType.DMA((SPLIT + 4,)),
+        ],
+        compiler_params=VMEM,
         cost_estimate=cost(
             4 * seed_count * width * (SPLIT * sent + 2 * hidden),
             2 * (2 * arrived.size + 3 * w_neigh.size + 5 * base.size),
         ),
-    )(arrived, seeds, base, w_neigh, cotangent, self_rows)
+    )(arrived, seeds, base, w_neigh, cotangent, turned, self_turned)
 
 
 def after(value, earlier):
@@ -279,25 +297,20 @@
     _, tall, hidden = terms.shape
     block = tall - MARGIN
     part = block // lax.axis_size("x")
-    piece = part // lax.axis_size("z")
     summed = lax.psum_scatter(
         terms.reshape(-1, hidden), NEAR, scatter_dimension=0, tiled=True
     )
     parts = summed[:block].reshape(-1, part, hidden)
-    margin = summed[None, block : block + 8]
-    parts = jnp.concatenate([parts, jnp.repeat(margin, block // part, axis=0)], axis=1)
+    margin = jnp.broadcast_to(summed[None, block:], (block // part, MARGIN, hidden))
+    parts = jnp.concatenate([parts, margin], axis=1)
     line = lax.psum_scatter(
         parts.reshape(-1, hidden), "x", scatter_dimension=0, tiled=True
     )
-    line = after(line, earlier)
-    pieces = line[:part].reshape(-1, piece, hidden)
-    margin = line[None, part : part + 2]
-    pieces = jnp.concatenate([pieces, jnp.repeat(margin, part // piece, axis=0)], axis=1)
+    pieces = after(line, earlier[:1, :, :EXTRA]).reshape(lax.axis_size("z"), -1, hidden)
     total = jnp.sum(exchange(pieces, "z").astype(f32), axis=0).astype(bf16)
-    own = exchange(spread(total, FAR), FAR)
-    margin = jnp.concatenate([own[0, piece:]] * (MARGIN // 2), axis=0)
-    own = jnp.concatenate([own[:, :piece].reshape(block, hidden), margin], axis=0)
-    return lax.all_gather(after(own, meanwhile), NEAR, axis=0, tiled=True)
+    own = exchange(spread(total, FAR), FAR).reshape(-1, part + MARGIN, hidden)
+    own = jnp.concatenate([own[:, :part].reshape(block, hidden), own[0, part:]], axis=0)
+    return lax.all_gather(after(own, meanwhile[:16, :EXTRA]), NEAR, axis=0, tiled=True)
 
 
 def scaled_kernel(scale, upper_ref, lower_ref, self_ref, neigh_ref, bias_ref):
@@ -305,7 +318,7 @@
     self_ref[...] = upper_ref[:block, :].astype(f32) * scale
     neigh_ref[...] = lower_ref[:block, :].astype(f32) * scale
 
-    @pl.when(pl.program_id(0) == 0)
+    @pl.when(pl.program_id(1) == 0)
     def _():
         bias_ref[...] = upper_ref[block : block + MARGIN, :].astype(f32)[0:1] * scale
 
@@ -316,18 +329,20 @@
     tall = full.shape[0] // near
     half = near // 2
     block = width // half
-    grad_spec = pl.BlockSpec((block, hidden), lambda i: (i, 0))
+    pieces = 4
+    piece = hidden // pieces
+    grad_spec = pl.BlockSpec((block, piece), lambda c, i: (i, c))
     return pl.pallas_call(
         functools.partial(scaled_kernel, scale),
-        grid=(half,),
+        grid=(pieces, half),
         in_specs=[
-            pl.BlockSpec((tall, hidden), lambda i: (i, 0)),
-            pl.BlockSpec((tall, hidden), lambda i: (i + half, 0)),
+            pl.BlockSpec((tall, piece), lambda c, i: (i, c)),
+            pl.BlockSpec((tall, piece), lambda c, i: (i + half, c)),
         ],
         out_specs=[
             grad_spec,
             grad_spec,
-            pl.BlockSpec((1, hidden), lambda i: (0, 0)),
+            pl.BlockSpec((1, piece), lambda c, i: (0, c)),
         ],
         out_shape=[
             jax.ShapeDtypeStruct((width, hidden), f32),
@@ -339,25 +354,49 @@
     )(full, full)
 
 
-def scatter_kernel(select_ref, grad_ref, out_ref):
+def scatter_kernel(turned_any, grad_any, out_ref, turned_ref, grad_ref, sems):
     width = out_ref.shape[1]
-    total = contract_first(select_ref[0], grad_ref[:, :width])
-    for j in range(1, SPLIT):
-        total += contract_first(select_ref[j], grad_ref[:, j * width : (j + 1) * width])
+    copies = []
+    for j in range(SPLIT):
+        columns = slice(j * width, (j + 1) * width)
+        for k, (source, target) in enumerate(
+            (
+                (turned_any.at[j], turned_ref.at[j]),
+                (grad_any.at[:, columns], grad_ref.at[:, columns]),
+            )
+        ):
+            copy = pltpu.make_async_copy(source, target, sems.at[j, k])
+            copy.start()
+            copies.append(copy)
+    total = jnp.zeros(out_ref.shape, f32)
+    for j in range(SPLIT):
+        copies[2 * j].wait()
+        copies[2 * j + 1].wait()
+        total += jnp.dot(
+            turned_ref[j],
+            grad_ref[:, j * width : (j + 1) * width],
+            preferred_element_type=f32,
+        )
     out_ref[...] = total.astype(bf16)
 
 
-def scatter_sum(select, slot_grad):
-    _, sent, rows = select.shape
+def scatter_sum(turned, slot_grad):
+    _, rows, sent = turned.shape
     width = slot_grad.shape[1] // SPLIT
     return pl.pallas_call(
         scatter_kernel,
+        in_specs=[pl.BlockSpec(memory_space=pltpu.HBM)] * 2,
         out_shape=jax.ShapeDtypeStruct((rows, width), bf16),
+        scratch_shapes=[
+            pltpu.VMEM(turned.shape, bf16),
+            pltpu.VMEM(slot_grad.shape, bf16),
+            pltpu.SemaphoreType.DMA((SPLIT, 2)),
+        ],
         compiler_params=VMEM,
         cost_estimate=cost(
-            2 * SPLIT * sent * rows * width, 2 * (select.size + slot_grad.size)
+            2 * SPLIT * sent * rows * width, 2 * (turned.size + slot_grad.size)
         ),
-    )(select, slot_grad)
+    )(turned, slot_grad)
 
 
 def on_device(
@@ -378,12 +417,18 @@
     self_rows = jnp.take(feats, seed_rows, axis=0)
     base = jnp.dot(self_rows, w_self, preferred_element_type=f32) + bias[None, :]
     hidden_out, delta, routed, terms = middle(
-        arrived.reshape(sources * s_count, -1), seeds, base, w_neigh, cotangent, self_rows
+        arrived.reshape(sources * s_count, -1),
+        seeds,
+        base,
+        w_neigh,
+        cotangent,
+        (seeds.reshape(SPLIT, -1, 1) == jnp.arange(seed_count)).astype(bf16),
+        self_rows.T,
     )
 
     slot_grad = exchange(routed.reshape(sources, s_count, -1), DOM)
     self_grad = contract_last(delta, w_self).astype(bf16)
-    local = scatter_sum(select, slot_grad.reshape(sources * s_count, -1))
+    local = scatter_sum(jnp.swapaxes(select, 1, 2), slot_grad.reshape(sources * s_count, -1))
     feat_grads = lax.psum_scatter(local, "rep", scatter_dimension=0, tiled=True)
     full = reduce_everywhere(terms, slot_grad, feat_grads)
     scale = float(seed_count * lax.axis_size(DOM) * replicas) ** (-0.5)

time: 290 us -> 288 us (level)
  waiting for transfers between devices: 173 us -> 165 us
  Pallas kernels: 33.5 us -> 38.8 us
    all_to_all x2, waiting for transfers between devices: 104 us -> 94.4 us  [exchange(): return lax.all_to_all(value, axes, split_axis=0, concat_axis=0, tiled=True)]
    pallas_call x0 -> x1, local copies, waits for them, and re-layouts: none -> 6.27 us  [select_and_sum(): pl.pallas_call(select_kernel, grid=(steps,), in_specs=[edge_spec, edge_sp...]
    unnamed x22 -> x12, local copies, waits for them, and re-layouts: 5.64 us -> 0.03 us
    pallas_call x3, Pallas kernels: 23.4 us -> 28.5 us  [the longest x1 10.6 us: scaled_parts(): pl.pallas_call(functools.partial(scaled_kernel, scale), grid=(pieces, hal...]
  transfers between devices with their start and end apart: 6 -> 6, of which waited for: 4 -> 4; matrix products, arithmetic and copies ran while one was open for 4% -> 6% of each run, Pallas kernels for 3% -> 3%
where the time goes in v6:
time: 288 us; the launch traced here: 287 us
  waiting for transfers between devices  165 us (57%)
  Pallas kernels  38.8 us (13%)
  blocking collectives  28.7 us (10%)
  starting transfers between devices  20.5 us (7%)
  between operations  13.9 us (5%)
  local copies, waits for them, and re-layouts  13 us (5%)
  other arithmetic  3.76 us (1%)
  matrix products  2.95 us (1%)
    all_to_all x2, waiting for transfers between devices, exchange(): return lax.all_to_all(value, axes, split_axis=0, concat_axis=0, tiled=True)  94.4 us
    reduce_scatter x1, waiting for transfers between devices, reduce_everywhere(): lax.psum_scatter(terms.reshape(-1, hidden), NEAR, scatter_dimension=0, ti...  38.3 us
    all_gather x1, waiting for transfers between devices, reduce_everywhere(): lax.all_gather(after(own, meanwhile[:16, :EXTRA]), NEAR, axis=0, tiled=True)  32.5 us
    all_to_all x2, blocking collectives, exchange(): return lax.all_to_all(value, axes, split_axis=0, concat_axis=0, tiled=True)  28.7 us
    all_to_all x2, starting transfers between devices, exchange(): return lax.all_to_all(value, axes, split_axis=0, concat_axis=0, tiled=True)  20.1 us
    pallas_call x1, Pallas kernels, scaled_parts(): pl.pallas_call(functools.partial(scaled_kernel, scale), grid=(pieces, hal...  10.6 us
    pallas_call x1, Pallas kernels, select_and_sum(): pl.pallas_call(select_kernel, grid=(steps,), in_specs=[edge_spec, edge_sp...  10.2 us
    pallas_call x1, Pallas kernels, middle(): pl.pallas_call(middle_kernel, in_specs=[hbm, pl.BlockSpec(memory_space=pl...  10.1 us
  transfers between devices with their start and end apart: 6, of which 4 were waited for; matrix products, arithmetic and copies ran while one was open for 6% of the time, Pallas kernels for 3%

profile of v6, /device:TPU:1, one launch (start us, length us, event | category | flops | bytes accessed | tf_op | source)
XLA Modules:
  0.0 286.8 jit_solution(3322142862753634413)
XLA Ops:
  7.2 0.0 copy-start
  7.2 10.2 %shard_map.136 = (bf16[4,512,1024]{2,1,0:T(8,128)(2,1)}, bf16[512,3200]{1,0:T(8,128)(2,1)}) custom-call(s32[64,64]{1,0:T(8,128)} %bitcast.36, s32[64,64]{1,0:T(8,128)} %bitcast.37, bf16[1024,768]{1,0:T(8,128)(2,1)} %feats_ref.1), custom_call_target="tpu_custom_call" | custom-call | flops 4294967296 | bytes 9043968 | tf_op jit(solution)/shard_map/pallas_call | solution.py:96
  17.4 0.0 copy-start.2
  17.4 0.0 copy-start.3
  17.4 0.0 copy-start.1
  17.4 13.3 %all-to-all-start = ((bf16[64,8,3200]{2,1,0:T(8,128)(2,1)}), bf16[64,8,3200]{2,1,0:T(8,128)(2,1)}, u32[]{:S(2)}, u32[]{:S(2)}) async-start(bf16[64,8,3200]{2,1,0:T(8,128)(2,1)} %bitcast.25), calls=%async_computation | async-start | bytes 6553600 | tf_op jit(solution)/shard_map/all_to_all | solution.py:38
  30.7 0.0 reduce-scatter.6.cloned.1.call-start
  30.8 0.0 copy-done.2
  30.8 0.1 copy.20
  30.9 0.1 eq.15
  31.0 0.7 reshape.78.seeds_ref
  31.7 0.0 copy-done.3
  31.8 0.0 copy-done.1
  31.8 1.2 gather_fusion
  33.0 0.0 copy-start.4
  33.0 0.2 copy.21
  33.2 0.8 fusion.1.self_any
  33.9 1.3 fusion.turned_any
  35.3 0.0 copy-done
  35.3 0.0 copy-done.4
  35.3 1.6 convolution_add_fusion.base_any
  36.8 69.2 %all-to-all-done = bf16[64,8,3200]{2,1,0:T(8,128)(2,1)} async-done(((bf16[64,8,3200]{2,1,0:T(8,128)(2,1)}), bf16[64,8,3200]{2,1,0:T(8,128)(2,1)}, u32[]{:S(2)}, u32[]{:S(2)}) %all-to-all-start) | async-done | bytes 3276832 | tf_op jit(solution)/shard_map/all_to_all | solution.py:38
  106.0 10.1 %shard_map.137 = (bf16[256,1024]{1,0:T(8,128)(2,1)}, bf16[256,1024]{1,0:T(8,128)(2,1)}, bf16[512,3072]{1,0:T(8,128)(2,1)}, bf16[8,208,1024]{2,1,0:T(8,128)(2,1)}) custom-call(bf16[512,3200]{1,0:T(8,128)(2,1)} %bitcast.3.arrived_any, s32[4,1,512]{2,1,0:T(1,128)} %reshape.78.seeds_ref, f32[256,1024]{1,0:T(8,128)} %convolution_add_fusion.base_any, ...), custom_call_target="tpu_custom_call" | custom-call | flops 3221225472 | bytes 13893632 | tf_op jit(solution)/shard_map/pallas_call | solution.py:262
  116.1 0.0 reduce-scatter.6.cloned.1.call-update
  116.1 6.8 %all-to-all-start.1 = ((bf16[64,8,3072]{2,1,0:T(8,128)(2,1)}), bf16[64,8,3072]{2,1,0:T(8,128)(2,1)}, u32[]{:S(2)}, u32[]{:S(2)}) async-start(bf16[64,8,3072]{2,1,0:T(8,128)(2,1)} %bitcast.26), calls=%async_computation.1 | async-start | bytes 6291456 | tf_op jit(solution)/shard_map/all_to_all | solution.py:38
  122.9 0.0 reduce-scatter.8.cloned.1.call-start
  123.0 38.3 %reduce-scatter.6.cloned.1.call-done = bf16[208,1024]{1,0:T(8,128)(2,1)} async-done(((bf16[1664,1024]{1,0:T(8,128)(2,1)}), bf16[208,1024]{1,0:T(8,128)(2,1)}) %reduce-scatter.6.cloned.1.call-update) | async-done | bytes 426000 | tf_op jit(solution)/shard_map/reduce_scatter | solution.py:300
  161.3 0.8 slice.27
  162.1 1.0 slice.26
  163.1 0.8 pad_maximum_fusion
  163.9 0.0 reduce-scatter.8.cloned.1.call-update
  163.9 0.2 reduce-scatter.4.cloned.1.call-start
  164.2 6.3 %copy.23 = bf16[4,512,1024]{1,2,0:T(8,128)(2,1)} copy(bf16[4,512,1024]{2,1,0:T(8,128)(2,1)} %get-tuple-element.18) | data formatting | bytes 8388608 | tf_op jit(solution)/shard_map/pallas_call | solution.py:96
  170.5 25.2 %all-to-all-done.1 = bf16[64,8,3072]{2,1,0:T(8,128)(2,1)} async-done(((bf16[64,8,3072]{2,1,0:T(8,128)(2,1)}), bf16[64,8,3072]{2,1,0:T(8,128)(2,1)}, u32[]{:S(2)}, u32[]{:S(2)}) %all-to-all-start.1) | async-done | bytes 3145760 | tf_op jit(solution)/shard_map/all_to_all | solution.py:38
  195.6 7.9 %shard_map.138 = bf16[1024,768]{1,0:T(8,128)(2,1)} custom-call(bf16[4,1024,512]{2,1,0:T(8,128)(2,1)} %bitcast.23, bf16[512,3072]{1,0:T(8,128)(2,1)} %bitcast.9.grad_any), custom_call_target="tpu_custom_call" | custom-call | flops 3221225472 | bytes 7340032 | tf_op jit(solution)/shard_map/pallas_call | solution.py:386
  203.6 0.0 reduce-scatter.4.cloned.1.call-update
  203.6 0.0 all-gather.2.cloned.1.call-start
  203.6 1.3 slice.28.earlier_ref
  204.9 0.0 reduce-scatter.8.cloned.1.call-done.value_ref
  204.9 13.1 %all_to_all.20 = bf16[8,8,1024]{2,1,0:T(8,128)(2,1)S(1)} all-to-all(bf16[8,8,1024]{2,1,0:T(8,128)(2,1)} %bitcast.34), channel_id=1, replica_groups=mesh['z'=8,'x'=4,'c'=2,'rep'=4] {'z'}, dimensions={0} | all-to-all | bytes 262144 | tf_op jit(solution)/shard_map/all_to_all | solution.py:38
  218.0 0.1 broadcast_in_dim.30
  218.0 0.0 copy-start.5
  218.0 15.6 %all_to_all.21 = bf16[32,8,1024]{2,1,0:T(8,128)(2,1)S(1)} all-to-all(bf16[32,8,1024]{2,1,0:T(8,128)(2,1)S(1)} %broadcast_in_dim.30), channel_id=1, replica_groups=mesh['z'=8,'x'=4,'c'=2,'rep'=4] {'x','z'}, dimensions={0} | all-to-all | bytes 1048576 | tf_op jit(solution)/shard_map/all_to_all | solution.py:38
  233.7 0.8 pad_maximum_fusion.1.value_ref
  234.5 0.0 reduce-scatter.4.cloned.1.call-done
  234.5 1.3 slice.31.earlier_ref
  235.8 0.0 all-gather.2.cloned.1.call-update
  235.8 0.0 copy-done.5
  235.8 1.4 convolution_convert_fusion
  237.2 32.5 %all-gather.2.cloned.1.call-done.upper_ref.lower_ref = bf16[1664,1024]{1,0:T(8,128)(2,1)} async-done(((bf16[208,1024]{1,0:T(8,128)(2,1)}), bf16[1664,1024]{1,0:T(8,128)(2,1)}) %all-gather.2.cloned.1.call-update) | async-done | bytes 3407888 | tf_op jit(solution)/shard_map/all_gather | solution.py:313
  269.7 10.6 %shard_map.141 = (f32[768,1024]{1,0:T(8,128)}, f32[768,1024]{1,0:T(8,128)}, f32[1,1024]{1,0:T(1,128)}) custom-call(bf16[1664,1024]{1,0:T(8,128)(2,1)} %all-gather.2.cloned.1.call-done.upper_ref.lower_ref, bf16[1664,1024]{1,0:T(8,128)(2,1)} %all-gather.2.cloned.1.call-done.upper_ref.lower_ref), custom_call_target="tpu_custom_call" | custom-call | flops 1703936 | bytes 10223616 | tf_op jit(solution)/shard_map/pallas_call | solution.py:335
  (9 shorter events, 0.1 us)
Async XLA Ops:
  7.2 28.1 %copy-start = (bf16[768,1024]{1,0:T(8,128)(2,1)S(1)}, bf16[768,1024]{1,0:T(8,128)(2,1)}, u32[]{:S(2)}) copy-start(bf16[768,1024]{1,0:T(8,128)(2,1)} %param.14) | copy-start | bytes 4718596
  17.4 13.4 %copy-start.2 = (s32[1,64,32]{1,2,0:T(8,128)S(1)}, s32[1,64,32]{1,2,0:T(8,128)}, u32[]{:S(2)}) copy-start(s32[1,64,32]{1,2,0:T(8,128)} %param.13) | copy-start | bytes 24580
  17.4 14.3 %copy-start.3 = (s32[256]{0:T(256)S(1)}, s32[256]{0:T(256)}, u32[]{:S(2)}) copy-start(s32[256]{0:T(256)} %param.10) | copy-start | bytes 3076
  17.4 14.3 %copy-start.1 = (bf16[1024,768]{1,0:T(8,128)(2,1)S(1)}, bf16[1024,768]{1,0:T(8,128)(2,1)}, u32[]{:S(2)}) copy-start(bf16[1024,768]{1,0:T(8,128)(2,1)} %feats_ref.1) | copy-start | bytes 4718596
  17.4 88.6 %all-to-all-start = ((bf16[64,8,3200]{2,1,0:T(8,128)(2,1)}), bf16[64,8,3200]{2,1,0:T(8,128)(2,1)}, u32[]{:S(2)}, u32[]{:S(2)}) async-start(bf16[64,8,3200]{2,1,0:T(8,128)(2,1)} %bitcast.25), calls=%async_computation | async-start | bytes 6553600 | tf_op jit(solution)/shard_map/all_to_all | solution.py:38
  30.7 130.5 %reduce-scatter.6.cloned.1.call-start = ((), (), s32[]{:S(2)}) async-start(), calls=%async_computation.8 | async-start | bytes 3833856 | tf_op jit(solution)/shard_map/reduce_scatter | solution.py:300
  33.0 2.3 copy-start.4
  116.1 79.5 %all-to-all-start.1 = ((bf16[64,8,3072]{2,1,0:T(8,128)(2,1)}), bf16[64,8,3072]{2,1,0:T(8,128)(2,1)}, u32[]{:S(2)}, u32[]{:S(2)}) async-start(bf16[64,8,3072]{2,1,0:T(8,128)(2,1)} %bitcast.26), calls=%async_computation.1 | async-start | bytes 6291456 | tf_op jit(solution)/shard_map/all_to_all | solution.py:38
  122.9 82.0 %reduce-scatter.8.cloned.1.call-start = ((), (), s32[]{:S(2)}) async-start(), calls=%async_computation.9 | async-start | bytes 655360 | tf_op jit(solution)/shard_map/reduce_scatter | solution.py:306
  163.9 70.6 %reduce-scatter.4.cloned.1.call-start = ((), (), s32[]{:S(2)}) async-start(), calls=%async_computation.7 | async-start | bytes 1966080 | tf_op jit(solution)/shard_map/reduce_scatter | solution.py:432
  203.6 66.1 %all-gather.2.cloned.1.call-start = ((), (), s32[]{:S(2)}) async-start(), calls=%async_computation.10 | async-start | bytes 3833856 | tf_op jit(solution)/shard_map/all_gather | solution.py:313
  218.0 17.8 %copy-start.5 = (bf16[256,1024]{1,0:T(8,128)(2,1)S(1)}, bf16[256,1024]{1,0:T(8,128)(2,1)}, u32[]{:S(2)}) copy-start(bf16[256,1024]{1,0:T(8,128)(2,1)} %get-tuple-element.17) | copy-start | bytes 1572868
Sparse Core Ops, SparseCore 0:
  116.2 45.0 reduce-scatter.5
  164.4 26.2 reduce-scatter.7
  203.7 24.6 reduce-scatter.3
  235.9 33.7 all-gather.1

commit v7 on v6

--- a/solution.py
+++ b/solution.py
@@ -306,55 +306,72 @@
     line = lax.psum_scatter(
         parts.reshape(-1, hidden), "x", scatter_dimension=0, tiled=True
     )
-    pieces = after(line, earlier[:1, :, :EXTRA]).reshape(lax.axis_size("z"), -1, hidden)
+    pieces = after(line, earlier).reshape(lax.axis_size("z"), -1, hidden)
     total = jnp.sum(exchange(pieces, "z").astype(f32), axis=0).astype(bf16)
     own = exchange(spread(total, FAR), FAR).reshape(-1, part + MARGIN, hidden)
     own = jnp.concatenate([own[:, :part].reshape(block, hidden), own[0, part:]], axis=0)
-    return lax.all_gather(after(own, meanwhile[:16, :EXTRA]), NEAR, axis=0, tiled=True)
-
-
-def scaled_kernel(scale, upper_ref, lower_ref, self_ref, neigh_ref, bias_ref):
-    block = self_ref.shape[0]
-    self_ref[...] = upper_ref[:block, :].astype(f32) * scale
-    neigh_ref[...] = lower_ref[:block, :].astype(f32) * scale
-
-    @pl.when(pl.program_id(1) == 0)
-    def _():
-        bias_ref[...] = upper_ref[block : block + MARGIN, :].astype(f32)[0:1] * scale
+    return lax.all_gather(after(own, meanwhile), NEAR, axis=0, tiled=True)
+
+
+def scaled_kernel(
+    scale,
+    full_any,
+    self_any,
+    neigh_any,
+    bias_ref,
+    full_ref,
+    self_ref,
+    neigh_ref,
+    in_sems,
+    out_sems,
+):
+    near, tall, _ = full_ref.shape
+    half = near // 2
+    block = tall - MARGIN
+    order = [b for pair in zip(range(half), range(half, near)) for b in pair]
+    loads, sends = {}, []
+    for b in order:
+        loads[b] = pltpu.make_async_copy(full_any.at[b], full_ref.at[b], in_sems.at[b])
+        loads[b].start()
+    for b in order:
+        loads[b].wait()
+        target, held = (self_any, self_ref) if b < half else (neigh_any, neigh_ref)
+        here = slice(b % half * block, (b % half + 1) * block)
+        held[here, :] = full_ref[b, :block, :].astype(f32) * scale
+        copy = pltpu.make_async_copy(held.at[here], target.at[here], out_sems.at[b])
+        copy.start()
+        sends.append(copy)
+    bias_ref[...] = full_ref[0, block:, :].astype(f32)[0:1] * scale
+    for copy in sends:
+        copy.wait()
 
 
 def scaled_parts(full, width, scale):
     hidden = full.shape[1]
     near = lax.axis_size(NEAR)
-    tall = full.shape[0] // near
-    half = near // 2
-    block = width // half
-    pieces = 4
-    piece = hidden // pieces
-    grad_spec = pl.BlockSpec((block, piece), lambda c, i: (i, c))
+    full = full.reshape(near, -1, hidden)
+    grad = jax.ShapeDtypeStruct((width, hidden), f32)
+    hbm = pl.BlockSpec(memory_space=pltpu.HBM)
     return pl.pallas_call(
         functools.partial(scaled_kernel, scale),
-        grid=(pieces, half),
-        in_specs=[
-            pl.BlockSpec((tall, piece), lambda c, i: (i, c)),
-            pl.BlockSpec((tall, piece), lambda c, i: (i + half, c)),
-        ],
-        out_specs=[
-            grad_spec,
-            grad_spec,
-            pl.BlockSpec((1, piece), lambda c, i: (0, c)),
-        ],
-        out_shape=[
-            jax.ShapeDtypeStruct((width, hidden), f32),
-            jax.ShapeDtypeStruct((width, hidden), f32),
-            jax.ShapeDtypeStruct((1, hidden), f32),
+        in_specs=[hbm],
+        out_specs=[hbm, hbm, pl.BlockSpec(memory_space=pltpu.VMEM)],
+        out_shape=[grad, grad, jax.ShapeDtypeStruct((1, hidden), f32)],
+        scratch_shapes=[
+            pltpu.VMEM(full.shape, bf16),
+            pltpu.VMEM(grad.shape, f32),
+            pltpu.VMEM(grad.shape, f32),
+            pltpu.SemaphoreType.DMA((near,)),
+            pltpu.SemaphoreType.DMA((near,)),
         ],
         compiler_params=VMEM,
         cost_estimate=cost(full.size, 6 * full.size),
-    )(full, full)
-
-
-def scatter_kernel(turned_any, grad_any, out_ref, turned_ref, grad_ref, sems):
+    )(full)
+
+
+def scatter_kernel(
+    turned_any, grad_any, out_ref, token_ref, turned_ref, grad_ref, sems
+):
     width = out_ref.shape[1]
     copies = []
     for j in range(SPLIT):
@@ -378,6 +395,7 @@
             preferred_element_type=f32,
         )
     out_ref[...] = total.astype(bf16)
+    token_ref[...] = jnp.zeros(token_ref.shape, f32)
 
 
 def scatter_sum(turned, slot_grad):
@@ -386,7 +404,10 @@
     return pl.pallas_call(
         scatter_kernel,
         in_specs=[pl.BlockSpec(memory_space=pltpu.HBM)] * 2,
-        out_shape=jax.ShapeDtypeStruct((rows, width), bf16),
+        out_shape=[
+            jax.ShapeDtypeStruct((rows, width), bf16),
+            jax.ShapeDtypeStruct((8, EXTRA), f32),
+        ],
         scratch_shapes=[
             pltpu.VMEM(turned.shape, bf16),
             pltpu.VMEM(slot_grad.shape, bf16),
@@ -428,9 +449,11 @@
 
     slot_grad = exchange(routed.reshape(sources, s_count, -1), DOM)
     self_grad = contract_last(delta, w_self).astype(bf16)
-    local = scatter_sum(jnp.swapaxes(select, 1, 2), slot_grad.reshape(sources * s_count, -1))
+    local, summed = scatter_sum(
+        jnp.swapaxes(select, 1, 2), slot_grad.reshape(sources * s_count, -1)
+    )
     feat_grads = lax.psum_scatter(local, "rep", scatter_dimension=0, tiled=True)
-    full = reduce_everywhere(terms, slot_grad, feat_grads)
+    full = reduce_everywhere(terms, summed, feat_grads)
     scale = float(seed_count * lax.axis_size(DOM) * replicas) ** (-0.5)
     grad_self, grad_neigh, grad_bias = scaled_parts(full, width, scale)
     return (

time: 288 us -> 279 us (0.969)
  Pallas kernels: 38.8 us -> 32.6 us
    pallas_call x1, Pallas kernels: 10.6 us -> 4.46 us  [scaled_parts(): pl.pallas_call(functools.partial(scaled_kernel, scale), in_specs=[hbm], o...]
where the time goes in v7:
time: 279 us; the launch traced here: 278 us
  waiting for transfers between devices  165 us (59%)
  Pallas kernels  32.6 us (12%)
  blocking collectives  28.6 us (10%)
  starting transfers between devices  20.5 us (7%)
  between operations  13.9 us (5%)
  local copies, waits for them, and re-layouts  10.5 us (4%)
  other arithmetic  3.76 us (1%)
  matrix products  2.95 us (1%)
    all_to_all x2, waiting for transfers between devices, exchange(): return lax.all_to_all(value, axes, split_axis=0, concat_axis=0, tiled=True)  94.4 us
    reduce_scatter x1, waiting for transfers between devices, reduce_everywhere(): lax.psum_scatter(terms.reshape(-1, hidden), NEAR, scatter_dimension=0, ti...  38.3 us
    all_gather x1, waiting for transfers between devices, reduce_everywhere(): return lax.all_gather(after(own, meanwhile), NEAR, axis=0, tiled=True)  32.6 us
    all_to_all x2, blocking collectives, exchange(): return lax.all_to_all(value, axes, split_axis=0, concat_axis=0, tiled=True)  28.6 us
    all_to_all x2, starting transfers between devices, exchange(): return lax.all_to_all(value, axes, split_axis=0, concat_axis=0, tiled=True)  20.1 us
    pallas_call x1, Pallas kernels, select_and_sum(): pl.pallas_call(select_kernel, grid=(steps,), in_specs=[edge_spec, edge_sp...  10.2 us
    pallas_call x1, Pallas kernels, middle(): pl.pallas_call(middle_kernel, in_specs=[hbm, pl.BlockSpec(memory_space=pl...  10 us
    pallas_call x1, Pallas kernels, scatter_sum(): pl.pallas_call(scatter_kernel, in_specs=[pl.BlockSpec(memory_space=pltpu....  7.92 us
  transfers between devices with their start and end apart: 6, of which 4 were waited for; matrix products, arithmetic and copies ran while one was open for 6% of the time, Pallas kernels for 3%

profile of v7, /device:TPU:1, one launch (start us, length us, event | category | flops | bytes accessed | tf_op | source)
XLA Modules:
  0.0 278.2 jit_solution(10710958489705890189)
XLA Ops:
  7.2 0.0 copy-start
  7.2 10.2 %shard_map.136 = (bf16[4,512,1024]{2,1,0:T(8,128)(2,1)}, bf16[512,3200]{1,0:T(8,128)(2,1)}) custom-call(s32[64,64]{1,0:T(8,128)} %bitcast.38, s32[64,64]{1,0:T(8,128)} %bitcast.39, bf16[1024,768]{1,0:T(8,128)(2,1)} %feats_ref.1), custom_call_target="tpu_custom_call" | custom-call | flops 4294967296 | bytes 9043968 | tf_op jit(solution)/shard_map/pallas_call | solution.py:96
  17.4 0.0 copy-start.2
  17.4 0.0 copy-start.3
  17.4 0.0 copy-start.1
  17.4 13.3 %all-to-all-start = ((bf16[64,8,3200]{2,1,0:T(8,128)(2,1)}), bf16[64,8,3200]{2,1,0:T(8,128)(2,1)}, u32[]{:S(2)}, u32[]{:S(2)}) async-start(bf16[64,8,3200]{2,1,0:T(8,128)(2,1)} %bitcast.27), calls=%async_computation | async-start | bytes 6553600 | tf_op jit(solution)/shard_map/all_to_all | solution.py:38
  30.7 0.0 reduce-scatter.6.cloned.1.call-start
  30.8 0.0 copy-done.2
  30.8 0.1 copy.20
  30.9 0.1 eq.15
  31.0 0.7 reshape.82.seeds_ref
  31.7 0.0 copy-done.3
  31.7 0.0 copy-done.1
  31.7 1.2 gather_fusion
  32.9 0.0 copy-start.4
  32.9 0.2 copy.21
  33.1 0.8 fusion.1.self_any
  33.9 1.3 fusion.turned_any
  35.2 0.0 copy-done
  35.2 0.0 copy-done.4
  35.2 1.6 convolution_add_fusion.base_any
  36.8 69.2 %all-to-all-done = bf16[64,8,3200]{2,1,0:T(8,128)(2,1)} async-done(((bf16[64,8,3200]{2,1,0:T(8,128)(2,1)}), bf16[64,8,3200]{2,1,0:T(8,128)(2,1)}, u32[]{:S(2)}, u32[]{:S(2)}) %all-to-all-start) | async-done | bytes 3276832 | tf_op jit(solution)/shard_map/all_to_all | solution.py:38
  106.0 10.0 %shard_map.137 = (bf16[256,1024]{1,0:T(8,128)(2,1)}, bf16[256,1024]{1,0:T(8,128)(2,1)}, bf16[512,3072]{1,0:T(8,128)(2,1)}, bf16[8,208,1024]{2,1,0:T(8,128)(2,1)}) custom-call(bf16[512,3200]{1,0:T(8,128)(2,1)} %bitcast.3.arrived_any, s32[4,1,512]{2,1,0:T(1,128)} %reshape.82.seeds_ref, f32[256,1024]{1,0:T(8,128)} %convolution_add_fusion.base_any, ...), custom_call_target="tpu_custom_call" | custom-call | flops 3221225472 | bytes 13893632 | tf_op jit(solution)/shard_map/pallas_call | solution.py:262
  116.1 0.0 reduce-scatter.6.cloned.1.call-update
  116.1 6.8 %all-to-all-start.1 = ((bf16[64,8,3072]{2,1,0:T(8,128)(2,1)}), bf16[64,8,3072]{2,1,0:T(8,128)(2,1)}, u32[]{:S(2)}, u32[]{:S(2)}) async-start(bf16[64,8,3072]{2,1,0:T(8,128)(2,1)} %bitcast.28), calls=%async_computation.1 | async-start | bytes 6291456 | tf_op jit(solution)/shard_map/all_to_all | solution.py:38
  122.9 0.0 reduce-scatter.8.cloned.1.call-start
  123.0 38.3 %reduce-scatter.6.cloned.1.call-done = bf16[208,1024]{1,0:T(8,128)(2,1)} async-done(((bf16[1664,1024]{1,0:T(8,128)(2,1)}), bf16[208,1024]{1,0:T(8,128)(2,1)}) %reduce-scatter.6.cloned.1.call-update) | async-done | bytes 426000 | tf_op jit(solution)/shard_map/reduce_scatter | solution.py:300
  161.3 0.8 slice.19
  162.0 1.0 slice.18
  163.1 0.8 pad_maximum_fusion
  163.9 0.0 reduce-scatter.8.cloned.1.call-update
  163.9 0.2 reduce-scatter.4.cloned.1.call-start
  164.2 6.3 %copy.23 = bf16[4,512,1024]{1,2,0:T(8,128)(2,1)} copy(bf16[4,512,1024]{2,1,0:T(8,128)(2,1)} %get-tuple-element.20) | data formatting | bytes 8388608 | tf_op jit(solution)/shard_map/pallas_call | solution.py:96
  170.4 25.2 %all-to-all-done.1 = bf16[64,8,3072]{2,1,0:T(8,128)(2,1)} async-done(((bf16[64,8,3072]{2,1,0:T(8,128)(2,1)}), bf16[64,8,3072]{2,1,0:T(8,128)(2,1)}, u32[]{:S(2)}, u32[]{:S(2)}) %all-to-all-start.1) | async-done | bytes 3145760 | tf_op jit(solution)/shard_map/all_to_all | solution.py:38
  195.6 7.9 %shard_map.138 = (bf16[1024,768]{1,0:T(8,128)(2,1)}, f32[8,128]{1,0:T(8,128)}) custom-call(bf16[4,1024,512]{2,1,0:T(8,128)(2,1)} %bitcast.24, bf16[512,3072]{1,0:T(8,128)(2,1)} %bitcast.9.grad_any), custom_call_target="tpu_custom_call" | custom-call | flops 3221225472 | bytes 7340032 | tf_op jit(solution)/shard_map/pallas_call | solution.py:404
  203.5 0.0 reduce-scatter.4.cloned.1.call-update
  203.6 0.0 all-gather.2.cloned.1.call-start
  203.6 0.0 reduce-scatter.8.cloned.1.call-done.value_ref
  203.7 13.0 %all_to_all.20 = bf16[8,8,1024]{2,1,0:T(8,128)(2,1)S(1)} all-to-all(bf16[8,8,1024]{2,1,0:T(8,128)(2,1)} %bitcast.36), channel_id=1, replica_groups=mesh['z'=8,'x'=4,'c'=2,'rep'=4] {'z'}, dimensions={0} | all-to-all | bytes 262144 | tf_op jit(solution)/shard_map/all_to_all | solution.py:38
  216.7 0.1 broadcast_in_dim.30
  216.8 0.0 copy-start.5
  216.8 15.5 %all_to_all.21 = bf16[32,8,1024]{2,1,0:T(8,128)(2,1)S(1)} all-to-all(bf16[32,8,1024]{2,1,0:T(8,128)(2,1)S(1)} %broadcast_in_dim.30), channel_id=1, replica_groups=mesh['z'=8,'x'=4,'c'=2,'rep'=4] {'x','z'}, dimensions={0} | all-to-all | bytes 1048576 | tf_op jit(solution)/shard_map/all_to_all | solution.py:38
  232.4 0.8 pad_maximum_fusion.1.value_ref
  233.2 0.0 reduce-scatter.4.cloned.1.call-done.earlier_ref
  233.2 0.0 all-gather.2.cloned.1.call-update
  233.2 0.0 copy-done.5
  233.2 1.4 convolution_convert_fusion
  234.6 32.6 %all-gather.2.cloned.1.call-done = bf16[1664,1024]{1,0:T(8,128)(2,1)} async-done(((bf16[208,1024]{1,0:T(8,128)(2,1)}), bf16[1664,1024]{1,0:T(8,128)(2,1)}) %all-gather.2.cloned.1.call-update) | async-done | bytes 3407888 | tf_op jit(solution)/shard_map/all_gather | solution.py:313
  267.2 4.5 %shard_map.141 = (f32[768,1024]{1,0:T(8,128)}, f32[768,1024]{1,0:T(8,128)}, f32[1,1024]{1,0:T(1,128)}) custom-call(bf16[8,208,1024]{2,1,0:T(8,128)(2,1)} %bitcast.26), custom_call_target="tpu_custom_call" | custom-call | flops 1703936 | bytes 10223616 | tf_op jit(solution)/shard_map/pallas_call | solution.py:355
  (9 shorter events, 0.1 us)
Async XLA Ops:
  7.2 28.1 %copy-start = (bf16[768,1024]{1,0:T(8,128)(2,1)S(1)}, bf16[768,1024]{1,0:T(8,128)(2,1)}, u32[]{:S(2)}) copy-start(bf16[768,1024]{1,0:T(8,128)(2,1)} %param.14) | copy-start | bytes 4718596
  17.4 13.4 %copy-start.2 = (s32[1,64,32]{1,2,0:T(8,128)S(1)}, s32[1,64,32]{1,2,0:T(8,128)}, u32[]{:S(2)}) copy-start(s32[1,64,32]{1,2,0:T(8,128)} %param.13) | copy-start | bytes 24580
  17.4 14.3 %copy-start.3 = (s32[256]{0:T(256)S(1)}, s32[256]{0:T(256)}, u32[]{:S(2)}) copy-start(s32[256]{0:T(256)} %param.10) | copy-start | bytes 3076
  17.4 14.3 %copy-start.1 = (bf16[1024,768]{1,0:T(8,128)(2,1)S(1)}, bf16[1024,768]{1,0:T(8,128)(2,1)}, u32[]{:S(2)}) copy-start(bf16[1024,768]{1,0:T(8,128)(2,1)} %feats_ref.1) | copy-start | bytes 4718596
  17.4 88.6 %all-to-all-start = ((bf16[64,8,3200]{2,1,0:T(8,128)(2,1)}), bf16[64,8,3200]{2,1,0:T(8,128)(2,1)}, u32[]{:S(2)}, u32[]{:S(2)}) async-start(bf16[64,8,3200]{2,1,0:T(8,128)(2,1)} %bitcast.27), calls=%async_computation | async-start | bytes 6553600 | tf_op jit(solution)/shard_map/all_to_all | solution.py:38
  30.7 130.5 %reduce-scatter.6.cloned.1.call-start = ((), (), s32[]{:S(2)}) async-start(), calls=%async_computation.8 | async-start | bytes 3833856 | tf_op jit(solution)/shard_map/reduce_scatter | solution.py:300
  32.9 2.3 copy-start.4
  116.1 79.5 %all-to-all-start.1 = ((bf16[64,8,3072]{2,1,0:T(8,128)(2,1)}), bf16[64,8,3072]{2,1,0:T(8,128)(2,1)}, u32[]{:S(2)}, u32[]{:S(2)}) async-start(bf16[64,8,3072]{2,1,0:T(8,128)(2,1)} %bitcast.28), calls=%async_computation.1 | async-start | bytes 6291456 | tf_op jit(solution)/shard_map/all_to_all | solution.py:38
  122.9 80.7 %reduce-scatter.8.cloned.1.call-start = ((), (), s32[]{:S(2)}) async-start(), calls=%async_computation.9 | async-start | bytes 655360 | tf_op jit(solution)/shard_map/reduce_scatter | solution.py:306
  163.9 69.2 %reduce-scatter.4.cloned.1.call-start = ((), (), s32[]{:S(2)}) async-start(), calls=%async_computation.7 | async-start | bytes 1966080 | tf_op jit(solution)/shard_map/reduce_scatter | solution.py:455
  203.6 63.6 %all-gather.2.cloned.1.call-start = ((), (), s32[]{:S(2)}) async-start(), calls=%async_computation.10 | async-start | bytes 3833856 | tf_op jit(solution)/shard_map/all_gather | solution.py:313
  216.8 16.4 %copy-start.5 = (bf16[256,1024]{1,0:T(8,128)(2,1)S(1)}, bf16[256,1024]{1,0:T(8,128)(2,1)}, u32[]{:S(2)}) copy-start(bf16[256,1024]{1,0:T(8,128)(2,1)} %get-tuple-element.19) | copy-start | bytes 1572868
Sparse Core Ops, SparseCore 0:
  116.2 45.0 reduce-scatter.5
  164.4 26.2 reduce-scatter.7
  203.7 24.6 reduce-scatter.3
  233.3 33.8 all-gather.1

commit v8 on v7

--- a/solution.py
+++ b/solution.py
@@ -185,12 +185,14 @@
     degree = jnp.maximum(jnp.sum(counts, axis=1, keepdims=True), 1.0)
     degree_ref[...] = jnp.broadcast_to(degree, (seed_count, EXTRA))
     aggregate_ref[...] = (total / degree).astype(bf16)
-    for later in loads[1 + SPLIT :]:
-        later.wait()
+    w_neigh_load, base_load, cotangent_load, turned_load, self_load = loads[1 + SPLIT :]
+    w_neigh_load.wait()
+    base_load.wait()
     base_ref[...] += jnp.dot(
         aggregate_ref[...], w_neigh_ref[...], preferred_element_type=f32
     )
 
+    cotangent_load.wait()
     rows = 16
     slope = (2.0 / np.pi) ** 0.5
 
@@ -217,6 +219,7 @@
         copies.append(copy)
 
     grad = contract_last(neigh_ref[...], w_neigh_ref[...]).astype(bf16)
+    turned_load.wait()
     for j in range(SPLIT):
         routed_ref[:, columns(j)] = jnp.dot(
             turned_ref[j], grad, preferred_element_type=f32
@@ -230,6 +233,7 @@
     first = lax.broadcasted_iota(jnp.int32, (MARGIN, hidden), 0) == 0
     margin = jnp.where(first, column, 0.0).astype(bf16)
     half = near // 2
+    self_load.wait()
     products = (
         jnp.dot(self_ref[...], delta, preferred_element_type=f32),
         contract_first(aggregate_ref[...], delta),
@@ -369,26 +373,10 @@
     )(full)
 
 
-def scatter_kernel(
-    turned_any, grad_any, out_ref, token_ref, turned_ref, grad_ref, sems
-):
+def scatter_kernel(turned_ref, grad_ref, out_ref, token_ref):
     width = out_ref.shape[1]
-    copies = []
-    for j in range(SPLIT):
-        columns = slice(j * width, (j + 1) * width)
-        for k, (source, target) in enumerate(
-            (
-                (turned_any.at[j], turned_ref.at[j]),
-                (grad_any.at[:, columns], grad_ref.at[:, columns]),
-            )
-        ):
-            copy = pltpu.make_async_copy(source, target, sems.at[j, k])
-            copy.start()
-            copies.append(copy)
     total = jnp.zeros(out_ref.shape, f32)
     for j in range(SPLIT):
-        copies[2 * j].wait()
-        copies[2 * j + 1].wait()
         total += jnp.dot(
             turned_ref[j],
             grad_ref[:, j * width : (j + 1) * width],
@@ -403,17 +391,11 @@
     width = slot_grad.shape[1] // SPLIT
     return pl.pallas_call(
         scatter_kernel,
-        in_specs=[pl.BlockSpec(memory_space=pltpu.HBM)] * 2,
         out_shape=[
             jax.ShapeDtypeStruct((rows, width), bf16),
             jax.ShapeDtypeStruct((8, EXTRA), f32),
         ],
-        scratch_shapes=[
-            pltpu.VMEM(turned.shape, bf16),
-            pltpu.VMEM(slot_grad.shape, bf16),
-            pltpu.SemaphoreType.DMA((SPLIT, 2)),
-        ],
-        compiler_params=VMEM,
+        compiler_params=pltpu.CompilerParams(vmem_limit_bytes=32 * 1024 * 1024),
         cost_estimate=cost(
             2 * SPLIT * sent * rows * width, 2 * (turned.size + slot_grad.size)
         ),

time: 279 us -> 280 us (level)
  local copies, waits for them, and re-layouts: 10.5 us -> 13.3 us
  transfers between devices with their start and end apart: 6 -> 6, of which waited for: 4 -> 4; matrix products, arithmetic and copies ran while one was open for 6% -> 6% of each run, Pallas kernels for 3% -> 2%
where the time goes in v8:
time: 280 us
  waiting for transfers between devices  165 us (59%)
  Pallas kernels  31.4 us (11%)
  blocking collectives  28.6 us (10%)
  starting transfers between devices  20.5 us (7%)
  between operations  13.9 us (5%)
  local copies, waits for them, and re-layouts  13.3 us (5%)
  other arithmetic  3.76 us (1%)
  matrix products  2.94 us (1%)
    all_to_all x2, waiting for transfers between devices, exchange(): return lax.all_to_all(value, axes, split_axis=0, concat_axis=0, tiled=True)  94.3 us
    reduce_scatter x1, waiting for transfers between devices, reduce_everywhere(): lax.psum_scatter(terms.reshape(-1, hidden), NEAR, scatter_dimension=0, ti...  38.3 us
    all_gather x1, waiting for transfers between devices, reduce_everywhere(): return lax.all_gather(after(own, meanwhile), NEAR, axis=0, tiled=True)  32.6 us
    all_to_all x2, blocking collectives, exchange(): return lax.all_to_all(value, axes, split_axis=0, concat_axis=0, tiled=True)  28.6 us
    all_to_all x2, starting transfers between devices, exchange(): return lax.all_to_all(value, axes, split_axis=0, concat_axis=0, tiled=True)  20.1 us
    pallas_call x1, Pallas kernels, middle(): pl.pallas_call(middle_kernel, in_specs=[hbm, pl.BlockSpec(memory_space=pl...  10.2 us
    pallas_call x1, Pallas kernels, select_and_sum(): pl.pallas_call(select_kernel, grid=(steps,), in_specs=[edge_spec, edge_sp...  10.2 us
    pallas_call x1, Pallas kernels, scatter_sum(): pl.pallas_call(scatter_kernel, out_shape=[jax.ShapeDtypeStruct((rows, wid...  6.46 us
  transfers between devices with their start and end apart: 6, of which 4 were waited for; matrix products, arithmetic and copies ran while one was open for 6% of the time, Pallas kernels for 2%

profile of v8, /device:TPU:1, one launch (start us, length us, event | category | flops | bytes accessed | tf_op | source)
XLA Modules:
  0.0 279.7 jit_solution(6750090699330348758)
XLA Ops:
  7.2 0.0 copy-start
  7.2 10.2 %shard_map.136 = (bf16[4,512,1024]{2,1,0:T(8,128)(2,1)}, bf16[512,3200]{1,0:T(8,128)(2,1)}) custom-call(s32[64,64]{1,0:T(8,128)} %bitcast.38, s32[64,64]{1,0:T(8,128)} %bitcast.39, bf16[1024,768]{1,0:T(8,128)(2,1)} %feats_ref.1), custom_call_target="tpu_custom_call" | custom-call | flops 4294967296 | bytes 9043968 | tf_op jit(solution)/shard_map/pallas_call | solution.py:96
  17.4 0.0 copy-start.4
  17.4 0.0 copy-start.5
  17.4 0.0 copy-start.3
  17.4 13.3 %all-to-all-start = ((bf16[64,8,3200]{2,1,0:T(8,128)(2,1)}), bf16[64,8,3200]{2,1,0:T(8,128)(2,1)}, u32[]{:S(2)}, u32[]{:S(2)}) async-start(bf16[64,8,3200]{2,1,0:T(8,128)(2,1)} %bitcast.27), calls=%async_computation | async-start | bytes 6553600 | tf_op jit(solution)/shard_map/all_to_all | solution.py:38
  30.7 0.0 reduce-scatter.6.cloned.1.call-start
  30.8 0.0 copy-done.4
  30.8 0.1 copy.20
  30.9 0.1 eq.15
  31.0 0.7 reshape.82.seeds_ref
  31.7 0.0 copy-done.5
  31.7 0.0 copy-done.3
  31.7 1.2 gather_fusion
  32.9 0.0 copy-start.6
  32.9 0.2 copy.21
  33.1 0.8 fusion.1.self_any
  33.9 1.3 fusion.turned_any
  35.2 0.0 copy-done
  35.2 0.0 copy-done.6
  35.2 1.6 convolution_add_fusion.base_any
  36.8 69.2 %all-to-all-done = bf16[64,8,3200]{2,1,0:T(8,128)(2,1)} async-done(((bf16[64,8,3200]{2,1,0:T(8,128)(2,1)}), bf16[64,8,3200]{2,1,0:T(8,128)(2,1)}, u32[]{:S(2)}, u32[]{:S(2)}) %all-to-all-start) | async-done | bytes 3276832 | tf_op jit(solution)/shard_map/all_to_all | solution.py:38
  106.0 10.2 %shard_map.137 = (bf16[256,1024]{1,0:T(8,128)(2,1)}, bf16[256,1024]{1,0:T(8,128)(2,1)}, bf16[512,3072]{1,0:T(8,128)(2,1)}, bf16[8,208,1024]{2,1,0:T(8,128)(2,1)}) custom-call(bf16[512,3200]{1,0:T(8,128)(2,1)} %bitcast.3.arrived_any, s32[4,1,512]{2,1,0:T(1,128)} %reshape.82.seeds_ref, f32[256,1024]{1,0:T(8,128)} %convolution_add_fusion.base_any, ...), custom_call_target="tpu_custom_call" | custom-call | flops 3221225472 | bytes 13893632 | tf_op jit(solution)/shard_map/pallas_call | solution.py:266
  116.2 0.0 reduce-scatter.6.cloned.1.call-update
  116.3 6.8 %all-to-all-start.1 = ((bf16[64,8,3072]{2,1,0:T(8,128)(2,1)}), bf16[64,8,3072]{2,1,0:T(8,128)(2,1)}, u32[]{:S(2)}, u32[]{:S(2)}) async-start(bf16[64,8,3072]{2,1,0:T(8,128)(2,1)} %bitcast.28), calls=%async_computation.1 | async-start | bytes 6291456 | tf_op jit(solution)/shard_map/all_to_all | solution.py:38
  123.1 0.0 reduce-scatter.8.cloned.1.call-start
  123.1 38.3 %reduce-scatter.6.cloned.1.call-done = bf16[208,1024]{1,0:T(8,128)(2,1)} async-done(((bf16[1664,1024]{1,0:T(8,128)(2,1)}), bf16[208,1024]{1,0:T(8,128)(2,1)}) %reduce-scatter.6.cloned.1.call-update) | async-done | bytes 426000 | tf_op jit(solution)/shard_map/reduce_scatter | solution.py:304
  161.5 0.8 slice.19
  162.2 1.0 slice.18
  163.3 0.8 pad_maximum_fusion
  164.1 0.0 reduce-scatter.8.cloned.1.call-update
  164.1 0.2 reduce-scatter.4.cloned.1.call-start
  164.3 6.3 %copy.23 = bf16[4,512,1024]{1,2,0:T(8,128)(2,1)} copy(bf16[4,512,1024]{2,1,0:T(8,128)(2,1)} %get-tuple-element.20) | data formatting | bytes 8388608 | tf_op jit(solution)/shard_map/pallas_call | solution.py:96
  170.6 25.2 %all-to-all-done.1 = bf16[64,8,3072]{2,1,0:T(8,128)(2,1)} async-done(((bf16[64,8,3072]{2,1,0:T(8,128)(2,1)}), bf16[64,8,3072]{2,1,0:T(8,128)(2,1)}, u32[]{:S(2)}, u32[]{:S(2)}) %all-to-all-start.1) | async-done | bytes 3145760 | tf_op jit(solution)/shard_map/all_to_all | solution.py:38
  195.8 0.0 copy-start.1
  195.8 2.2 copy-done.1
  198.0 6.5 %shard_map.138 = (bf16[1024,768]{1,0:T(8,128)(2,1)}, f32[8,128]{1,0:T(8,128)S(1)}) custom-call(bf16[4,1024,512]{2,1,0:T(8,128)(2,1)S(1)} %bitcast.24, bf16[512,3072]{1,0:T(8,128)(2,1)} %bitcast.9.grad_ref), custom_call_target="tpu_custom_call" | custom-call | flops 3221225472 | bytes 7340032 | tf_op jit(solution)/shard_map/pallas_call | solution.py:392
  204.5 0.0 copy-start.2
  204.5 0.6 copy-done.2
  205.0 0.0 reduce-scatter.4.cloned.1.call-update
  205.1 0.0 all-gather.2.cloned.1.call-start
  205.1 0.0 reduce-scatter.8.cloned.1.call-done.value_ref
  205.2 13.0 %all_to_all.20 = bf16[8,8,1024]{2,1,0:T(8,128)(2,1)S(1)} all-to-all(bf16[8,8,1024]{2,1,0:T(8,128)(2,1)} %bitcast.36), channel_id=1, replica_groups=mesh['z'=8,'x'=4,'c'=2,'rep'=4] {'z'}, dimensions={0} | all-to-all | bytes 262144 | tf_op jit(solution)/shard_map/all_to_all | solution.py:38
  218.2 0.1 broadcast_in_dim.30
  218.3 0.0 copy-start.7
  218.3 15.5 %all_to_all.21 = bf16[32,8,1024]{2,1,0:T(8,128)(2,1)S(1)} all-to-all(bf16[32,8,1024]{2,1,0:T(8,128)(2,1)S(1)} %broadcast_in_dim.30), channel_id=1, replica_groups=mesh['z'=8,'x'=4,'c'=2,'rep'=4] {'x','z'}, dimensions={0} | all-to-all | bytes 1048576 | tf_op jit(solution)/shard_map/all_to_all | solution.py:38
  233.9 0.8 pad_maximum_fusion.1.value_ref
  234.7 0.0 reduce-scatter.4.cloned.1.call-done.earlier_ref
  234.7 0.0 all-gather.2.cloned.1.call-update
  234.7 0.0 copy-done.7
  234.7 1.4 convolution_convert_fusion
  236.1 32.6 %all-gather.2.cloned.1.call-done = bf16[1664,1024]{1,0:T(8,128)(2,1)} async-done(((bf16[208,1024]{1,0:T(8,128)(2,1)}), bf16[1664,1024]{1,0:T(8,128)(2,1)}) %all-gather.2.cloned.1.call-update) | async-done | bytes 3407888 | tf_op jit(solution)/shard_map/all_gather | solution.py:317
  268.7 4.5 %shard_map.141 = (f32[768,1024]{1,0:T(8,128)}, f32[768,1024]{1,0:T(8,128)}, f32[1,1024]{1,0:T(1,128)}) custom-call(bf16[8,208,1024]{2,1,0:T(8,128)(2,1)} %bitcast.26), custom_call_target="tpu_custom_call" | custom-call | flops 1703936 | bytes 10223616 | tf_op jit(solution)/shard_map/pallas_call | solution.py:359
  (9 shorter events, 0.1 us)
Async XLA Ops:
  7.2 28.1 %copy-start = (bf16[768,1024]{1,0:T(8,128)(2,1)S(1)}, bf16[768,1024]{1,0:T(8,128)(2,1)}, u32[]{:S(2)}) copy-start(bf16[768,1024]{1,0:T(8,128)(2,1)} %param.14) | copy-start | bytes 4718596
  17.4 13.4 %copy-start.4 = (s32[1,64,32]{1,2,0:T(8,128)S(1)}, s32[1,64,32]{1,2,0:T(8,128)}, u32[]{:S(2)}) copy-start(s32[1,64,32]{1,2,0:T(8,128)} %param.13) | copy-start | bytes 24580
  17.4 14.3 %copy-start.5 = (s32[256]{0:T(256)S(1)}, s32[256]{0:T(256)}, u32[]{:S(2)}) copy-start(s32[256]{0:T(256)} %param.10) | copy-start | bytes 3076
  17.4 14.3 %copy-start.3 = (bf16[1024,768]{1,0:T(8,128)(2,1)S(1)}, bf16[1024,768]{1,0:T(8,128)(2,1)}, u32[]{:S(2)}) copy-start(bf16[1024,768]{1,0:T(8,128)(2,1)} %feats_ref.1) | copy-start | bytes 4718596
  17.4 88.6 %all-to-all-start = ((bf16[64,8,3200]{2,1,0:T(8,128)(2,1)}), bf16[64,8,3200]{2,1,0:T(8,128)(2,1)}, u32[]{:S(2)}, u32[]{:S(2)}) async-start(bf16[64,8,3200]{2,1,0:T(8,128)(2,1)} %bitcast.27), calls=%async_computation | async-start | bytes 6553600 | tf_op jit(solution)/shard_map/all_to_all | solution.py:38
  30.7 130.7 %reduce-scatter.6.cloned.1.call-start = ((), (), s32[]{:S(2)}) async-start(), calls=%async_computation.8 | async-start | bytes 3833856 | tf_op jit(solution)/shard_map/reduce_scatter | solution.py:304
  32.9 2.3 copy-start.6
  116.3 79.5 %all-to-all-start.1 = ((bf16[64,8,3072]{2,1,0:T(8,128)(2,1)}), bf16[64,8,3072]{2,1,0:T(8,128)(2,1)}, u32[]{:S(2)}, u32[]{:S(2)}) async-start(bf16[64,8,3072]{2,1,0:T(8,128)(2,1)} %bitcast.28), calls=%async_computation.1 | async-start | bytes 6291456 | tf_op jit(solution)/shard_map/all_to_all | solution.py:38
  123.1 82.0 %reduce-scatter.8.cloned.1.call-start = ((), (), s32[]{:S(2)}) async-start(), calls=%async_computation.9 | async-start | bytes 655360 | tf_op jit(solution)/shard_map/reduce_scatter | solution.py:310
  164.1 70.5 %reduce-scatter.4.cloned.1.call-start = ((), (), s32[]{:S(2)}) async-start(), calls=%async_computation.7 | async-start | bytes 1966080 | tf_op jit(solution)/shard_map/reduce_scatter | solution.py:437
  195.8 2.2 copy-start.1
  204.5 0.6 copy-start.2
  205.1 63.6 %all-gather.2.cloned.1.call-start = ((), (), s32[]{:S(2)}) async-start(), calls=%async_computation.10 | async-start | bytes 3833856 | tf_op jit(solution)/shard_map/all_gather | solution.py:317
  218.3 16.4 %copy-start.7 = (bf16[256,1024]{1,0:T(8,128)(2,1)S(1)}, bf16[256,1024]{1,0:T(8,128)(2,1)}, u32[]{:S(2)}) copy-start(bf16[256,1024]{1,0:T(8,128)(2,1)} %get-tuple-element.19) | copy-start | bytes 1572868
Sparse Core Ops, SparseCore 0:
  116.4 45.0 reduce-scatter.5
  164.6 26.0 reduce-scatter.7
  205.2 24.6 reduce-scatter.3
  234.8 33.8 all-gather.1

commit v9 on v7

--- a/solution.py
+++ b/solution.py
@@ -10,7 +10,6 @@
 
 DOM = ("z", "x", "c")
 NEAR = ("c", "rep")
-FAR = ("x", "z")
 bf16 = jnp.bfloat16
 f32 = jnp.float32
 
@@ -46,7 +45,15 @@
     return pl.CostEstimate(flops=flops, bytes_accessed=bytes_accessed, transcendentals=0)
 
 
-def select_kernel(rows_ref, slots_ref, feats_ref, select_ref, partial_ref):
+def select_kernel(
+    rows_ref, slots_ref, feats_any, select_ref, partial_ref, feats_ref, feats_sem
+):
+    feats_load = pltpu.make_async_copy(feats_any, feats_ref, feats_sem)
+
+    @pl.when(pl.program_id(0) == 0)
+    def _():
+        feats_load.start()
+
     row_count, width = feats_ref.shape
     dests, entry_cap = rows_ref.shape
     entries = GROUP * entry_cap
@@ -78,6 +85,10 @@
             select_ref[j, here, :] = chosen[j * part : (j + 1) * part]
             tail = jnp.where(lanes == j, count[j * part : (j + 1) * part], tail)
         partial_ref[here, SPLIT * width :] = tail.astype(bf16)
+    @pl.when(pl.program_id(0) == 0)
+    def _():
+        feats_load.wait()
+
     height = STEP * part
     chosen = select_ref[...].reshape(SPLIT * height, row_count)
     sums = jnp.dot(chosen, feats_ref[...], preferred_element_type=f32).astype(bf16)
@@ -99,7 +110,7 @@
         in_specs=[
             edge_spec,
             edge_spec,
-            pl.BlockSpec((row_count, width), lambda i: (0, 0)),
+            pl.BlockSpec(memory_space=pltpu.HBM),
         ],
         out_specs=[
             pl.BlockSpec((SPLIT, sent // steps, row_count), lambda i: (0, i, 0)),
@@ -108,6 +119,10 @@
         out_shape=[
             jax.ShapeDtypeStruct((SPLIT, sent, row_count), bf16),
             jax.ShapeDtypeStruct((sent, wide), bf16),
+        ],
+        scratch_shapes=[
+            pltpu.VMEM((row_count, width), bf16),
+            pltpu.SemaphoreType.DMA,
         ],
         compiler_params=VMEM,
         cost_estimate=cost(
@@ -216,6 +231,8 @@
         copy.start()
         copies.append(copy)
 
+    send(hidden_ref, hidden_any)
+    send(delta_ref, delta_any)
     grad = contract_last(neigh_ref[...], w_neigh_ref[...]).astype(bf16)
     for j in range(SPLIT):
         routed_ref[:, columns(j)] = jnp.dot(
@@ -223,8 +240,6 @@
         ).astype(bf16)
         send(routed_ref.at[:, columns(j)], routed_any.at[:, columns(j)])
 
-    send(hidden_ref, hidden_any)
-    send(delta_ref, delta_any)
     delta = delta_ref[...]
     column = jnp.sum(delta.astype(f32), axis=0, keepdims=True)
     first = lax.broadcasted_iota(jnp.int32, (MARGIN, hidden), 0) == 0
@@ -296,20 +311,22 @@
 def reduce_everywhere(terms, earlier, meanwhile):
     _, tall, hidden = terms.shape
     block = tall - MARGIN
-    part = block // lax.axis_size("x")
+    height = lax.axis_size("z")
+    part = block // height
     summed = lax.psum_scatter(
         terms.reshape(-1, hidden), NEAR, scatter_dimension=0, tiled=True
     )
-    parts = summed[:block].reshape(-1, part, hidden)
-    margin = jnp.broadcast_to(summed[None, block:], (block // part, MARGIN, hidden))
+    parts = summed[:block].reshape(height, part, hidden)
+    margin = jnp.broadcast_to(summed[None, block : block + 8], (height, 8, hidden))
     parts = jnp.concatenate([parts, margin], axis=1)
     line = lax.psum_scatter(
-        parts.reshape(-1, hidden), "x", scatter_dimension=0, tiled=True
-    )
-    pieces = after(line, earlier).reshape(lax.axis_size("z"), -1, hidden)
-    total = jnp.sum(exchange(pieces, "z").astype(f32), axis=0).astype(bf16)
-    own = exchange(spread(total, FAR), FAR).reshape(-1, part + MARGIN, hidden)
-    own = jnp.concatenate([own[:, :part].reshape(block, hidden), own[0, part:]], axis=0)
+        parts.reshape(-1, hidden), "z", scatter_dimension=0, tiled=True
+    )
+    lines = exchange(spread(after(line, earlier), "x"), "x")
+    total = jnp.sum(lines.astype(f32), axis=0).astype(bf16)
+    own = exchange(spread(total, "z"), "z")
+    margin = jnp.concatenate([own[0, part:]] * (MARGIN // 8), axis=0)
+    own = jnp.concatenate([own[:, :part].reshape(block, hidden), margin], axis=0)
     return lax.all_gather(after(own, meanwhile), NEAR, axis=0, tiled=True)
 
 

time: 279 us -> 283 us (1.014)
  waiting for transfers between devices: 165 us -> 171 us
    all_to_all x2, waiting for transfers between devices: 94.4 us -> 97.4 us  [exchange(): return lax.all_to_all(value, axes, split_axis=0, concat_axis=0, tiled=True)]
  transfers between devices with their start and end apart: 6 -> 6, of which waited for: 4 -> 5; matrix products, arithmetic and copies ran while one was open for 6% -> 6% of each run, Pallas kernels for 3% -> 3%
where the time goes in v9:
time: 283 us; the launch traced here: 282 us
  waiting for transfers between devices  171 us (60%)
  Pallas kernels  32.5 us (11%)
  blocking collectives  26.4 us (9%)
  starting transfers between devices  20.5 us (7%)
  between operations  14 us (5%)
  local copies, waits for them, and re-layouts  11.3 us (4%)
  other arithmetic  3.78 us (1%)
  matrix products  2.95 us (1%)
    all_to_all x2, waiting for transfers between devices, exchange(): return lax.all_to_all(value, axes, split_axis=0, concat_axis=0, tiled=True)  97.4 us
    reduce_scatter x1, waiting for transfers between devices, reduce_everywhere(): lax.psum_scatter(terms.reshape(-1, hidden), NEAR, scatter_dimension=0, ti...  38.3 us
    all_gather x1, waiting for transfers between devices, reduce_everywhere(): return lax.all_gather(after(own, meanwhile), NEAR, axis=0, tiled=True)  33.6 us
    all_to_all x2, blocking collectives, exchange(): return lax.all_to_all(value, axes, split_axis=0, concat_axis=0, tiled=True)  26.4 us
    all_to_all x2, starting transfers between devices, exchange(): return lax.all_to_all(value, axes, split_axis=0, concat_axis=0, tiled=True)  20.1 us
    pallas_call x1, Pallas kernels, select_and_sum(): pl.pallas_call(select_kernel, grid=(steps,), in_specs=[edge_spec, edge_sp...  10.3 us
    pallas_call x1, Pallas kernels, middle(): pl.pallas_call(middle_kernel, in_specs=[hbm, pl.BlockSpec(memory_space=pl...  9.79 us
    pallas_call x1, Pallas kernels, scatter_sum(): pl.pallas_call(scatter_kernel, in_specs=[pl.BlockSpec(memory_space=pltpu....  7.93 us
  transfers between devices with their start and end apart: 6, of which 5 were waited for; matrix products, arithmetic and copies ran while one was open for 6% of the time, Pallas kernels for 3%

profile of v9, /device:TPU:1, one launch (start us, length us, event | category | flops | bytes accessed | tf_op | source)
XLA Modules:
  0.0 282.1 jit_solution(1470406013960878614)
XLA Ops:
  7.2 0.0 copy-start
  7.2 10.3 %shard_map.136 = (bf16[4,512,1024]{2,1,0:T(8,128)(2,1)}, bf16[512,3200]{1,0:T(8,128)(2,1)}) custom-call(s32[64,64]{1,0:T(8,128)} %bitcast.33, s32[64,64]{1,0:T(8,128)} %bitcast.34, bf16[1024,768]{1,0:T(8,128)(2,1)} %feats_any.1), custom_call_target="tpu_custom_call" | custom-call | flops 4294967296 | bytes 9043968 | tf_op jit(solution)/shard_map/pallas_call | solution.py:107
  17.5 0.0 copy-start.2
  17.5 0.0 copy-start.3
  17.5 0.0 copy-start.1
  17.6 13.3 %all-to-all-start = ((bf16[64,8,3200]{2,1,0:T(8,128)(2,1)}), bf16[64,8,3200]{2,1,0:T(8,128)(2,1)}, u32[]{:S(2)}, u32[]{:S(2)}) async-start(bf16[64,8,3200]{2,1,0:T(8,128)(2,1)} %bitcast.25), calls=%async_computation | async-start | bytes 6553600 | tf_op jit(solution)/shard_map/all_to_all | solution.py:37
  30.9 0.0 reduce-scatter.6.cloned.1.call-start
  30.9 0.0 copy-done.2
  30.9 0.1 copy.24
  31.0 0.1 eq.15
  31.1 0.7 reshape.75.seeds_ref
  31.9 0.0 copy-done.3
  31.9 0.0 copy-done.1
  31.9 1.2 gather_fusion
  33.1 0.0 copy-start.4
  33.1 0.2 copy.25
  33.3 0.8 fusion.1.self_any
  34.1 1.3 fusion.turned_any
  35.4 0.0 copy-done
  35.4 0.0 copy-done.4
  35.4 1.6 convolution_add_fusion.base_any
  37.0 69.2 %all-to-all-done = bf16[64,8,3200]{2,1,0:T(8,128)(2,1)} async-done(((bf16[64,8,3200]{2,1,0:T(8,128)(2,1)}), bf16[64,8,3200]{2,1,0:T(8,128)(2,1)}, u32[]{:S(2)}, u32[]{:S(2)}) %all-to-all-start) | async-done | bytes 3276832 | tf_op jit(solution)/shard_map/all_to_all | solution.py:37
  106.1 9.8 %shard_map.137 = (bf16[256,1024]{1,0:T(8,128)(2,1)}, bf16[256,1024]{1,0:T(8,128)(2,1)}, bf16[512,3072]{1,0:T(8,128)(2,1)}, bf16[8,208,1024]{2,1,0:T(8,128)(2,1)}) custom-call(bf16[512,3200]{1,0:T(8,128)(2,1)} %bitcast.3.arrived_any, s32[4,1,512]{2,1,0:T(1,128)} %reshape.75.seeds_ref, f32[256,1024]{1,0:T(8,128)} %convolution_add_fusion.base_any, ...), custom_call_target="tpu_custom_call" | custom-call | flops 3221225472 | bytes 13893632 | tf_op jit(solution)/shard_map/pallas_call | solution.py:277
  115.9 0.0 reduce-scatter.6.cloned.1.call-update
  116.0 6.8 %all-to-all-start.1 = ((bf16[64,8,3072]{2,1,0:T(8,128)(2,1)}), bf16[64,8,3072]{2,1,0:T(8,128)(2,1)}, u32[]{:S(2)}, u32[]{:S(2)}) async-start(bf16[64,8,3072]{2,1,0:T(8,128)(2,1)} %bitcast.26), calls=%async_computation.1 | async-start | bytes 6291456 | tf_op jit(solution)/shard_map/all_to_all | solution.py:37
  122.8 0.0 reduce-scatter.8.cloned.1.call-start
  122.8 38.3 %reduce-scatter.6.cloned.1.call-done = bf16[208,1024]{1,0:T(8,128)(2,1)} async-done(((bf16[1664,1024]{1,0:T(8,128)(2,1)}), bf16[208,1024]{1,0:T(8,128)(2,1)}) %reduce-scatter.6.cloned.1.call-update) | async-done | bytes 426000 | tf_op jit(solution)/shard_map/reduce_scatter | solution.py:316
  161.1 0.7 slice.19
  161.9 1.0 slice.18
  162.9 0.8 pad_maximum_fusion
  163.7 0.0 reduce-scatter.8.cloned.1.call-update
  163.8 0.2 reduce-scatter.4.cloned.1.call-start
  164.0 6.3 %copy.27 = bf16[4,512,1024]{1,2,0:T(8,128)(2,1)} copy(bf16[4,512,1024]{2,1,0:T(8,128)(2,1)} %get-tuple-element.20) | data formatting | bytes 8388608 | tf_op jit(solution)/shard_map/pallas_call | solution.py:107
  170.3 28.2 %all-to-all-done.1 = bf16[64,8,3072]{2,1,0:T(8,128)(2,1)} async-done(((bf16[64,8,3072]{2,1,0:T(8,128)(2,1)}), bf16[64,8,3072]{2,1,0:T(8,128)(2,1)}, u32[]{:S(2)}, u32[]{:S(2)}) %all-to-all-start.1) | async-done | bytes 3145760 | tf_op jit(solution)/shard_map/all_to_all | solution.py:37
  198.5 7.9 %shard_map.138 = (bf16[1024,768]{1,0:T(8,128)(2,1)}, f32[8,128]{1,0:T(8,128)}) custom-call(bf16[4,1024,512]{2,1,0:T(8,128)(2,1)} %bitcast.22, bf16[512,3072]{1,0:T(8,128)(2,1)} %bitcast.9.grad_any), custom_call_target="tpu_custom_call" | custom-call | flops 3221225472 | bytes 7340032 | tf_op jit(solution)/shard_map/pallas_call | solution.py:421
  206.4 0.0 reduce-scatter.4.cloned.1.call-update
  206.4 0.0 all-gather.2.cloned.1.call-start
  206.5 0.0 reduce-scatter.8.cloned.1.call-done.value_ref
  206.5 0.9 broadcast_in_dim.36
  207.4 9.3 %all_to_all.20 = bf16[4,32,1024]{2,1,0:T(8,128)(2,1)S(1)} all-to-all(bf16[4,32,1024]{2,1,0:T(8,128)(2,1)S(1)} %broadcast_in_dim.36), channel_id=1, replica_groups=mesh['z'=8,'x'=4,'c'=2,'rep'=4] {'x'}, dimensions={0} | all-to-all | bytes 524288 | tf_op jit(solution)/shard_map/all_to_all | solution.py:37
  216.7 0.1 broadcast_in_dim.37
  216.8 0.0 copy-start.5
  216.8 17.1 %all_to_all.21 = bf16[8,32,1024]{2,1,0:T(8,128)(2,1)S(1)} all-to-all(bf16[8,32,1024]{2,1,0:T(8,128)(2,1)S(1)} %broadcast_in_dim.37), channel_id=1, replica_groups=mesh['z'=8,'x'=4,'c'=2,'rep'=4] {'z'}, dimensions={0} | all-to-all | bytes 1048576 | tf_op jit(solution)/shard_map/all_to_all | solution.py:37
  233.9 0.8 pad_maximum_fusion.1.value_ref
  234.7 1.4 reduce-scatter.4.cloned.1.call-done.earlier_ref
  236.1 0.0 all-gather.2.cloned.1.call-update
  236.1 0.0 copy-done.5
  236.1 1.4 convolution_convert_fusion
  237.5 33.6 %all-gather.2.cloned.1.call-done = bf16[1664,1024]{1,0:T(8,128)(2,1)} async-done(((bf16[208,1024]{1,0:T(8,128)(2,1)}), bf16[1664,1024]{1,0:T(8,128)(2,1)}) %all-gather.2.cloned.1.call-update) | async-done | bytes 3407888 | tf_op jit(solution)/shard_map/all_gather | solution.py:330
  271.1 4.5 %shard_map.141 = (f32[768,1024]{1,0:T(8,128)}, f32[768,1024]{1,0:T(8,128)}, f32[1,1024]{1,0:T(1,128)}) custom-call(bf16[8,208,1024]{2,1,0:T(8,128)(2,1)} %bitcast.24), custom_call_target="tpu_custom_call" | custom-call | flops 1703936 | bytes 10223616 | tf_op jit(solution)/shard_map/pallas_call | solution.py:372
  (9 shorter events, 0.1 us)
Async XLA Ops:
  7.2 28.2 %copy-start = (bf16[768,1024]{1,0:T(8,128)(2,1)S(1)}, bf16[768,1024]{1,0:T(8,128)(2,1)}, u32[]{:S(2)}) copy-start(bf16[768,1024]{1,0:T(8,128)(2,1)} %param.14) | copy-start | bytes 4718596
  17.5 13.4 %copy-start.2 = (s32[1,64,32]{1,2,0:T(8,128)S(1)}, s32[1,64,32]{1,2,0:T(8,128)}, u32[]{:S(2)}) copy-start(s32[1,64,32]{1,2,0:T(8,128)} %param.13) | copy-start | bytes 24580
  17.5 14.3 %copy-start.3 = (s32[256]{0:T(256)S(1)}, s32[256]{0:T(256)}, u32[]{:S(2)}) copy-start(s32[256]{0:T(256)} %param.10) | copy-start | bytes 3076
  17.5 14.3 %copy-start.1 = (bf16[1024,768]{1,0:T(8,128)(2,1)S(1)}, bf16[1024,768]{1,0:T(8,128)(2,1)}, u32[]{:S(2)}) copy-start(bf16[1024,768]{1,0:T(8,128)(2,1)} %feats_any.1) | copy-start | bytes 4718596
  17.6 88.6 %all-to-all-start = ((bf16[64,8,3200]{2,1,0:T(8,128)(2,1)}), bf16[64,8,3200]{2,1,0:T(8,128)(2,1)}, u32[]{:S(2)}, u32[]{:S(2)}) async-start(bf16[64,8,3200]{2,1,0:T(8,128)(2,1)} %bitcast.25), calls=%async_computation | async-start | bytes 6553600 | tf_op jit(solution)/shard_map/all_to_all | solution.py:37
  30.9 130.3 %reduce-scatter.6.cloned.1.call-start = ((), (), s32[]{:S(2)}) async-start(), calls=%async_computation.8 | async-start | bytes 3833856 | tf_op jit(solution)/shard_map/reduce_scatter | solution.py:316
  33.1 2.3 copy-start.4
  116.0 82.5 %all-to-all-start.1 = ((bf16[64,8,3072]{2,1,0:T(8,128)(2,1)}), bf16[64,8,3072]{2,1,0:T(8,128)(2,1)}, u32[]{:S(2)}, u32[]{:S(2)}) async-start(bf16[64,8,3072]{2,1,0:T(8,128)(2,1)} %bitcast.26), calls=%async_computation.1 | async-start | bytes 6291456 | tf_op jit(solution)/shard_map/all_to_all | solution.py:37
  122.8 83.7 %reduce-scatter.8.cloned.1.call-start = ((), (), s32[]{:S(2)}) async-start(), calls=%async_computation.9 | async-start | bytes 589824 | tf_op jit(solution)/shard_map/reduce_scatter | solution.py:322
  163.8 72.3 %reduce-scatter.4.cloned.1.call-start = ((), (), s32[]{:S(2)}) async-start(), calls=%async_computation.7 | async-start | bytes 1966080 | tf_op jit(solution)/shard_map/reduce_scatter | solution.py:472
  206.4 64.6 %all-gather.2.cloned.1.call-start = ((), (), s32[]{:S(2)}) async-start(), calls=%async_computation.10 | async-start | bytes 3833856 | tf_op jit(solution)/shard_map/all_gather | solution.py:330
  216.8 19.4 %copy-start.5 = (bf16[256,1024]{1,0:T(8,128)(2,1)S(1)}, bf16[256,1024]{1,0:T(8,128)(2,1)}, u32[]{:S(2)}) copy-start(bf16[256,1024]{1,0:T(8,128)(2,1)} %get-tuple-element.19) | copy-start | bytes 1572868
Sparse Core Ops, SparseCore 0:
  116.1 45.0 reduce-scatter.5
  164.2 37.6 reduce-scatter.7
  206.6 29.5 reduce-scatter.3
  238.5 32.4 all-gather.1

commit v10 on v8

--- a/solution.py
+++ b/solution.py
@@ -165,11 +165,6 @@
 
     for j in (SPLIT, *range(SPLIT)):
         load(arrived_any.at[:, columns(j)], arrived_ref.at[:, columns(j)])
-    load(w_neigh_any, w_neigh_ref)
-    load(base_any, base_ref)
-    load(cotangent_any, cotangent_ref)
-    load(turned_any, turned_ref)
-    load(self_any, self_ref)
 
     total = jnp.zeros((seed_count, width), f32)
     counts = jnp.zeros((seed_count, EXTRA), f32)
@@ -177,6 +172,13 @@
     for j in range(SPLIT):
         route = jnp.where(ids == seeds_ref[j], 1.0, 0.0).astype(bf16)
         loads[1 + j].wait()
+        if j == 1:
+            load(w_neigh_any, w_neigh_ref)
+            load(base_any, base_ref)
+        if j == SPLIT - 1:
+            load(cotangent_any, cotangent_ref)
+            load(turned_any, turned_ref)
+            load(self_any, self_ref)
         total += jnp.dot(route, arrived_ref[:, columns(j)], preferred_element_type=f32)
         found = jnp.dot(
             route, arrived_ref[:, columns(SPLIT)], preferred_element_type=f32
@@ -218,6 +220,8 @@
         copy.start()
         copies.append(copy)
 
+    send(hidden_ref, hidden_any)
+    send(delta_ref, delta_any)
     grad = contract_last(neigh_ref[...], w_neigh_ref[...]).astype(bf16)
     turned_load.wait()
     for j in range(SPLIT):
@@ -226,14 +230,12 @@
         ).astype(bf16)
         send(routed_ref.at[:, columns(j)], routed_any.at[:, columns(j)])
 
-    send(hidden_ref, hidden_any)
-    send(delta_ref, delta_any)
+    self_load.wait()
     delta = delta_ref[...]
     column = jnp.sum(delta.astype(f32), axis=0, keepdims=True)
     first = lax.broadcasted_iota(jnp.int32, (MARGIN, hidden), 0) == 0
     margin = jnp.where(first, column, 0.0).astype(bf16)
     half = near // 2
-    self_load.wait()
     products = (
         jnp.dot(self_ref[...], delta, preferred_element_type=f32),
         contract_first(aggregate_ref[...], delta),
@@ -389,13 +391,24 @@
 def scatter_sum(turned, slot_grad):
     _, rows, sent = turned.shape
     width = slot_grad.shape[1] // SPLIT
+    steps = 2
+    tall = rows // steps
     return pl.pallas_call(
         scatter_kernel,
+        grid=(steps,),
+        in_specs=[
+            pl.BlockSpec((SPLIT, tall, sent), lambda i: (0, i, 0)),
+            pl.BlockSpec(slot_grad.shape, lambda i: (0, 0)),
+        ],
+        out_specs=[
+            pl.BlockSpec((tall, width), lambda i: (i, 0)),
+            pl.BlockSpec((8, EXTRA), lambda i: (0, 0)),
+        ],
         out_shape=[
             jax.ShapeDtypeStruct((rows, width), bf16),
             jax.ShapeDtypeStruct((8, EXTRA), f32),
         ],
-        compiler_params=pltpu.CompilerParams(vmem_limit_bytes=32 * 1024 * 1024),
+        compiler_params=VMEM,
         cost_estimate=cost(
             2 * SPLIT * sent * rows * width, 2 * (turned.size + slot_grad.size)
         ),

time: 280 us -> 278 us (level)
  local copies, waits for them, and re-layouts: 13.3 us -> 10.5 us
  transfers between devices with their start and end apart: 6 -> 6, of which waited for: 4 -> 4; matrix products, arithmetic and copies ran while one was open for 6% -> 6% of each run, Pallas kernels for 2% -> 3%
where the time goes in v10:
time: 278 us
  waiting for transfers between devices  165 us (59%)
  Pallas kernels  32 us (12%)
  blocking collectives  28.7 us (10%)
  starting transfers between devices  20.5 us (7%)
  between operations  13.9 us (5%)
  local copies, waits for them, and re-layouts  10.5 us (4%)
  other arithmetic  3.76 us (1%)
  matrix products  2.95 us (1%)
    all_to_all x2, waiting for transfers between devices, exchange(): return lax.all_to_all(value, axes, split_axis=0, concat_axis=0, tiled=True)  94.4 us
    reduce_scatter x1, waiting for transfers between devices, reduce_everywhere(): lax.psum_scatter(terms.reshape(-1, hidden), NEAR, scatter_dimension=0, ti...  38.3 us
    all_gather x1, waiting for transfers between devices, reduce_everywhere(): return lax.all_gather(after(own, meanwhile), NEAR, axis=0, tiled=True)  32.5 us
    all_to_all x2, blocking collectives, exchange(): return lax.all_to_all(value, axes, split_axis=0, concat_axis=0, tiled=True)  28.7 us
    all_to_all x2, starting transfers between devices, exchange(): return lax.all_to_all(value, axes, split_axis=0, concat_axis=0, tiled=True)  20.1 us
    pallas_call x1, Pallas kernels, middle(): pl.pallas_call(middle_kernel, in_specs=[hbm, pl.BlockSpec(memory_space=pl...  10.3 us
    pallas_call x1, Pallas kernels, select_and_sum(): pl.pallas_call(select_kernel, grid=(steps,), in_specs=[edge_spec, edge_sp...  10.2 us
    pallas_call x1, Pallas kernels, scatter_sum(): pl.pallas_call(scatter_kernel, grid=(steps,), in_specs=[pl.BlockSpec((SPL...  7.03 us
  transfers between devices with their start and end apart: 6, of which 4 were waited for; matrix products, arithmetic and copies ran while one was open for 6% of the time, Pallas kernels for 3%

profile of v10, /device:TPU:1, one launch (start us, length us, event | category | flops | bytes accessed | tf_op | source)
XLA Modules:
  0.0 277.6 jit_solution(14927740227221007184)
XLA Ops:
  7.2 0.0 copy-start
  7.2 10.2 %shard_map.136 = (bf16[4,512,1024]{2,1,0:T(8,128)(2,1)}, bf16[512,3200]{1,0:T(8,128)(2,1)}) custom-call(s32[64,64]{1,0:T(8,128)} %bitcast.38, s32[64,64]{1,0:T(8,128)} %bitcast.39, bf16[1024,768]{1,0:T(8,128)(2,1)} %feats_ref.1), custom_call_target="tpu_custom_call" | custom-call | flops 4294967296 | bytes 9043968 | tf_op jit(solution)/shard_map/pallas_call | solution.py:96
  17.4 0.0 copy-start.2
  17.4 0.0 copy-start.3
  17.4 0.0 copy-start.1
  17.4 13.3 %all-to-all-start = ((bf16[64,8,3200]{2,1,0:T(8,128)(2,1)}), bf16[64,8,3200]{2,1,0:T(8,128)(2,1)}, u32[]{:S(2)}, u32[]{:S(2)}) async-start(bf16[64,8,3200]{2,1,0:T(8,128)(2,1)} %bitcast.27), calls=%async_computation | async-start | bytes 6553600 | tf_op jit(solution)/shard_map/all_to_all | solution.py:38
  30.7 0.0 reduce-scatter.6.cloned.1.call-start
  30.8 0.0 copy-done.2
  30.8 0.1 copy.20
  30.9 0.1 eq.15
  31.0 0.7 reshape.82.seeds_ref
  31.7 0.0 copy-done.3
  31.7 0.0 copy-done.1
  31.7 1.2 gather_fusion
  32.9 0.0 copy-start.4
  32.9 0.2 copy.21
  33.1 0.8 fusion.1.self_any
  33.9 1.3 fusion.turned_any
  35.2 0.0 copy-done
  35.2 0.0 copy-done.4
  35.2 1.6 convolution_add_fusion.base_any
  36.8 69.2 %all-to-all-done = bf16[64,8,3200]{2,1,0:T(8,128)(2,1)} async-done(((bf16[64,8,3200]{2,1,0:T(8,128)(2,1)}), bf16[64,8,3200]{2,1,0:T(8,128)(2,1)}, u32[]{:S(2)}, u32[]{:S(2)}) %all-to-all-start) | async-done | bytes 3276832 | tf_op jit(solution)/shard_map/all_to_all | solution.py:38
  106.0 10.3 %shard_map.137 = (bf16[256,1024]{1,0:T(8,128)(2,1)}, bf16[256,1024]{1,0:T(8,128)(2,1)}, bf16[512,3072]{1,0:T(8,128)(2,1)}, bf16[8,208,1024]{2,1,0:T(8,128)(2,1)}) custom-call(bf16[512,3200]{1,0:T(8,128)(2,1)} %bitcast.3.arrived_any, s32[4,1,512]{2,1,0:T(1,128)} %reshape.82.seeds_ref, f32[256,1024]{1,0:T(8,128)} %convolution_add_fusion.base_any, ...), custom_call_target="tpu_custom_call" | custom-call | flops 3221225472 | bytes 13893632 | tf_op jit(solution)/shard_map/pallas_call | solution.py:268
  116.3 0.0 reduce-scatter.6.cloned.1.call-update
  116.3 6.8 %all-to-all-start.1 = ((bf16[64,8,3072]{2,1,0:T(8,128)(2,1)}), bf16[64,8,3072]{2,1,0:T(8,128)(2,1)}, u32[]{:S(2)}, u32[]{:S(2)}) async-start(bf16[64,8,3072]{2,1,0:T(8,128)(2,1)} %bitcast.28), calls=%async_computation.1 | async-start | bytes 6291456 | tf_op jit(solution)/shard_map/all_to_all | solution.py:38
  123.2 0.0 reduce-scatter.8.cloned.1.call-start
  123.2 38.3 %reduce-scatter.6.cloned.1.call-done = bf16[208,1024]{1,0:T(8,128)(2,1)} async-done(((bf16[1664,1024]{1,0:T(8,128)(2,1)}), bf16[208,1024]{1,0:T(8,128)(2,1)}) %reduce-scatter.6.cloned.1.call-update) | async-done | bytes 426000 | tf_op jit(solution)/shard_map/reduce_scatter | solution.py:306
  161.5 0.8 slice.19
  162.3 1.0 slice.18
  163.3 0.8 pad_maximum_fusion
  164.2 0.0 reduce-scatter.8.cloned.1.call-update
  164.2 0.2 reduce-scatter.4.cloned.1.call-start
  164.4 6.3 %copy.23 = bf16[4,512,1024]{1,2,0:T(8,128)(2,1)} copy(bf16[4,512,1024]{2,1,0:T(8,128)(2,1)} %get-tuple-element.20) | data formatting | bytes 8388608 | tf_op jit(solution)/shard_map/pallas_call | solution.py:96
  170.7 25.2 %all-to-all-done.1 = bf16[64,8,3072]{2,1,0:T(8,128)(2,1)} async-done(((bf16[64,8,3072]{2,1,0:T(8,128)(2,1)}), bf16[64,8,3072]{2,1,0:T(8,128)(2,1)}, u32[]{:S(2)}, u32[]{:S(2)}) %all-to-all-start.1) | async-done | bytes 3145760 | tf_op jit(solution)/shard_map/all_to_all | solution.py:38
  195.9 7.0 %shard_map.138 = (bf16[1024,768]{1,0:T(8,128)(2,1)}, f32[8,128]{1,0:T(8,128)}) custom-call(bf16[4,1024,512]{2,1,0:T(8,128)(2,1)} %bitcast.24, bf16[512,3072]{1,0:T(8,128)(2,1)} %bitcast.9.grad_ref), custom_call_target="tpu_custom_call" | custom-call | flops 3221225472 | bytes 7340032 | tf_op jit(solution)/shard_map/pallas_call | solution.py:396
  202.9 0.0 reduce-scatter.4.cloned.1.call-update
  202.9 0.0 all-gather.2.cloned.1.call-start
  203.0 0.0 reduce-scatter.8.cloned.1.call-done.value_ref
  203.0 13.1 %all_to_all.20 = bf16[8,8,1024]{2,1,0:T(8,128)(2,1)S(1)} all-to-all(bf16[8,8,1024]{2,1,0:T(8,128)(2,1)} %bitcast.36), channel_id=1, replica_groups=mesh['z'=8,'x'=4,'c'=2,'rep'=4] {'z'}, dimensions={0} | all-to-all | bytes 262144 | tf_op jit(solution)/shard_map/all_to_all | solution.py:38
  216.1 0.1 broadcast_in_dim.30
  216.2 0.0 copy-start.5
  216.2 15.6 %all_to_all.21 = bf16[32,8,1024]{2,1,0:T(8,128)(2,1)S(1)} all-to-all(bf16[32,8,1024]{2,1,0:T(8,128)(2,1)S(1)} %broadcast_in_dim.30), channel_id=1, replica_groups=mesh['z'=8,'x'=4,'c'=2,'rep'=4] {'x','z'}, dimensions={0} | all-to-all | bytes 1048576 | tf_op jit(solution)/shard_map/all_to_all | solution.py:38
  231.9 0.8 pad_maximum_fusion.1.value_ref
  232.6 0.0 reduce-scatter.4.cloned.1.call-done.earlier_ref
  232.7 0.0 all-gather.2.cloned.1.call-update
  232.7 0.0 copy-done.5
  232.7 1.4 convolution_convert_fusion
  234.1 32.5 %all-gather.2.cloned.1.call-done = bf16[1664,1024]{1,0:T(8,128)(2,1)} async-done(((bf16[208,1024]{1,0:T(8,128)(2,1)}), bf16[1664,1024]{1,0:T(8,128)(2,1)}) %all-gather.2.cloned.1.call-update) | async-done | bytes 3407888 | tf_op jit(solution)/shard_map/all_gather | solution.py:319
  266.6 4.5 %shard_map.141 = (f32[768,1024]{1,0:T(8,128)}, f32[768,1024]{1,0:T(8,128)}, f32[1,1024]{1,0:T(1,128)}) custom-call(bf16[8,208,1024]{2,1,0:T(8,128)(2,1)} %bitcast.26), custom_call_target="tpu_custom_call" | custom-call | flops 1703936 | bytes 10223616 | tf_op jit(solution)/shard_map/pallas_call | solution.py:361
  (9 shorter events, 0.1 us)
Async XLA Ops:
  7.2 28.1 %copy-start = (bf16[768,1024]{1,0:T(8,128)(2,1)S(1)}, bf16[768,1024]{1,0:T(8,128)(2,1)}, u32[]{:S(2)}) copy-start(bf16[768,1024]{1,0:T(8,128)(2,1)} %param.14) | copy-start | bytes 4718596
  17.4 13.4 %copy-start.2 = (s32[1,64,32]{1,2,0:T(8,128)S(1)}, s32[1,64,32]{1,2,0:T(8,128)}, u32[]{:S(2)}) copy-start(s32[1,64,32]{1,2,0:T(8,128)} %param.13) | copy-start | bytes 24580
  17.4 14.3 %copy-start.3 = (s32[256]{0:T(256)S(1)}, s32[256]{0:T(256)}, u32[]{:S(2)}) copy-start(s32[256]{0:T(256)} %param.10) | copy-start | bytes 3076
  17.4 14.3 %copy-start.1 = (bf16[1024,768]{1,0:T(8,128)(2,1)S(1)}, bf16[1024,768]{1,0:T(8,128)(2,1)}, u32[]{:S(2)}) copy-start(bf16[1024,768]{1,0:T(8,128)(2,1)} %feats_ref.1) | copy-start | bytes 4718596
  17.4 88.6 %all-to-all-start = ((bf16[64,8,3200]{2,1,0:T(8,128)(2,1)}), bf16[64,8,3200]{2,1,0:T(8,128)(2,1)}, u32[]{:S(2)}, u32[]{:S(2)}) async-start(bf16[64,8,3200]{2,1,0:T(8,128)(2,1)} %bitcast.27), calls=%async_computation | async-start | bytes 6553600 | tf_op jit(solution)/shard_map/all_to_all | solution.py:38
  30.7 130.8 %reduce-scatter.6.cloned.1.call-start = ((), (), s32[]{:S(2)}) async-start(), calls=%async_computation.8 | async-start | bytes 3833856 | tf_op jit(solution)/shard_map/reduce_scatter | solution.py:306
  32.9 2.3 copy-start.4
  116.3 79.5 %all-to-all-start.1 = ((bf16[64,8,3072]{2,1,0:T(8,128)(2,1)}), bf16[64,8,3072]{2,1,0:T(8,128)(2,1)}, u32[]{:S(2)}, u32[]{:S(2)}) async-start(bf16[64,8,3072]{2,1,0:T(8,128)(2,1)} %bitcast.28), calls=%async_computation.1 | async-start | bytes 6291456 | tf_op jit(solution)/shard_map/all_to_all | solution.py:38
  123.2 79.8 %reduce-scatter.8.cloned.1.call-start = ((), (), s32[]{:S(2)}) async-start(), calls=%async_computation.9 | async-start | bytes 655360 | tf_op jit(solution)/shard_map/reduce_scatter | solution.py:312
  164.2 68.5 %reduce-scatter.4.cloned.1.call-start = ((), (), s32[]{:S(2)}) async-start(), calls=%async_computation.7 | async-start | bytes 1966080 | tf_op jit(solution)/shard_map/reduce_scatter | solution.py:450
  202.9 63.6 %all-gather.2.cloned.1.call-start = ((), (), s32[]{:S(2)}) async-start(), calls=%async_computation.10 | async-start | bytes 3833856 | tf_op jit(solution)/shard_map/all_gather | solution.py:319
  216.2 16.5 %copy-start.5 = (bf16[256,1024]{1,0:T(8,128)(2,1)S(1)}, bf16[256,1024]{1,0:T(8,128)(2,1)}, u32[]{:S(2)}) copy-start(bf16[256,1024]{1,0:T(8,128)(2,1)} %get-tuple-element.19) | copy-start | bytes 1572868
Sparse Core Ops, SparseCore 0:
  116.5 45.0 reduce-scatter.5
  164.6 26.0 reduce-scatter.7
  203.1 24.6 reduce-scatter.3
  232.8 33.7 all-gather.1

commit v11 on v10

--- a/solution.py
+++ b/solution.py
@@ -15,7 +15,7 @@
 f32 = jnp.float32
 
 GROUP = 4
-STEP = 4
+STEP = 2
 SPLIT = 4
 EXTRA = 128
 VMEM = pltpu.CompilerParams(vmem_limit_bytes=60 * 1024 * 1024)

time: 278 us -> 280 us (level)
  no operation moved by 1% of the time
where the time goes in v11:
time: 280 us
  waiting for transfers between devices  166 us (59%)
  Pallas kernels  34 us (12%)
  blocking collectives  28.6 us (10%)
  starting transfers between devices  20.3 us (7%)
  between operations  13.9 us (5%)
  local copies, waits for them, and re-layouts  10.5 us (4%)
  other arithmetic  3.76 us (1%)
  matrix products  2.96 us (1%)
    all_to_all x2, waiting for transfers between devices, exchange(): return lax.all_to_all(value, axes, split_axis=0, concat_axis=0, tiled=True)  94.5 us
    reduce_scatter x1, waiting for transfers between devices, reduce_everywhere(): lax.psum_scatter(terms.reshape(-1, hidden), NEAR, scatter_dimension=0, ti...  38.3 us
    all_gather x1, waiting for transfers between devices, reduce_everywhere(): return lax.all_gather(after(own, meanwhile), NEAR, axis=0, tiled=True)  32.6 us
    all_to_all x2, blocking collectives, exchange(): return lax.all_to_all(value, axes, split_axis=0, concat_axis=0, tiled=True)  28.6 us
    all_to_all x2, starting transfers between devices, exchange(): return lax.all_to_all(value, axes, split_axis=0, concat_axis=0, tiled=True)  20.1 us
    pallas_call x1, Pallas kernels, select_and_sum(): pl.pallas_call(select_kernel, grid=(steps,), in_specs=[edge_spec, edge_sp...  12.2 us
    pallas_call x1, Pallas kernels, middle(): pl.pallas_call(middle_kernel, in_specs=[hbm, pl.BlockSpec(memory_space=pl...  10.3 us
    pallas_call x1, Pallas kernels, scatter_sum(): pl.pallas_call(scatter_kernel, grid=(steps,), in_specs=[pl.BlockSpec((SPL...  7.03 us
  transfers between devices with their start and end apart: 6, of which 4 were waited for; matrix products, arithmetic and copies ran while one was open for 6% of the time, Pallas kernels for 3%

profile of v11, /device:TPU:1, one launch (start us, length us, event | category | flops | bytes accessed | tf_op | source)
XLA Modules:
  0.0 279.6 jit_solution(5051669122456721417)
XLA Ops:
  7.2 0.0 copy-start
  7.2 12.2 %shard_map.136 = (bf16[4,512,1024]{2,1,0:T(8,128)(2,1)}, bf16[512,3200]{1,0:T(8,128)(2,1)}) custom-call(s32[64,64]{1,0:T(8,128)} %bitcast.38, s32[64,64]{1,0:T(8,128)} %bitcast.39, bf16[1024,768]{1,0:T(8,128)(2,1)} %feats_ref.1), custom_call_target="tpu_custom_call" | custom-call | flops 4294967296 | bytes 9043968 | tf_op jit(solution)/shard_map/pallas_call | solution.py:96
  19.4 0.0 copy-start.2
  19.4 0.0 copy-start.3
  19.4 0.0 copy-start.1
  19.4 13.3 %all-to-all-start = ((bf16[64,8,3200]{2,1,0:T(8,128)(2,1)}), bf16[64,8,3200]{2,1,0:T(8,128)(2,1)}, u32[]{:S(2)}, u32[]{:S(2)}) async-start(bf16[64,8,3200]{2,1,0:T(8,128)(2,1)} %bitcast.27), calls=%async_computation | async-start | bytes 6553600 | tf_op jit(solution)/shard_map/all_to_all | solution.py:38
  32.7 0.0 reduce-scatter.6.cloned.1.call-start
  32.8 0.0 copy-done.2
  32.8 0.1 copy.20
  32.9 0.1 eq.15
  33.0 0.7 reshape.82.seeds_ref
  33.7 0.0 copy-done.3
  33.7 0.0 copy-done.1
  33.7 1.2 gather_fusion
  34.9 0.0 copy-start.4
  34.9 0.2 copy.21
  35.1 0.8 fusion.1.self_any
  35.9 1.3 fusion.turned_any
  37.2 0.0 copy-done
  37.2 0.0 copy-done.4
  37.2 1.6 convolution_add_fusion.base_any
  38.8 69.2 %all-to-all-done = bf16[64,8,3200]{2,1,0:T(8,128)(2,1)} async-done(((bf16[64,8,3200]{2,1,0:T(8,128)(2,1)}), bf16[64,8,3200]{2,1,0:T(8,128)(2,1)}, u32[]{:S(2)}, u32[]{:S(2)}) %all-to-all-start) | async-done | bytes 3276832 | tf_op jit(solution)/shard_map/all_to_all | solution.py:38
  108.0 10.3 %shard_map.137 = (bf16[256,1024]{1,0:T(8,128)(2,1)}, bf16[256,1024]{1,0:T(8,128)(2,1)}, bf16[512,3072]{1,0:T(8,128)(2,1)}, bf16[8,208,1024]{2,1,0:T(8,128)(2,1)}) custom-call(bf16[512,3200]{1,0:T(8,128)(2,1)} %bitcast.3.arrived_any, s32[4,1,512]{2,1,0:T(1,128)} %reshape.82.seeds_ref, f32[256,1024]{1,0:T(8,128)} %convolution_add_fusion.base_any, ...), custom_call_target="tpu_custom_call" | custom-call | flops 3221225472 | bytes 13893632 | tf_op jit(solution)/shard_map/pallas_call | solution.py:268
  118.3 0.0 reduce-scatter.6.cloned.1.call-update
  118.3 6.8 %all-to-all-start.1 = ((bf16[64,8,3072]{2,1,0:T(8,128)(2,1)}), bf16[64,8,3072]{2,1,0:T(8,128)(2,1)}, u32[]{:S(2)}, u32[]{:S(2)}) async-start(bf16[64,8,3072]{2,1,0:T(8,128)(2,1)} %bitcast.28), calls=%async_computation.1 | async-start | bytes 6291456 | tf_op jit(solution)/shard_map/all_to_all | solution.py:38
  125.2 0.0 reduce-scatter.8.cloned.1.call-start
  125.2 38.3 %reduce-scatter.6.cloned.1.call-done = bf16[208,1024]{1,0:T(8,128)(2,1)} async-done(((bf16[1664,1024]{1,0:T(8,128)(2,1)}), bf16[208,1024]{1,0:T(8,128)(2,1)}) %reduce-scatter.6.cloned.1.call-update) | async-done | bytes 426000 | tf_op jit(solution)/shard_map/reduce_scatter | solution.py:306
  163.5 0.8 slice.19
  164.3 1.0 slice.18
  165.3 0.8 pad_maximum_fusion
  166.2 0.0 reduce-scatter.8.cloned.1.call-update
  166.2 0.0 reduce-scatter.4.cloned.1.call-start
  166.2 6.3 %copy.23 = bf16[4,512,1024]{1,2,0:T(8,128)(2,1)} copy(bf16[4,512,1024]{2,1,0:T(8,128)(2,1)} %get-tuple-element.20) | data formatting | bytes 8388608 | tf_op jit(solution)/shard_map/pallas_call | solution.py:96
  172.5 25.4 %all-to-all-done.1 = bf16[64,8,3072]{2,1,0:T(8,128)(2,1)} async-done(((bf16[64,8,3072]{2,1,0:T(8,128)(2,1)}), bf16[64,8,3072]{2,1,0:T(8,128)(2,1)}, u32[]{:S(2)}, u32[]{:S(2)}) %all-to-all-start.1) | async-done | bytes 3145760 | tf_op jit(solution)/shard_map/all_to_all | solution.py:38
  197.9 7.0 %shard_map.138 = (bf16[1024,768]{1,0:T(8,128)(2,1)}, f32[8,128]{1,0:T(8,128)}) custom-call(bf16[4,1024,512]{2,1,0:T(8,128)(2,1)} %bitcast.24, bf16[512,3072]{1,0:T(8,128)(2,1)} %bitcast.9.grad_ref), custom_call_target="tpu_custom_call" | custom-call | flops 3221225472 | bytes 7340032 | tf_op jit(solution)/shard_map/pallas_call | solution.py:396
  204.9 0.0 reduce-scatter.4.cloned.1.call-update
  204.9 0.0 all-gather.2.cloned.1.call-start
  205.0 0.0 reduce-scatter.8.cloned.1.call-done.value_ref
  205.0 13.0 %all_to_all.20 = bf16[8,8,1024]{2,1,0:T(8,128)(2,1)S(1)} all-to-all(bf16[8,8,1024]{2,1,0:T(8,128)(2,1)} %bitcast.36), channel_id=1, replica_groups=mesh['z'=8,'x'=4,'c'=2,'rep'=4] {'z'}, dimensions={0} | all-to-all | bytes 262144 | tf_op jit(solution)/shard_map/all_to_all | solution.py:38
  218.1 0.1 broadcast_in_dim.30
  218.2 0.0 copy-start.5
  218.2 15.5 %all_to_all.21 = bf16[32,8,1024]{2,1,0:T(8,128)(2,1)S(1)} all-to-all(bf16[32,8,1024]{2,1,0:T(8,128)(2,1)S(1)} %broadcast_in_dim.30), channel_id=1, replica_groups=mesh['z'=8,'x'=4,'c'=2,'rep'=4] {'x','z'}, dimensions={0} | all-to-all | bytes 1048576 | tf_op jit(solution)/shard_map/all_to_all | solution.py:38
  233.7 0.8 pad_maximum_fusion.1.value_ref
  234.5 0.0 reduce-scatter.4.cloned.1.call-done.earlier_ref
  234.5 0.0 all-gather.2.cloned.1.call-update
  234.5 0.0 copy-done.5
  234.6 1.4 convolution_convert_fusion
  235.9 32.6 %all-gather.2.cloned.1.call-done = bf16[1664,1024]{1,0:T(8,128)(2,1)} async-done(((bf16[208,1024]{1,0:T(8,128)(2,1)}), bf16[1664,1024]{1,0:T(8,128)(2,1)}) %all-gather.2.cloned.1.call-update) | async-done | bytes 3407888 | tf_op jit(solution)/shard_map/all_gather | solution.py:319
  268.6 4.5 %shard_map.141 = (f32[768,1024]{1,0:T(8,128)}, f32[768,1024]{1,0:T(8,128)}, f32[1,1024]{1,0:T(1,128)}) custom-call(bf16[8,208,1024]{2,1,0:T(8,128)(2,1)} %bitcast.26), custom_call_target="tpu_custom_call" | custom-call | flops 1703936 | bytes 10223616 | tf_op jit(solution)/shard_map/pallas_call | solution.py:361
  (9 shorter events, 0.1 us)
Async XLA Ops:
  7.2 30.1 %copy-start = (bf16[768,1024]{1,0:T(8,128)(2,1)S(1)}, bf16[768,1024]{1,0:T(8,128)(2,1)}, u32[]{:S(2)}) copy-start(bf16[768,1024]{1,0:T(8,128)(2,1)} %param.14) | copy-start | bytes 4718596
  19.4 13.4 %copy-start.2 = (s32[1,64,32]{1,2,0:T(8,128)S(1)}, s32[1,64,32]{1,2,0:T(8,128)}, u32[]{:S(2)}) copy-start(s32[1,64,32]{1,2,0:T(8,128)} %param.13) | copy-start | bytes 24580
  19.4 14.3 %copy-start.3 = (s32[256]{0:T(256)S(1)}, s32[256]{0:T(256)}, u32[]{:S(2)}) copy-start(s32[256]{0:T(256)} %param.10) | copy-start | bytes 3076
  19.4 14.3 %copy-start.1 = (bf16[1024,768]{1,0:T(8,128)(2,1)S(1)}, bf16[1024,768]{1,0:T(8,128)(2,1)}, u32[]{:S(2)}) copy-start(bf16[1024,768]{1,0:T(8,128)(2,1)} %feats_ref.1) | copy-start | bytes 4718596
  19.4 88.6 %all-to-all-start = ((bf16[64,8,3200]{2,1,0:T(8,128)(2,1)}), bf16[64,8,3200]{2,1,0:T(8,128)(2,1)}, u32[]{:S(2)}, u32[]{:S(2)}) async-start(bf16[64,8,3200]{2,1,0:T(8,128)(2,1)} %bitcast.27), calls=%async_computation | async-start | bytes 6553600 | tf_op jit(solution)/shard_map/all_to_all | solution.py:38
  32.7 130.8 %reduce-scatter.6.cloned.1.call-start = ((), (), s32[]{:S(2)}) async-start(), calls=%async_computation.8 | async-start | bytes 3833856 | tf_op jit(solution)/shard_map/reduce_scatter | solution.py:306
  34.9 2.3 copy-start.4
  118.3 79.5 %all-to-all-start.1 = ((bf16[64,8,3072]{2,1,0:T(8,128)(2,1)}), bf16[64,8,3072]{2,1,0:T(8,128)(2,1)}, u32[]{:S(2)}, u32[]{:S(2)}) async-start(bf16[64,8,3072]{2,1,0:T(8,128)(2,1)} %bitcast.28), calls=%async_computation.1 | async-start | bytes 6291456 | tf_op jit(solution)/shard_map/all_to_all | solution.py:38
  125.2 79.8 %reduce-scatter.8.cloned.1.call-start = ((), (), s32[]{:S(2)}) async-start(), calls=%async_computation.9 | async-start | bytes 655360 | tf_op jit(solution)/shard_map/reduce_scatter | solution.py:312
  166.2 68.3 %reduce-scatter.4.cloned.1.call-start = ((), (), s32[]{:S(2)}) async-start(), calls=%async_computation.7 | async-start | bytes 1966080 | tf_op jit(solution)/shard_map/reduce_scatter | solution.py:450
  204.9 63.6 %all-gather.2.cloned.1.call-start = ((), (), s32[]{:S(2)}) async-start(), calls=%async_computation.10 | async-start | bytes 3833856 | tf_op jit(solution)/shard_map/all_gather | solution.py:319
  218.2 16.4 %copy-start.5 = (bf16[256,1024]{1,0:T(8,128)(2,1)S(1)}, bf16[256,1024]{1,0:T(8,128)(2,1)}, u32[]{:S(2)}) copy-start(bf16[256,1024]{1,0:T(8,128)(2,1)} %get-tuple-element.19) | copy-start | bytes 1572868
Sparse Core Ops, SparseCore 0:
  118.5 45.0 reduce-scatter.5
  166.6 26.2 reduce-scatter.7
  205.1 24.6 reduce-scatter.3
  234.7 33.8 all-gather.1
